TPU v7x, 512 devices: a whole 4x4x16 slice. The times are simulated.
512 devices in a mesh: seq: 128 (over z, y, core), head: 4 (over x).
Axes of the slice: x: 4, y: 4, z: 16, core: 2. Of those that a mesh axis runs over, the one named last changes fastest.
Arguments:
- patches: bfloat16 [32768, 1280], P('seq'), may hold values from -6 to 6
- norm_gain: float32 [1280], replicated, may hold values from 0.5 to 1.5
- w_qkv: bfloat16 [1280, 3, 1280], P('seq', None, 'head'), as said below
- w_out: bfloat16 [1280, 1280], P('head', 'seq'), may hold values from -0.15625 to 0.15625
- window_order: int32 [128, 64], P('seq'), may hold values from 0 to 63, each once within a row
- merge_gain: float32 [1280], replicated, may hold values from 0.5 to 1.5
- w_kv: bfloat16 [5120, 2, 1024], P('seq', None, 'head'), as said below
- queries: bfloat16 [256, 8192], P('seq', 'head'), may hold values from -6 to 6
- suffix_kv: bfloat16 [256, 64, 2, 1024], P('seq', None, None, 'head'), may hold values from -12 to 12
- question_lengths: int32 [256], P('seq'), may hold values from 1 to 64
- frame_range: int32 [256, 2], replicated, may hold values from 0 to 128, as said below
Outputs:
- answers: bfloat16 [256, 8192], P('seq', 'head')
Inputs may be any that keep to these rules, and one draw needn't show every extreme that they name: `window_order`: each row is an ordering of a frame's units; positions w * 16 to (w + 1) * 16 - 1 form window w. `frame_range`: the first entry of a row is below the second. `w_qkv`: entries of order one over the square root of 1280. `w_kv`: entries of order one over the square root of 5120.
All inputs are finite; a program needn't handle non-finite values.
Results may differ from a plain program's by a relative error of at most 0.007.
Values may be sent and summed in bfloat16 or wider, within the bound.
No kernel may reach another device: no remote copies, remote signals or barrier semaphores. Data moves between devices by JAX's collectives and lax.ppermute only.
A program may use at most 64 MiB of HBM per device.

v0:
```python
import jax
import jax.numpy as jnp
from jax import lax
from jax.sharding import Mesh
from jax.sharding import PartitionSpec as P

VD = 1280
VH = 16
HD = 128
FPATCH = 256
WIN = 64
SEQ = ("seq_0", "seq_1", "seq_2")


NEGATIVE = -1e30


def in_order(blocks, dim):
    dims = list(blocks.shape[1:])
    dims[dim] *= blocks.shape[0]
    return jnp.moveaxis(blocks, 0, dim).reshape(dims)


def all_blocks(value, axes, sequence):
    blocks = value[None]
    for k in sequence:
        blocks = lax.all_gather(blocks, axes[k], axis=0, tiled=True)
    current = [lax.axis_size(axes[k]) for k in reversed(sequence)]
    blocks = blocks.reshape(*current, *value.shape)
    turned = sorted(range(len(sequence)), key=lambda place: sequence[len(sequence) - 1 - place])
    return blocks.transpose(*turned, *range(len(sequence), blocks.ndim)).reshape(-1, *value.shape)


def whole_of(value, axes, sequence, dim):
    return in_order(all_blocks(value, axes, sequence), dim)


def from_everyone(value, axis):
    copies = jnp.broadcast_to(value, (lax.axis_size(axis), *value.shape))
    return lax.all_to_all(copies, axis, split_axis=0, concat_axis=0, tiled=True)


def of_everyone(value, axis):
    everything = from_everyone(value, axis)
    return jnp.sum(everything.astype(jnp.float32), axis=0)


def rms_scale(values, gain):
    return values * lax.rsqrt(jnp.mean(values * values, axis=-1, keepdims=True) + 1e-06) * gain


def frame_window(frame_rows, unit_order, local_heads, head_size):
    unit_count = unit_order.shape[0]
    grouped = frame_rows.reshape(unit_count, 4, 3, local_heads * head_size)[unit_order]
    windows = grouped.reshape(-1, WIN, 3, local_heads, head_size)
    scores = jnp.einsum(
        "wqhd,wkhd->whqk", windows[:, :, 0], windows[:, :, 1], preferred_element_type=jnp.float32
    ) * head_size ** (-0.5)
    weights = jax.nn.softmax(scores, axis=-1).astype(jnp.bfloat16)
    mixed = jnp.einsum(
        "whqk,wkhd->wqhd", weights, windows[:, :, 2], preferred_element_type=jnp.float32
    ).astype(jnp.bfloat16)
    mixed = mixed.reshape(unit_count, 4, local_heads * head_size)
    return (
        jnp.zeros_like(mixed)
        .at[unit_order]
        .set(mixed)
        .reshape(unit_count * 4, local_heads * head_size)
    )


def prefix_scores(asking, keys_values, bounds, frame_tokens):
    token_count = keys_values.shape[0]
    kv_local, head_size = (asking.shape[1], asking.shape[3])
    keys = keys_values[:, 0].reshape(token_count, kv_local, head_size)
    values = keys_values[:, 1].reshape(token_count, kv_local, head_size)
    frame_index = jnp.arange(token_count) // frame_tokens
    live = (frame_index[None, :] >= bounds[:, 0:1]) & (frame_index[None, :] < bounds[:, 1:2])
    scores = jnp.einsum(
        "qgjd,ngd->qgjn", asking, keys, preferred_element_type=jnp.float32
    ) * head_size ** (-0.5)
    return (jnp.where(live[:, None, None, :], scores, -jnp.inf), values)


def add_suffix(maxima, totals, weighted, asking, suffix_kv, lengths):
    quest_count, span = (suffix_kv.shape[0], suffix_kv.shape[1])
    kv_local, head_size = (asking.shape[1], asking.shape[3])
    keys = suffix_kv[:, :, 0].reshape(quest_count, span, kv_local, head_size)
    values = suffix_kv[:, :, 1].reshape(quest_count, span, kv_local, head_size)
    scores = jnp.einsum(
        "qgjd,qsgd->qgjs", asking, keys, preferred_element_type=jnp.float32
    ) * head_size ** (-0.5)
    live = (jnp.arange(span)[None, :] < lengths[:, None])[:, None, None, :]
    scores = jnp.where(live, scores, -jnp.inf)
    highest = jnp.maximum(maxima, jnp.max(scores, axis=-1))
    weights = jnp.exp(scores - highest[..., None])
    carried = jnp.exp(maxima - highest)
    totals = totals * carried + jnp.sum(weights, axis=-1)
    weighted = weighted * carried[..., None] + jnp.einsum(
        "qgjs,qsgd->qgjd", weights.astype(jnp.bfloat16), values, preferred_element_type=jnp.float32
    )
    return (weighted / totals[..., None]).reshape(quest_count, -1).astype(jnp.bfloat16)


def on_device(
    patches,
    norm_gain,
    w_qkv,
    w_out,
    window_order,
    merge_gain,
    w_kv,
    queries,
    suffix_kv,
    question_lengths,
    frame_range,
):
    row_count = patches.shape[0]
    columns = w_qkv.shape[2]
    head_size = VD // VH
    local_heads = columns // head_size
    source = patches.astype(jnp.float32)
    normed = rms_scale(source, norm_gain).astype(jnp.bfloat16)
    portion = whole_of(w_qkv, SEQ, (1, 0, 2), 0)
    inputs = normed
    projected = jnp.dot(
        inputs, portion.reshape(portion.shape[0], 3 * columns), preferred_element_type=jnp.float32
    )
    projected = projected.astype(jnp.bfloat16).reshape(window_order.shape[0], -1, 3, columns)
    attended = jax.vmap(
        lambda frame_rows, unit_order: frame_window(frame_rows, unit_order, local_heads, head_size)
    )(projected, window_order)
    attended = attended.reshape(row_count, columns)
    w_full = lax.all_gather(w_out, SEQ, axis=1, tiled=True)
    summed = of_everyone(
        jnp.dot(attended, w_full, preferred_element_type=jnp.float32).astype(jnp.bfloat16), "head"
    ).astype(jnp.float32)
    merged_all = (
        rms_scale(source + summed, merge_gain).astype(jnp.bfloat16).reshape(row_count // 4, 4 * VD)
    )
    token_count = merged_all.shape[0]
    kv_columns = w_kv.shape[2]
    portion = lax.all_gather(w_kv, SEQ, axis=0, tiled=True)
    inputs = merged_all
    visual = jnp.dot(
        inputs,
        portion.reshape(portion.shape[0], 2 * kv_columns),
        preferred_element_type=jnp.float32,
    )
    visual = visual.astype(jnp.bfloat16).reshape(token_count, 2, kv_columns)
    quest_count = queries.shape[0]
    kv_local = kv_columns // HD
    asking = queries.reshape(quest_count, kv_local, -1, HD)
    group = asking.shape[2]
    frame_tokens = FPATCH // 4
    seq_index = lax.axis_index(SEQ)
    own_bounds = lax.dynamic_slice_in_dim(frame_range, seq_index * quest_count, quest_count, 0)
    maxima = jnp.full((quest_count, kv_local, group), NEGATIVE, jnp.float32)
    scores, values = prefix_scores(
        asking, whole_of(visual, SEQ, (1, 0, 2), 0), own_bounds, frame_tokens
    )
    highest = jnp.maximum(maxima, jnp.max(scores, axis=-1))
    weights = jnp.exp(scores - highest[..., None])
    totals = jnp.sum(weights, axis=-1)
    weighted = jnp.einsum(
        "qgjn,ngd->qgjd", weights.astype(jnp.bfloat16), values, preferred_element_type=jnp.float32
    )
    maxima, totals, weighted = (highest, totals, weighted)
    return add_suffix(maxima, totals, weighted, asking, suffix_kv, question_lengths)


def solution(mesh):
    torus = Mesh(
        mesh.devices.reshape(16, 4, 2, mesh.shape["head"]), ("seq_0", "seq_1", "seq_2", "head")
    )
    in_specs = (
        P(SEQ, None),
        P(),
        P(SEQ, None, "head"),
        P("head", SEQ),
        P(SEQ, None),
        P(),
        P(SEQ, None, "head"),
        P(SEQ, "head"),
        P(SEQ, None, None, "head"),
        P(SEQ),
        P(),
    )
    out_specs = P(SEQ, "head")
    return jax.shard_map(
        on_device, mesh=torus, in_specs=in_specs, out_specs=out_specs, check_vma=False
    )
```

profile of v0, /device:TPU:1, one launch (start us, length us, event | category | flops | bytes accessed | tf_op | source)
XLA Modules:
  0.0 429.4 jit_solution(2125874026757927389)
XLA Ops:
  6.5 12.5 %all-gather = bf16[40,3,320]{2,1,0:T(4,128)(2,1)} all-gather(bf16[10,3,320]{2,1,0:T(4,128)(2,1)} %param.13), channel_id=2, replica_groups=mesh['seq_0'=16,'seq_1'=4,'seq_2'=2,'head'=4] {'seq_1'}, dimensions={0}, use_global_device_ids=true | all-gather | bytes 96000 | tf_op jit(solution)/shard_map/all_gather | solution.py:27
  19.1 69.1 %all-gather.8.cloned.1.call-done = bf16[64,10,3,320]{3,2,1,0:T(4,128)(2,1)} async-done(((bf16[4,10,3,320]{3,2,1,0:T(4,128)(2,1)}), bf16[64,10,3,320]{3,2,1,0:T(4,128)(2,1)}) %all-gather.8.cloned.1.call-update) | async-done | bytes 1228816 | tf_op jit(solution)/shard_map/all_gather | solution.py:27
  88.2 3.1 copy.104
  91.4 0.7 all-gather.12.cloned.1.call-update
  92.1 111.3 %all-gather.1 = bf16[128,10,320]{2,1,0:T(8,128)(2,1)S(1)} all-gather(bf16[1,10,320]{2,1,0:T(8,128)(2,1)S(1)} %bitcast.119), channel_id=1, replica_groups=mesh['seq_0'=16,'seq_1'=4,'seq_2'=2,'head'=4] {'seq_0','seq_1','seq_2'}, dimensions={0}, use_global_device_ids=true | all-gather | bytes 825600 | tf_op jit(solution)/shard_map/all_gather | solution.py:134
  203.4 1.5 reshape.215
  204.9 0.2 fusion.3
  205.2 4.6 %reshape.179 = bf16[2,16,4,10,3,320]{5,2,1,0,4,3:T(4,128)(2,1)S(1)} reshape(bf16[128,10,3,320]{3,0,2,1:T(8,128)(2,1)} %all-gather.10.cloned.1.call-done) | data formatting | bytes 4915200 | tf_op jit(solution)/shard_map/reshape | solution.py:29
  209.8 4.5 %copy.105 = bf16[16,4,2,10,3,320]{5,4,3,2,1,0:T(4,128)(2,1)} copy(bf16[16,4,2,10,3,320]{5,1,0,2,4,3:T(4,128)(2,1)S(1)} %bitcast.112) | data formatting | bytes 4915200 | tf_op jit(solution)/shard_map/transpose | solution.py:31
  214.3 7.0 %reshape_reshape_reshape.3 = bf16[1280,960]{1,0:T(8,128)(2,1)S(1)} reshape(bf16[16,4,2,10,3,320]{5,4,3,2,1,0:T(4,128)(2,1)} %copy.105) | data formatting | bytes 4915200 | tf_op jit(solution)/shard_map/reshape;reshape;reshape | solution.py:127
  221.3 2.0 convolution_convert_fusion.1
  223.3 1.2 copy.106
  224.5 0.4 reshape_reshape.6
  224.9 0.3 copy.107
  225.2 1.1 gather_fusion
  226.3 0.2 copy.108
  226.6 0.6 reshape.180
  227.1 0.3 fusion.37
  227.5 0.3 fusion.38
  227.8 0.3 convolution_multiply_fusion.1
  228.1 0.3 fusion.8
  228.4 0.2 copy.113
  228.6 0.3 reshape.206
  228.9 2.5 scatter_fusion
  231.5 0.5 convolution_convert_fusion
  232.0 0.2 broadcast_in_dim.37
  232.2 35.4 %all_to_all.5 = bf16[4,256,1280]{2,1,0:T(8,128)(2,1)S(1)} all-to-all(bf16[4,256,1280]{2,1,0:T(8,128)(2,1)S(1)} %broadcast_in_dim.37), channel_id=1, replica_groups=mesh['seq_0'=16,'seq_1'=4,'seq_2'=2,'head'=4] {'head'}, dimensions={0} | all-to-all | bytes 5242880 | tf_op jit(solution)/shard_map/all_to_all | solution.py:40
  267.6 0.4 convert_reduce_fusion
  268.0 0.3 multiply_reduce_fusion
  268.3 0.3 multiply_convert_fusion
  268.6 0.4 reshape.186
  269.0 3.4 copy.144
  272.4 1.0 convolution_convert_fusion.3
  273.5 11.1 %all_gather.29 = bf16[4,64,2,256]{3,1,2,0:T(8,128)(2,1)} all-gather(bf16[1,64,2,256]{3,1,2,0:T(8,128)(2,1)S(1)} %copy.114), channel_id=1, replica_groups=mesh['seq_0'=16,'seq_1'=4,'seq_2'=2,'head'=4] {'seq_1'}, dimensions={0}, use_global_device_ids=true | all-gather | bytes 327680 | tf_op jit(solution)/shard_map/all_gather | solution.py:27
  284.7 66.7 %all-gather.14.cloned.1.call-done = bf16[64,64,2,256]{3,1,2,0:T(8,128)(2,1)} async-done(((bf16[4,64,2,256]{3,1,2,0:T(8,128)(2,1)}), bf16[64,64,2,256]{3,1,2,0:T(8,128)(2,1)}) %all-gather.14.cloned.1.call-update) | async-done | bytes 4194320 | tf_op jit(solution)/shard_map/all_gather | solution.py:27
  351.5 0.5 slice_reduce_fusion
  352.1 0.2 fusion.39
  352.5 38.0 %all-gather.16.cloned.1.call-done = bf16[128,64,2,256]{3,1,2,0:T(8,128)(2,1)} async-done(((bf16[64,64,2,256]{3,1,2,0:T(8,128)(2,1)}), bf16[128,64,2,256]{3,1,2,0:T(8,128)(2,1)}) %all-gather.16.cloned.1.call-update) | async-done | bytes 8388624 | tf_op jit(solution)/shard_map/all_gather | solution.py:27
  390.5 8.3 %copy.115 = bf16[16,4,2,64,2,256]{5,3,2,1,0,4:T(8,128)(2,1)} copy(bf16[16,4,2,64,2,256]{5,3,4,1,0,2:T(8,128)(2,1)} %bitcast.113) | data formatting | bytes 16777216 | tf_op jit(solution)/shard_map/transpose | solution.py:31
  398.7 5.7 %fusion.36 = (bf16[8192,1,256]{2,0,1:T(8,128)(2,1)}, bf16[8192,1,256]{2,0,1:T(8,128)(2,1)}) fusion(bf16[8192,2,256]{2,0,1:T(8,128)(2,1)} %bitcast.108), kind=kLoop, calls=%fused_computation.81 | loop fusion | bytes 16777216 | tf_op jit(solution)/shard_map/slice | solution.py:75
  404.4 6.4 %copy.116 = bf16[8192,1,256]{0,2,1:T(8,128)(2,1)} copy(bf16[8192,1,256]{2,0,1:T(8,128)(2,1)} %get-tuple-element.10) | data formatting | bytes 8388608 | tf_op jit(solution)/shard_map/slice | solution.py:76
  410.8 6.4 %copy.117 = bf16[8192,1,256]{0,2,1:T(8,128)(2,1)} copy(bf16[8192,1,256]{2,0,1:T(8,128)(2,1)} %get-tuple-element.9) | data formatting | bytes 8388608 | tf_op jit(solution)/shard_map/slice | solution.py:75
  417.2 3.1 fusion.40
  420.3 0.2 fusion.29
  420.5 0.3 fusion.13
  420.8 1.2 fusion.11
  422.1 0.1 fusion.12
  422.2 0.6 copy.190
  (53 shorter events, 0.9 us)
Async XLA Ops:
  6.5 344.9 %copy-start = (s32[256,2]{0,1:T(2,128)S(1)}, s32[256,2]{0,1:T(2,128)}, u32[]{:S(2)}) copy-start(s32[256,2]{0,1:T(2,128)} %param.21) | copy-start | bytes 6148
  6.5 85.6 %copy-start.7 = (bf16[320,10]{0,1:T(8,128)(2,1)S(1)}, bf16[320,10]{0,1:T(8,128)(2,1)}, u32[]{:S(2)}) copy-start(bf16[320,10]{0,1:T(8,128)(2,1)} %param.14) | copy-start | bytes 19204
  6.5 81.7 %all-gather.8.cloned.1.call-start = ((), (), s32[]{:S(2)}) async-start(), calls=%async_computation.1 | async-start | bytes 2088960 | tf_op jit(solution)/shard_map/all_gather | solution.py:27
  19.1 186.1 %all-gather.10.cloned.1.call-start = ((), (), s32[]{:S(2)}) async-start(), calls=%async_computation.2 | async-start | bytes 4423680 | tf_op jit(solution)/shard_map/all_gather | solution.py:27
  91.3 113.6 %copy-start.10 = (s32[1,64]{1,0:T(1,128)S(1)}, s32[1,64]{1,0:T(1,128)}, u32[]{:S(2)}) copy-start(s32[1,64]{1,0:T(1,128)} %param.15) | copy-start | bytes 772
  91.3 113.6 %copy-start.2 = (bf16[256,1280]{1,0:T(8,128)(2,1)S(1)}, bf16[256,1280]{1,0:T(8,128)(2,1)}, u32[]{:S(2)}) copy-start(bf16[256,1280]{1,0:T(8,128)(2,1)} %param.11) | copy-start | bytes 1966084
  91.3 177.7 %all-gather.12.cloned.1.call-start = ((), (), s32[]{:S(2)}) async-start(), calls=%async_computation.3 | async-start | bytes 5283840 | tf_op jit(solution)/shard_map/all_gather | solution.py:143
  92.1 259.3 %all-gather.14.cloned.1.call-start = ((), (), s32[]{:S(2)}) async-start(), calls=%async_computation.4 | async-start | bytes 4456448 | tf_op jit(solution)/shard_map/all_gather | solution.py:27
  214.3 7.0 %copy-start.3 = (bf16[256,1280]{1,0:T(8,128)(2,1)S(1)}, bf16[256,1280]{1,0:T(8,128)(2,1)}, u32[]{:S(2)}) copy-start(bf16[256,1280]{1,0:T(8,128)(2,1)} %param.11) | copy-start | bytes 1966084
  214.3 7.0 %copy-start.9 = (f32[1280]{0:T(1024)S(1)}, f32[1280]{0:T(1024)}, u32[]{:S(2)}) copy-start(f32[1280]{0:T(1024)} %param.12) | copy-start | bytes 15364
  227.8 3.7 copy-start.4
  267.6 0.7 copy-start.8
  273.4 78.1 %copy-start.5 = (bf16[2,64,2,256]{3,2,1,0:T(2,128)(2,1)S(1)}, bf16[2,64,2,256]{3,2,1,0:T(2,128)(2,1)}, u32[]{:S(2)}) copy-start(bf16[2,64,2,256]{3,2,1,0:T(2,128)(2,1)} %param.19) | copy-start | bytes 393220
  273.5 78.5 %copy-start.11 = (s32[2]{0:T(128)S(1)}, s32[2]{0:T(128)}, u32[]{:S(2)}) copy-start(s32[2]{0:T(128)} %param.20) | copy-start | bytes 28
  273.5 78.6 %copy-start.6 = (bf16[2,2048]{1,0:T(2,128)(2,1)S(1)}, bf16[2,2048]{1,0:T(2,128)(2,1)}, u32[]{:S(2)}) copy-start(bf16[2,2048]{1,0:T(2,128)(2,1)} %param.18) | copy-start | bytes 24580
  284.6 105.8 %all-gather.16.cloned.1.call-start = ((), (), s32[]{:S(2)}) async-start(), calls=%async_computation.5 | async-start | bytes 12582912 | tf_op jit(solution)/shard_map/all_gather | solution.py:27
  417.2 3.6 copy-start.1
Sparse Core Ops, SparseCore 0:
  19.2 68.9 all-gather.7
  91.4 30.2 all-gather.9
  124.9 143.7 all-gather.11
  284.8 66.5 all-gather.13
  353.3 37.1 all-gather.15
where the time goes:
time: 430 us; the launch traced here: 429 us
  waiting for transfers between devices  175 us (41%)
  blocking collectives  170 us (40%)
  local copies, waits for them, and re-layouts  59.8 us (14%)
  between operations  13.5 us (3%)
  matrix products  9.15 us (2%)
    all_gather x4, waiting for transfers between devices, all_blocks(): blocks = lax.all_gather(blocks, axes[k], axis=0, tiled=True)  174 us
    all_gather x1, blocking collectives, on_device(): w_full = lax.all_gather(w_out, SEQ, axis=1, tiled=True)  111 us
    all_to_all x1, blocking collectives, from_everyone(): return lax.all_to_all(copies, axis, split_axis=0, concat_axis=0, tiled=True)  35.4 us
    all_gather x2, blocking collectives, all_blocks(): blocks = lax.all_gather(blocks, axes[k], axis=0, tiled=True)  23.6 us
    transpose x2, local copies, waits for them, and re-layouts, all_blocks(): blocks.transpose(*turned, *range(len(sequence), blocks.ndim))  12.7 us
    slice x2, local copies, waits for them, and re-layouts, prefix_scores(): keys = keys_values[:, 0].reshape(token_count, kv_local, head_size)  12.1 us
  transfers between devices with their start and end apart: 5, of which 3 were waited for; matrix products, arithmetic and copies ran while one was open for 7% of the time, Pallas kernels for 0%

commit v1 on v0

v1 whole, which is shorter than its diff:
```python
import functools

import jax
import jax.numpy as jnp
import numpy as np
from jax import lax
from jax.experimental import pallas as pl
from jax.experimental.pallas import tpu as pltpu
from jax.sharding import Mesh
from jax.sharding import PartitionSpec as P

VD = 1280
VH = 16
HD = 128
FPATCH = 256
WIN = 64
SEQ = ("seq_0", "seq_1", "seq_2")
NZ, NY, NC, NX = 16, 4, 2, 4
ROWS = VD // (NZ * NY * NC)
COLS = VD // NX
HEAD = VD // VH
HEADS = COLS // HEAD
UNITS = FPATCH // 4
GROUP = 8
LAYER = NY * NC
NEGATIVE = -1e30
f32 = jnp.float32
bf16 = jnp.bfloat16


def dot(a, b):
    return lax.dot_general(a, b, (((1,), (0,)), ((), ())), preferred_element_type=f32)


def dot_t(a, b):
    return lax.dot_general(a, b, (((1,), (1,)), ((), ())), preferred_element_type=f32)


def iota(shape, dim):
    return lax.broadcasted_iota(jnp.int32, shape, dim)


def one_hot(condition):
    return jnp.where(condition, 1.0, 0.0).astype(bf16)


def row_order():
    order = np.zeros((VD, VD), np.float32)
    z, y, c, r = np.meshgrid(np.arange(NZ), np.arange(NY), np.arange(NC), np.arange(ROWS), indexing="ij")
    order[((z * NY + y) * NC + c) * ROWS + r, ((c * NY + y) * NZ + z) * ROWS + r] = 1.0
    return order


def copies_over(value, axes, count):
    copies = jnp.broadcast_to(value[None], (count, *value.shape))
    return lax.all_to_all(copies, axes, split_axis=0, concat_axis=0, tiled=True)


def call(body, outs, operands, specs=None, vmem=40 << 20):
    vm = pl.BlockSpec(memory_space=pltpu.VMEM)
    return pl.pallas_call(
        body,
        out_shape=outs,
        in_specs=specs or [vm] * len(operands),
        out_specs=jax.tree.map(lambda _: vm, outs),
        compiler_params=pltpu.CompilerParams(vmem_limit_bytes=vmem),
    )(*operands)


VMEM = pl.BlockSpec(memory_space=pltpu.VMEM)
SMEM = pl.BlockSpec(memory_space=pltpu.SMEM)


def compact_kernel(got_ref, weights_ref, asked_ref):
    got = got_ref[...]
    shape = (NZ * ROWS, NZ * 16)
    row, col = iota(shape, 0), iota(shape, 1)
    pick = one_hot(col == (row // ROWS) * 16 + row % ROWS)
    weights = dot(pick, got).astype(bf16)
    for k in range(NY):
        weights_ref[k] = weights
    shape = (NZ * 4, NZ * 16)
    row, col = iota(shape, 0), iota(shape, 1)
    pick = one_hot(col == (row // 4) * 16 + ROWS + row % 4)
    asked_ref[...] = dot(pick, got[:, : GROUP * HD]).astype(bf16)


def vision_kernel(core_ref, patches_ref, gain_ref, own_ref, other_ref, window_ref, order_ref, out_ref):
    first = core_ref[0] == 0
    source = patches_ref[...].astype(f32)
    scale = lax.rsqrt(jnp.mean(source * source, axis=-1, keepdims=True) + 1e-06)
    normed = (source * scale * gain_ref[...]).astype(bf16)
    normed = dot(normed, order_ref[...]).astype(bf16)
    half = VD // 2
    left, right = normed[:, :half], normed[:, half:]
    mine = jnp.where(first, left.astype(f32), right.astype(f32)).astype(bf16)
    theirs = jnp.where(first, right.astype(f32), left.astype(f32)).astype(bf16)
    wide = 1024
    projected = dot(mine, own_ref[:, :wide]) + dot(theirs, other_ref[:, :wide])
    projected = projected.astype(bf16).astype(f32)
    query = pltpu.roll(projected[:, 0:384], 64, 1)
    key = projected[:, 256:640].astype(bf16)
    value = projected[:, 640:1024]
    shape = (FPATCH, UNITS)
    member = one_hot(window_ref[...] == iota(shape, 0) // 4)
    shape = (UNITS, 128)
    member = dot(member, one_hot(iota(shape, 0) // (WIN // 4) == iota(shape, 1))).astype(bf16)
    together = dot_t(member, member) > 0.5
    lane = iota((1, 384), 1)
    mixed = jnp.zeros((FPATCH, 384), f32)
    for h in range(HEADS):
        at = 64 + h * HEAD
        asking = jnp.where((lane >= at) & (lane < at + HEAD), query, 0.0).astype(bf16)
        scores = dot_t(asking, key) * HEAD ** (-0.5)
        scores = jnp.where(together, scores, NEGATIVE)
        weights = jnp.exp(scores - jnp.max(scores, axis=-1, keepdims=True))
        weights = (weights / jnp.sum(weights, axis=-1, keepdims=True)).astype(bf16)
        at = h * HEAD
        mixed += dot(weights, jnp.where((lane >= at) & (lane < at + HEAD), value, 0.0).astype(bf16))
    mixed = pltpu.roll(mixed, 64, 1).astype(bf16)
    shape = (FPATCH, FPATCH)
    row, col = iota(shape, 0), iota(shape, 1)
    mixed = dot(one_hot(col == (row % UNITS) * 4 + row // UNITS), mixed).astype(bf16)
    mine = dot_t(mixed, own_ref[:, 896:1280])
    theirs = dot_t(mixed, other_ref[:, 896:1280])
    left = jnp.where(first, mine, theirs)
    right = jnp.where(first, theirs, mine)
    summed = jnp.concatenate([left, right], axis=1).astype(bf16)
    out_ref[...] = dot_t(summed, order_ref[...]).astype(bf16)


def merge_kernel(place_ref, got_ref, patches_ref, gain_ref, out_ref):
    shape = (UNITS, FPATCH)
    pick = one_hot(iota(shape, 1) == iota(shape, 0) * 4 + place_ref[0])
    hidden = jnp.zeros((UNITS, VD), f32)
    for k in range(NX):
        hidden += got_ref[k * UNITS : (k + 1) * UNITS].astype(f32)
    hidden += dot(pick, patches_ref[...])
    scale = lax.rsqrt(jnp.mean(hidden * hidden, axis=-1, keepdims=True) + 1e-06)
    out_ref[...] = (hidden * scale * gain_ref[...]).astype(bf16)


def visual_kernel(merged_ref, weights_ref, out_ref, total_ref):
    step = pl.program_id(0)
    part = dot(merged_ref[...], weights_ref[...])

    @pl.when(step == 0)
    def _():
        total_ref[...] = part

    @pl.when(step > 0)
    def _():
        total_ref[...] += part

    @pl.when(step == 3)
    def _():
        visual = total_ref[...].astype(bf16)
        for k in range(LAYER):
            out_ref[k] = visual


def project_visual(merged, weights):
    return pl.pallas_call(
        visual_kernel,
        grid=(4,),
        in_specs=[
            pl.BlockSpec((UNITS, VD), lambda i: (i, 0)),
            pl.BlockSpec((VD, 512), lambda i: (i, 0)),
        ],
        out_specs=pl.BlockSpec((LAYER, UNITS, 512), lambda i: (0, 0, 0)),
        out_shape=jax.ShapeDtypeStruct((LAYER, UNITS, 512), bf16),
        scratch_shapes=[pltpu.VMEM((UNITS, 512), f32)],
        compiler_params=pltpu.CompilerParams(vmem_limit_bytes=40 << 20),
    )(merged, weights)


def attend_kernel(place_ref, visual_ref, asked_ref, range_ref, out_ref):
    layer, inner = place_ref[0], place_ref[1]
    count = NZ * 4 * GROUP
    tokens = LAYER * UNITS
    asking = jnp.concatenate([asked_ref[:, j * HD : (j + 1) * HD] for j in range(GROUP)], axis=0)
    row = iota((count, 1), 0)
    even = row % 2 == 0
    question = (((row // 4) % NZ) * LAYER + inner) * 2 + (row // 2) % 2
    pick = one_hot(iota((count, 256), 1) == question)
    bounds = dot(pick, range_ref[...].astype(f32).astype(bf16))
    lower, upper = bounds[:, 0:1], bounds[:, 1:2]
    frame = (layer * LAYER + iota((1, tokens), 1) // UNITS).astype(f32)
    live = (frame >= lower) & (frame < upper)
    scores = jnp.where(even, dot_t(asking, visual_ref[:, 0:128]), dot_t(asking, visual_ref[:, 128:256]))
    scores = jnp.where(live, scores * HD ** (-0.5), NEGATIVE)
    highest = jnp.max(scores, axis=-1, keepdims=True)
    weights = jnp.exp(scores - highest)
    total = jnp.sum(weights, axis=-1, keepdims=True)
    weights = weights.astype(bf16)
    mixed = jnp.where(even, dot(weights, visual_ref[:, 256:384]), dot(weights, visual_ref[:, 384:512]))
    mixed = mixed / total
    level = highest + jnp.log(total)
    high = level.astype(bf16).astype(f32)
    middle = (level - high).astype(bf16).astype(f32)
    low = level - high - middle
    lane = iota((1, HD), 1)
    levels = jnp.where(lane == 0, high, jnp.where(lane == 1, middle, jnp.where(lane == 2, low, 0.0)))
    sent = jnp.concatenate([mixed, levels], axis=1).astype(bf16)
    shape = (count, count)
    row, col = iota(shape, 0), iota(shape, 1)
    order = one_hot(col == (row % GROUP) * (NZ * 4) + row // GROUP)
    out_ref[...] = dot(order, sent).astype(bf16)


def answer_kernel(length_ref, got_ref, asking_ref, suffix_ref, out_ref):
    asking = asking_ref[...]
    count = asking.shape[0]
    span = suffix_ref.shape[0] // 2
    row = iota((count, 1), 0)
    even = (row // GROUP) % 2 == 0
    second = row // (2 * GROUP)
    scores = jnp.where(even, dot_t(asking, suffix_ref[:, 0:128]), dot_t(asking, suffix_ref[:, 128:256]))
    col = iota((1, 2 * span), 1)
    length = jnp.where(second == 0, length_ref[0], length_ref[1])
    live = (col // span == second) & (col % span < length)
    scores = jnp.where(live, scores * HD ** (-0.5), NEGATIVE)
    highest = jnp.max(scores, axis=-1, keepdims=True)
    weights = jnp.exp(scores - highest)
    total = jnp.sum(weights, axis=-1, keepdims=True)
    weights = weights.astype(bf16)
    mixed = jnp.where(even, dot(weights, suffix_ref[:, 256:384]), dot(weights, suffix_ref[:, 384:512]))
    levels = []
    top = highest
    for k in range(NZ):
        parts = got_ref[k * count : (k + 1) * count, HD:].astype(f32)
        level = parts[:, 0:1] + parts[:, 1:2] + parts[:, 2:3]
        levels.append(level)
        top = jnp.maximum(top, level)
    share = jnp.exp(highest - top)
    mixed = mixed * share
    total = total * share
    for k in range(NZ):
        share = jnp.exp(levels[k] - top)
        mixed += got_ref[k * count : (k + 1) * count, :HD].astype(f32) * share
        total += share
    out_ref[...] = (mixed / total).astype(bf16)


def on_device(
    patches,
    norm_gain,
    w_qkv,
    w_out,
    window_order,
    merge_gain,
    w_kv,
    queries,
    suffix_kv,
    question_lengths,
    frame_range,
):
    sds = jax.ShapeDtypeStruct
    layer = lax.axis_index("seq_0")
    inner = lax.axis_index(("seq_1", "seq_2"))
    core = lax.axis_index("seq_2")
    place = lax.axis_index("head")

    near = copies_over(w_kv.reshape(-1, 512), ("seq_1", "seq_2"), LAYER).reshape(-1, 512)
    packed = jnp.concatenate([w_qkv.reshape(ROWS, 3 * COLS), w_out.T], axis=1)
    asking = jnp.pad(queries.reshape(4, GROUP * HD), ((0, 2), (0, VD - GROUP * HD)))
    packed = jnp.concatenate([packed, asking], axis=0)
    packed, near = lax.optimization_barrier((packed, near))
    kv_weights = lax.all_gather(near, "seq_0", axis=0, tiled=True)

    got = copies_over(packed, "seq_0", NZ).reshape(NZ * 16, VD)
    weights, asked = call(
        compact_kernel,
        (sds((NY, NZ * ROWS, VD), bf16), sds((NZ * 4, GROUP * HD), bf16)),
        (got,),
    )
    own = lax.all_to_all(weights, "seq_1", split_axis=0, concat_axis=0, tiled=True).reshape(VD // 2, VD)
    other = lax.ppermute(own, "seq_2", [(0, 1), (1, 0)])
    order = jnp.asarray(row_order(), bf16)
    partial = call(
        vision_kernel,
        sds((FPATCH, VD), bf16),
        (core.reshape(1), patches, norm_gain.reshape(1, VD), own, other, window_order, order),
        [SMEM] + [VMEM] * 6,
    )
    partial = lax.all_to_all(
        partial.reshape(NX, UNITS, VD), "head", split_axis=0, concat_axis=0, tiled=True
    ).reshape(FPATCH, VD)
    merged = call(
        merge_kernel,
        sds((UNITS, VD), bf16),
        (place.reshape(1), partial, patches, merge_gain.reshape(1, VD)),
        [SMEM] + [VMEM] * 3,
    )
    merged = lax.all_gather(merged, "head", axis=0, tiled=True)
    visual = project_visual(merged, kv_weights)
    visual = lax.all_to_all(
        visual, ("seq_1", "seq_2"), split_axis=0, concat_axis=0, tiled=True
    ).reshape(LAYER * UNITS, 512)
    sent = call(
        attend_kernel,
        sds((NZ * 4 * GROUP, 2 * HD), bf16),
        (jnp.stack([layer, inner]), visual, asked, frame_range),
        [SMEM] + [VMEM] * 3,
    )
    got = lax.all_to_all(
        sent.reshape(NZ, 4 * GROUP, 2 * HD), "seq_0", split_axis=0, concat_axis=0, tiled=True
    ).reshape(-1, 2 * HD)
    answers = call(
        answer_kernel,
        sds((4 * GROUP, HD), bf16),
        (question_lengths, got, queries.reshape(4 * GROUP, HD), suffix_kv.reshape(-1, 512)),
        [SMEM] + [VMEM] * 3,
    )
    return answers.reshape(2, -1)


def solution(mesh):
    torus = Mesh(
        mesh.devices.reshape(NZ, NY, NC, NX), ("seq_0", "seq_1", "seq_2", "head")
    )
    in_specs = (
        P(SEQ, None),
        P(),
        P(SEQ, None, "head"),
        P("head", SEQ),
        P(SEQ, None),
        P(),
        P(SEQ, None, "head"),
        P(SEQ, "head"),
        P(SEQ, None, None, "head"),
        P(SEQ),
        P(),
    )
    return jax.shard_map(
        on_device, mesh=torus, in_specs=in_specs, out_specs=P(SEQ, "head"), check_vma=False
    )
```

time: 430 us -> 200 us (0.47)
  the two profiles are of different devices: /device:TPU:1 before, /device:TPU:64 now
where the time goes in v1:
time: 200 us
  blocking collectives  91.1 us (46%)
  waiting for transfers between devices  48.7 us (24%)
  starting transfers between devices  21.6 us (11%)
  Pallas kernels  14.7 us (7%)
  between operations  13.6 us (7%)
  local copies, waits for them, and re-layouts  9.12 us (5%)
    all_to_all x1, blocking collectives, copies_over(): return lax.all_to_all(copies, axes, split_axis=0, concat_axis=0, tiled=True)  57 us
    all_to_all x1, blocking collectives, on_device(): lax.all_to_all(weights, 'seq_1', split_axis=0, concat_axis=0, tiled=True)  20.3 us
    all_to_all x1, waiting for transfers between devices, on_device(): lax.all_to_all(sent.reshape(NZ, 4 * GROUP, 2 * HD), 'seq_0', split_axis=0...  18 us
    all_gather x1, blocking collectives, on_device(): merged = lax.all_gather(merged, 'head', axis=0, tiled=True)  13.8 us
    pallas_call x5, Pallas kernels, call(): pl.pallas_call(body, out_shape=outs, in_specs=specs or [vm] * len(operand...  12.4 us
    all_to_all x1, waiting for transfers between devices, on_device(): lax.all_to_all(partial.reshape(NX, UNITS, VD), 'head', split_axis=0, conc...  11.2 us
    all_to_all x1, waiting for transfers between devices, on_device(): lax.all_to_all(visual, ('seq_1', 'seq_2'), split_axis=0, concat_axis=0, t...  10 us
    all_to_all x1, starting transfers between devices, on_device(): lax.all_to_all(sent.reshape(NZ, 4 * GROUP, 2 * HD), 'seq_0', split_axis=0...  7.11 us
  transfers between devices with their start and end apart: 6, of which 5 were waited for; matrix products, arithmetic and copies ran while one was open for 1% of the time, Pallas kernels for 4%

profile of v1, /device:TPU:64, one launch (start us, length us, event | category | flops | bytes accessed | tf_op | source)
XLA Modules:
  0.0 199.6 jit_solution(17555570552585192810)
XLA Ops:
  6.5 0.8 copy.15
  7.3 0.7 broadcast_in_dim.14
  8.1 4.5 %all-to-all-start = ((bf16[8,40,512]{2,1,0:T(8,128)(2,1)}), bf16[8,40,512]{2,1,0:T(8,128)(2,1)S(1)}, u32[]{:S(2)}, u32[]{:S(2)}) async-start(bf16[8,40,512]{2,1,0:T(8,128)(2,1)} %broadcast_in_dim.14), calls=%async_computation | async-start | bytes 655360 | tf_op jit(solution)/shard_map/all_to_all | solution.py:56
  12.5 0.0 all-gather.2.cloned.1.call-start
  12.6 0.7 reshape.57
  13.3 0.8 reshape.56
  14.1 0.8 fusion.1
  14.9 5.9 %all-to-all-done = bf16[8,40,512]{2,1,0:T(8,128)(2,1)S(1)} async-done(((bf16[8,40,512]{2,1,0:T(8,128)(2,1)}), bf16[8,40,512]{2,1,0:T(8,128)(2,1)S(1)}, u32[]{:S(2)}, u32[]{:S(2)}) %all-to-all-start) | async-done | bytes 327712 | tf_op jit(solution)/shard_map/all_to_all | solution.py:56
  20.8 0.0 copy-start.5
  20.8 0.7 copy-done.5
  21.5 0.0 all-gather.2.cloned.1.call-update
  21.6 57.0 %all_to_all.30 = bf16[16,16,1280]{2,1,0:T(8,128)(2,1)S(1)} all-to-all(bf16[16,16,1280]{2,1,0:T(8,128)(2,1)S(1)} %broadcast_in_dim.15), channel_id=1, replica_groups=mesh['seq_0'=16,'seq_1'=4,'seq_2'=2,'head'=4] {'seq_0'}, dimensions={0} | all-to-all | bytes 1310720 | tf_op jit(solution)/shard_map/all_to_all | solution.py:56
  78.5 0.3 shard_map.118
  78.9 0.0 copy-start.8
  78.9 0.0 copy-start.2
  78.9 0.0 copy-start.3
  78.9 20.3 %all_to_all.31 = bf16[4,160,1280]{2,1,0:T(8,128)(2,1)S(1)} all-to-all(bf16[4,160,1280]{2,1,0:T(8,128)(2,1)S(1)} %get-tuple-element.10), channel_id=1, replica_groups=mesh['seq_0'=16,'seq_1'=4,'seq_2'=2,'head'=4] {'seq_1'}, dimensions={0} | all-to-all | bytes 3276800 | tf_op jit(solution)/shard_map/all_to_all | solution.py:277
  99.2 1.9 collective-permute-start
  101.2 0.0 copy-done.8
  101.2 3.6 %collective-permute-done.other_ref = bf16[640,1280]{1,0:T(8,128)(2,1)} collective-permute-done((bf16[640,1280]{1,0:T(8,128)(2,1)S(1)}, bf16[640,1280]{1,0:T(8,128)(2,1)}, u32[]{:S(2)}, u32[]{:S(2)}) %collective-permute-start) | collective-permute-done | bytes 1638432 | tf_op jit(solution)/shard_map/ppermute | solution.py:278
  104.7 0.0 copy-done.2
  104.8 0.0 copy-done.3
  104.8 0.0 copy-start.1
  104.8 2.0 copy-done.1
  106.7 0.0 copy-start.9
  106.7 7.8 %shard_map.119 = bf16[256,1280]{1,0:T(8,128)(2,1)} custom-call(s32[1]{0:T(128)} %bitcast.3.core_ref, bf16[256,1280]{1,0:T(8,128)(2,1)S(1)} %copy-done.2, f32[1,1280]{1,0:T(1,128)S(1)} %reshape.55.gain_ref, bf16[640,1280]{1,0:T(8,128)(2,1)S(1)} %bitcast.19, bf16[640,1280]{1,0:T(8,128)(2,1)} %collective-permute-done.other_ref, s32[1,64]{1,0:T(1,128)S(1)} %copy-done.3, ...), custom_call_target="tpu_custom_call" | custom-call | tf_op jit(solution)/shard_map/pallas_call | solution.py:61
  114.5 4.5 %all-to-all-start.3 = ((bf16[4,64,1280]{2,1,0:T(8,128)(2,1)}), bf16[4,64,1280]{2,1,0:T(8,128)(2,1)S(1)}, u32[]{:S(2)}, u32[]{:S(2)}) async-start(bf16[4,64,1280]{2,1,0:T(8,128)(2,1)} %bitcast.8), calls=%async_computation.3 | async-start | bytes 1310720 | tf_op jit(solution)/shard_map/all_to_all | solution.py:286
  119.0 0.0 copy-done.9
  119.0 11.2 %all-to-all-done.3 = bf16[4,64,1280]{2,1,0:T(8,128)(2,1)S(1)} async-done(((bf16[4,64,1280]{2,1,0:T(8,128)(2,1)}), bf16[4,64,1280]{2,1,0:T(8,128)(2,1)S(1)}, u32[]{:S(2)}, u32[]{:S(2)}) %all-to-all-start.3) | async-done | bytes 655392 | tf_op jit(solution)/shard_map/all_to_all | solution.py:286
  130.2 0.4 shard_map.120
  130.6 13.8 %all_gather.6.merged_ref = bf16[256,1280]{1,0:T(8,128)(2,1)S(1)} all-gather(bf16[64,1280]{1,0:T(8,128)(2,1)S(1)} %shard_map.120), channel_id=1, replica_groups=mesh['seq_0'=16,'seq_1'=4,'seq_2'=2,'head'=4] {'head'}, dimensions={0}, use_global_device_ids=true | all-gather | bytes 819200 | tf_op jit(solution)/shard_map/all_gather | solution.py:295
  144.4 0.0 all-gather.2.cloned.1.call-done.weights_ref
  144.4 0.0 copy-start
  144.4 2.5 %copy-done = bf16[5120,512]{1,0:T(8,128)(2,1)S(1)} copy-done((bf16[5120,512]{1,0:T(8,128)(2,1)S(1)}, bf16[5120,512]{1,0:T(8,128)(2,1)}, u32[]{:S(2)}) %copy-start) | copy-done | bytes 5242904
  146.9 2.3 %shard_map.121 = bf16[8,64,512]{2,1,0:T(8,128)(2,1)} custom-call(bf16[256,1280]{1,0:T(8,128)(2,1)S(1)} %all_gather.6.merged_ref, bf16[5120,512]{1,0:T(8,128)(2,1)S(1)} %copy-done), custom_call_target="tpu_custom_call" | custom-call | tf_op jit(solution)/shard_map/pallas_call | solution.py:163
  149.2 3.6 %all-to-all-start.4 = ((bf16[8,64,512]{2,1,0:T(8,128)(2,1)}), bf16[8,64,512]{2,1,0:T(8,128)(2,1)S(1)}, u32[]{:S(2)}, u32[]{:S(2)}) async-start(bf16[8,64,512]{2,1,0:T(8,128)(2,1)} %shard_map.121), calls=%async_computation.4 | async-start | bytes 1048576 | tf_op jit(solution)/shard_map/all_to_all | solution.py:297
  152.8 0.0 copy-done.10
  152.9 0.1 copy.14.range_ref
  153.0 0.1 pad_add_fusion.place_ref
  153.1 10.0 %all-to-all-done.4 = bf16[8,64,512]{2,1,0:T(8,128)(2,1)S(1)} async-done(((bf16[8,64,512]{2,1,0:T(8,128)(2,1)}), bf16[8,64,512]{2,1,0:T(8,128)(2,1)S(1)}, u32[]{:S(2)}, u32[]{:S(2)}) %all-to-all-start.4) | async-done | bytes 524320 | tf_op jit(solution)/shard_map/all_to_all | solution.py:297
  163.1 2.9 %shard_map.122 = bf16[512,256]{1,0:T(8,128)(2,1)} custom-call(s32[2]{0:T(128)S(1)} %pad_add_fusion.place_ref, bf16[512,512]{1,0:T(8,128)(2,1)S(1)} %bitcast.22, bf16[64,1024]{1,0:T(8,128)(2,1)S(1)} %get-tuple-element.12.asked_ref, s32[256,2]{1,0:T(8,128)S(1)} %copy.14.range_ref), custom_call_target="tpu_custom_call" | custom-call | tf_op jit(solution)/shard_map/pallas_call | solution.py:61
  166.0 7.1 %all-to-all-start.5 = ((bf16[16,32,256]{2,1,0:T(8,128)(2,1)}), bf16[16,32,256]{2,1,0:T(8,128)(2,1)S(1)}, u32[]{:S(2)}, u32[]{:S(2)}) async-start(bf16[16,32,256]{2,1,0:T(8,128)(2,1)} %bitcast.11), calls=%async_computation.5 | async-start | bytes 524288 | tf_op jit(solution)/shard_map/all_to_all | solution.py:306
  173.1 0.0 copy-done.7
  173.1 0.0 copy-done.6
  173.2 18.0 %all-to-all-done.5 = bf16[16,32,256]{2,1,0:T(8,128)(2,1)S(1)} async-done(((bf16[16,32,256]{2,1,0:T(8,128)(2,1)}), bf16[16,32,256]{2,1,0:T(8,128)(2,1)S(1)}, u32[]{:S(2)}, u32[]{:S(2)}) %all-to-all-start.5) | async-done | bytes 262176 | tf_op jit(solution)/shard_map/all_to_all | solution.py:306
  191.2 0.0 copy-done.4
  191.2 0.9 shard_map.123
  192.1 0.6 reshape.69
  (9 shorter events, 0.1 us)
Async XLA Ops:
  8.1 12.7 %all-to-all-start = ((bf16[8,40,512]{2,1,0:T(8,128)(2,1)}), bf16[8,40,512]{2,1,0:T(8,128)(2,1)S(1)}, u32[]{:S(2)}, u32[]{:S(2)}) async-start(bf16[8,40,512]{2,1,0:T(8,128)(2,1)} %broadcast_in_dim.14), calls=%async_computation | async-start | bytes 655360 | tf_op jit(solution)/shard_map/all_to_all | solution.py:56
  12.5 131.9 %all-gather.2.cloned.1.call-start = ((), (), s32[]{:S(2)}) async-start(), calls=%async_computation.6 | async-start | bytes 5570560 | tf_op jit(solution)/shard_map/all_gather | solution.py:269
  20.8 0.7 copy-start.5
  78.9 22.3 %copy-start.8 = (f32[1280]{0:T(1024)S(1)}, f32[1280]{0:T(1024)}, u32[]{:S(2)}) copy-start(f32[1280]{0:T(1024)} %param.13) | copy-start | bytes 15364
  78.9 25.9 %copy-start.2 = (bf16[256,1280]{1,0:T(8,128)(2,1)S(1)}, bf16[256,1280]{1,0:T(8,128)(2,1)}, u32[]{:S(2)}) copy-start(bf16[256,1280]{1,0:T(8,128)(2,1)} %patches_ref.3) | copy-start | bytes 1966084
  78.9 25.9 %copy-start.3 = (s32[1,64]{1,0:T(1,128)S(1)}, s32[1,64]{1,0:T(1,128)}, u32[]{:S(2)}) copy-start(s32[1,64]{1,0:T(1,128)} %window_ref.1) | copy-start | bytes 772
  99.2 5.5 %collective-permute-start = (bf16[640,1280]{1,0:T(8,128)(2,1)S(1)}, bf16[640,1280]{1,0:T(8,128)(2,1)}, u32[]{:S(2)}, u32[]{:S(2)}) collective-permute-start(bf16[640,1280]{1,0:T(8,128)(2,1)S(1)} %bitcast.18), channel_id=1, source_target_pairs={{0,4},{4,0},{1,5},{5,1},{2,6},{6,2},{3,7},{7,3},{8,12},{12,8},{9,1... | collective-permute-start | bytes 4915208 | tf_op jit(solution)/shard_map/ppermute | solution.py:278
  104.8 2.0 copy-start.1
  106.7 12.3 %copy-start.9 = (f32[1280]{0:T(1024)S(1)}, f32[1280]{0:T(1024)}, u32[]{:S(2)}) copy-start(f32[1280]{0:T(1024)} %param.17) | copy-start | bytes 15364
  114.5 15.7 %all-to-all-start.3 = ((bf16[4,64,1280]{2,1,0:T(8,128)(2,1)}), bf16[4,64,1280]{2,1,0:T(8,128)(2,1)S(1)}, u32[]{:S(2)}, u32[]{:S(2)}) async-start(bf16[4,64,1280]{2,1,0:T(8,128)(2,1)} %bitcast.8), calls=%async_computation.3 | async-start | bytes 1310720 | tf_op jit(solution)/shard_map/all_to_all | solution.py:286
  144.4 2.5 %copy-start = (bf16[5120,512]{1,0:T(8,128)(2,1)S(1)}, bf16[5120,512]{1,0:T(8,128)(2,1)}, u32[]{:S(2)}) copy-start(bf16[5120,512]{1,0:T(8,128)(2,1)} %all-gather.2.cloned.1.call-done.weights_ref) | copy-start | bytes 15728644
  146.9 5.9 %copy-start.10 = (s32[256,2]{0,1:T(2,128)S(1)}, s32[256,2]{0,1:T(2,128)}, u32[]{:S(2)}) copy-start(s32[256,2]{0,1:T(2,128)} %param.22) | copy-start | bytes 6148
  149.2 23.9 %copy-start.7 = (bf16[2,2048]{1,0:T(2,128)(2,1)S(1)}, bf16[2,2048]{1,0:T(2,128)(2,1)}, u32[]{:S(2)}) copy-start(bf16[2,2048]{1,0:T(2,128)(2,1)} %param.19) | copy-start | bytes 24580
  149.2 23.9 %copy-start.6 = (bf16[2,64,2,256]{3,2,1,0:T(2,128)(2,1)S(1)}, bf16[2,64,2,256]{3,2,1,0:T(2,128)(2,1)}, u32[]{:S(2)}) copy-start(bf16[2,64,2,256]{3,2,1,0:T(2,128)(2,1)} %param.20) | copy-start | bytes 393220
  149.2 42.0 %copy-start.4 = (s32[2]{0:T(128)S(1)}, s32[2]{0:T(128)}, u32[]{:S(2)}) copy-start(s32[2]{0:T(128)} %length_ref.1) | copy-start | bytes 28
  149.2 13.9 %all-to-all-start.4 = ((bf16[8,64,512]{2,1,0:T(8,128)(2,1)}), bf16[8,64,512]{2,1,0:T(8,128)(2,1)S(1)}, u32[]{:S(2)}, u32[]{:S(2)}) async-start(bf16[8,64,512]{2,1,0:T(8,128)(2,1)} %shard_map.121), calls=%async_computation.4 | async-start | bytes 1048576 | tf_op jit(solution)/shard_map/all_to_all | solution.py:297
  166.0 25.2 %all-to-all-start.5 = ((bf16[16,32,256]{2,1,0:T(8,128)(2,1)}), bf16[16,32,256]{2,1,0:T(8,128)(2,1)S(1)}, u32[]{:S(2)}, u32[]{:S(2)}) async-start(bf16[16,32,256]{2,1,0:T(8,128)(2,1)} %bitcast.11), calls=%async_computation.5 | async-start | bytes 524288 | tf_op jit(solution)/shard_map/all_to_all | solution.py:306
Sparse Core Ops, SparseCore 0:
  21.6 104.5 all-gather.1

commit v2 on v1

v2 whole, which is shorter than its diff:
```python
import jax
import jax.numpy as jnp
from jax import lax
from jax.experimental import pallas as pl
from jax.experimental.pallas import tpu as pltpu
from jax.sharding import Mesh
from jax.sharding import PartitionSpec as P

VD = 1280
VH = 16
HD = 128
FPATCH = 256
WIN = 64
SEQ = ("seq_0", "seq_1", "seq_2")
NZ, NY, NC, NX = 16, 4, 2, 4
ROWS = VD // (NZ * NY * NC)
PACKED = 24
COLS = VD // NX
HEAD = VD // VH
HEADS = COLS // HEAD
UNITS = FPATCH // 4
GROUP = 8
LAYER = NY * NC
NEGATIVE = -1e30
f32 = jnp.float32
bf16 = jnp.bfloat16


def dot(a, b):
    return lax.dot_general(a, b, (((1,), (0,)), ((), ())), preferred_element_type=f32)


def dot_t(a, b):
    return lax.dot_general(a, b, (((1,), (1,)), ((), ())), preferred_element_type=f32)


def iota(shape, dim):
    return lax.broadcasted_iota(jnp.int32, shape, dim)


def one_hot(condition):
    return jnp.where(condition, 1.0, 0.0).astype(bf16)


def copies_over(value, axes, count):
    copies = jnp.broadcast_to(value[None], (count, *value.shape))
    return lax.all_to_all(copies, axes, split_axis=0, concat_axis=0, tiled=True)


def call(body, outs, operands, specs=None, vmem=40 << 20):
    vm = pl.BlockSpec(memory_space=pltpu.VMEM)
    return pl.pallas_call(
        body,
        out_shape=outs,
        in_specs=specs or [vm] * len(operands),
        out_specs=jax.tree.map(lambda _: vm, outs),
        compiler_params=pltpu.CompilerParams(vmem_limit_bytes=vmem),
    )(*operands)


VMEM = pl.BlockSpec(memory_space=pltpu.VMEM)
SMEM = pl.BlockSpec(memory_space=pltpu.SMEM)


def prepare_kernel(
    length_ref, place_ref, patches_ref, gain_ref, merge_gain_ref, window_ref, asking_ref, suffix_ref,
    normed_ref, source_ref, merge_ref, order_ref, member_ref, mixed_ref, level_ref,
):
    shape = (VD, VD)
    row = iota((VD, 1), 0)
    z, y, c, r = row // (VD // NZ), row // (NC * ROWS) % NY, row // ROWS % NC, row % ROWS
    target = ((c + place_ref[2]) % NC) * (VD // NC) + (y * NZ + z) * ROWS + r
    order = one_hot(iota(shape, 1) == target)
    order_ref[...] = order
    source = patches_ref[...].astype(f32)
    scale = lax.rsqrt(jnp.mean(source * source, axis=-1, keepdims=True) + 1e-06)
    normed = (source * scale * gain_ref[...]).astype(bf16)
    normed_ref[...] = dot(normed, order).astype(bf16)
    shape = (UNITS, FPATCH)
    pick = one_hot(iota(shape, 1) == iota(shape, 0) * 4 + place_ref[3])
    source_ref[...] = dot(dot(pick, patches_ref[...]).astype(bf16), order)
    gain = merge_gain_ref[...]
    high = gain.astype(bf16).astype(f32)
    middle = (gain - high).astype(bf16).astype(f32)
    low = gain - high - middle
    part = iota((8, 1), 0)
    parts = jnp.where(part == 0, high, jnp.where(part == 1, middle, jnp.where(part == 2, low, 0.0)))
    merge_ref[...] = jnp.sum(dot(parts.astype(bf16), order), axis=0, keepdims=True)
    member = one_hot(window_ref[...] == iota((FPATCH, UNITS), 0) // 4)
    shape = (UNITS, 128)
    member_ref[...] = dot(member, one_hot(iota(shape, 0) // (WIN // 4) == iota(shape, 1))).astype(bf16)

    asking = asking_ref[...]
    count = asking.shape[0]
    span = suffix_ref.shape[0] // 2
    row = iota((count, 1), 0)
    even = (row // GROUP) % 2 == 0
    second = row // (2 * GROUP)
    scores = jnp.where(even, dot_t(asking, suffix_ref[:, 0:128]), dot_t(asking, suffix_ref[:, 128:256]))
    col = iota((1, 2 * span), 1)
    length = jnp.where(second == 0, length_ref[0], length_ref[1])
    live = (col // span == second) & (col % span < length)
    scores = jnp.where(live, scores * HD ** (-0.5), NEGATIVE)
    highest = jnp.max(scores, axis=-1, keepdims=True)
    weights = jnp.exp(scores - highest)
    total = jnp.sum(weights, axis=-1, keepdims=True)
    weights = weights.astype(bf16)
    mixed_ref[...] = jnp.where(even, dot(weights, suffix_ref[:, 256:384]), dot(weights, suffix_ref[:, 384:512]))
    lane = iota((1, HD), 1)
    level_ref[...] = jnp.where(lane == 0, highest, total)


def compact_kernel(got_ref, weights_ref):
    got = got_ref[...]
    shape = (NZ * ROWS, NZ * PACKED)
    row, col = iota(shape, 0), iota(shape, 1)
    for half in range(2):
        pick = one_hot(col == (row // ROWS) * PACKED + half * ROWS + row % ROWS)
        weights = dot(pick, got).astype(bf16)
        for k in range(NY):
            weights_ref[k, :, half * 640 : (half + 1) * 640] = weights


def vision_kernel(normed_ref, own_ref, other_ref, member_ref, out_ref):
    wide = 1024
    half = VD // 2
    projected = dot(normed_ref[:, :half], own_ref[:, :wide]) + dot(normed_ref[:, half:], other_ref[:, :wide])
    projected = projected.astype(bf16).astype(f32)
    query = pltpu.roll(projected[:, 0:384], 64, 1)
    key = projected[:, 256:640].astype(bf16)
    value = projected[:, 640:1024]
    together = dot_t(member_ref[...], member_ref[...]) > 0.5
    lane = iota((1, 384), 1)
    mixed = jnp.zeros((FPATCH, 384), f32)
    for h in range(HEADS):
        at = 64 + h * HEAD
        asking = jnp.where((lane >= at) & (lane < at + HEAD), query, 0.0).astype(bf16)
        scores = dot_t(asking, key) * HEAD ** (-0.5)
        scores = jnp.where(together, scores, NEGATIVE)
        weights = jnp.exp(scores - jnp.max(scores, axis=-1, keepdims=True))
        weights = (weights / jnp.sum(weights, axis=-1, keepdims=True)).astype(bf16)
        at = h * HEAD
        mixed += dot(weights, jnp.where((lane >= at) & (lane < at + HEAD), value, 0.0).astype(bf16))
    mixed = pltpu.roll(mixed, 64, 1).astype(bf16)
    shape = (FPATCH, FPATCH)
    row, col = iota(shape, 0), iota(shape, 1)
    mixed = dot(one_hot(col == (row % UNITS) * 4 + row // UNITS), mixed).astype(bf16)
    out_ref[:, :half] = dot_t(mixed, own_ref[:, 896:1280]).astype(bf16)
    out_ref[:, half:] = dot_t(mixed, other_ref[:, 896:1280]).astype(bf16)


def merge_kernel(got_ref, source_ref, gain_ref, order_ref, out_ref):
    hidden = source_ref[...]
    for k in range(NX):
        hidden += got_ref[k * UNITS : (k + 1) * UNITS].astype(f32)
    scale = lax.rsqrt(jnp.mean(hidden * hidden, axis=-1, keepdims=True) + 1e-06)
    merged = (hidden * scale * gain_ref[...]).astype(bf16)
    out_ref[...] = dot_t(merged, order_ref[...]).astype(bf16)


def visual_kernel(merged_ref, weights_ref, out_ref, held_ref, sems):
    rows = 4 * VD // NZ

    def copy(k):
        return pltpu.make_async_copy(
            weights_ref.at[k, pl.ds(0, rows)], held_ref.at[pl.ds(k * rows, rows)], sems.at[k]
        )

    for k in range(NZ):
        copy(k).start()
    total = jnp.zeros((UNITS, 512), f32)
    for i in range(4):
        for k in range(4):
            copy(i * 4 + k).wait()
        total += dot(merged_ref[i * UNITS : (i + 1) * UNITS], held_ref[i * VD : (i + 1) * VD])
    visual = total.astype(bf16)
    for k in range(LAYER):
        out_ref[k] = visual


def attend_kernel(place_ref, visual_ref, asked_ref, range_ref, out_ref):
    layer, inner = place_ref[0], place_ref[1]
    count = NZ * 4 * GROUP
    tokens = LAYER * UNITS
    asked = asked_ref[...]
    asking = jnp.concatenate([asked[:, b * HD : (b + 1) * HD] for b in range(4)], axis=0)
    row = iota((count, 1), 0)
    even = row % 4 < 2
    question = ((row // 8) % NZ * LAYER + inner) * 2 + (row // 4) % 2
    pick = one_hot(iota((count, 256), 1) == question)
    bounds = dot(pick, range_ref[...].astype(f32).astype(bf16))
    lower, upper = bounds[:, 0:1], bounds[:, 1:2]
    frame = (layer * LAYER + iota((1, tokens), 1) // UNITS).astype(f32)
    live = (frame >= lower) & (frame < upper)
    scores = jnp.where(even, dot_t(asking, visual_ref[:, 0:128]), dot_t(asking, visual_ref[:, 128:256]))
    scores = jnp.where(live, scores * HD ** (-0.5), NEGATIVE)
    highest = jnp.max(scores, axis=-1, keepdims=True)
    weights = jnp.exp(scores - highest)
    total = jnp.sum(weights, axis=-1, keepdims=True)
    weights = weights.astype(bf16)
    mixed = jnp.where(even, dot(weights, visual_ref[:, 256:384]), dot(weights, visual_ref[:, 384:512]))
    mixed = mixed / total
    level = highest + jnp.log(total)
    high = level.astype(bf16).astype(f32)
    middle = (level - high).astype(bf16).astype(f32)
    low = level - high - middle
    lane = iota((1, HD), 1)
    levels = jnp.where(lane == 0, high, jnp.where(lane == 1, middle, jnp.where(lane == 2, low, 0.0)))
    sent = jnp.concatenate([mixed, levels], axis=1).astype(bf16)
    shape = (count, count)
    row, col = iota(shape, 0), iota(shape, 1)
    head = row % 16
    order = one_hot(col == (head % 4) * (NZ * 8) + row // 32 * 8 + row // 16 % 2 * 4 + head // 4)
    out_ref[...] = dot(order, sent).astype(bf16)


def answer_kernel(got_ref, mixed_ref, level_ref, out_ref):
    count = mixed_ref.shape[0]
    highest, total = level_ref[:, 0:1], level_ref[:, 1:2]
    levels = []
    top = highest
    for k in range(NZ):
        parts = got_ref[k * count : (k + 1) * count, HD:].astype(f32)
        level = parts[:, 0:1] + parts[:, 1:2] + parts[:, 2:3]
        levels.append(level)
        top = jnp.maximum(top, level)
    share = jnp.exp(highest - top)
    mixed = mixed_ref[...] * share
    total = total * share
    for k in range(NZ):
        share = jnp.exp(levels[k] - top)
        mixed += got_ref[k * count : (k + 1) * count, :HD].astype(f32) * share
        total += share
    mixed = mixed / total
    heads = count // 2
    for h in range(heads):
        pair = jnp.concatenate([mixed[h : h + 1], mixed[heads + h : heads + h + 1]], axis=0)
        out_ref[:, h * HD : (h + 1) * HD] = pair.astype(bf16)


def on_device(
    patches,
    norm_gain,
    w_qkv,
    w_out,
    window_order,
    merge_gain,
    w_kv,
    queries,
    suffix_kv,
    question_lengths,
    frame_range,
):
    sds = jax.ShapeDtypeStruct
    barrier = lax.optimization_barrier
    layer = lax.axis_index("seq_0")
    inner = lax.axis_index(("seq_1", "seq_2"))
    place = jnp.stack([layer, inner, lax.axis_index("seq_2"), lax.axis_index("head")])

    near = copies_over(w_kv.reshape(-1, 512), ("seq_1", "seq_2"), LAYER).reshape(-1, 512)
    packed = jnp.concatenate([w_qkv.reshape(ROWS, 3 * COLS), w_out.T], axis=1)
    packed = jnp.concatenate(
        [packed[:, :640], packed[:, 640:], jnp.zeros((PACKED - 2 * ROWS, 640), bf16)], axis=0
    )
    packed, near = barrier((packed, near))
    asked = jnp.concatenate([queries.reshape(8, 512), jnp.zeros((8, 512), bf16)], axis=0)
    near = jnp.concatenate([near, asked], axis=0)
    far = lax.all_gather(near, "seq_0", axis=0)

    prepared = call(
        prepare_kernel,
        (
            sds((FPATCH, VD), bf16),
            sds((UNITS, VD), f32),
            sds((1, VD), f32),
            sds((VD, VD), bf16),
            sds((FPATCH, 128), bf16),
            sds((4 * GROUP, HD), f32),
            sds((4 * GROUP, HD), f32),
        ),
        (
            question_lengths, place, patches, norm_gain.reshape(1, VD), merge_gain.reshape(1, VD),
            window_order, queries.reshape(4 * GROUP, HD), suffix_kv.reshape(-1, 512),
        ),
        [SMEM] * 2 + [VMEM] * 6,
    )
    got = copies_over(packed, "seq_0", NZ).reshape(NZ * PACKED, 640)
    got, prepared, place, ranges = barrier((got, prepared, place, frame_range))
    normed, source, merge, order, member, mixed, level = prepared
    weights = call(compact_kernel, sds((NY, NZ * ROWS, VD), bf16), (got,))
    own = lax.all_to_all(weights, "seq_1", split_axis=0, concat_axis=0, tiled=True).reshape(VD // 2, VD)
    other = lax.ppermute(own, "seq_2", [(0, 1), (1, 0)])
    partial = call(vision_kernel, sds((FPATCH, VD), bf16), (normed, own, other, member))
    partial = lax.all_to_all(
        partial.reshape(NX, UNITS, VD), "head", split_axis=0, concat_axis=0, tiled=True
    ).reshape(FPATCH, VD)
    merged = call(merge_kernel, sds((UNITS, VD), bf16), (partial, source, merge, order))
    merged = lax.all_gather(merged, "head", axis=0, tiled=True)
    visual = pl.pallas_call(
        visual_kernel,
        out_shape=sds((LAYER, UNITS, 512), bf16),
        in_specs=[VMEM, pl.BlockSpec(memory_space=pltpu.HBM)],
        out_specs=VMEM,
        scratch_shapes=[pltpu.VMEM((4 * VD, 512), bf16), pltpu.SemaphoreType.DMA((NZ,))],
        compiler_params=pltpu.CompilerParams(vmem_limit_bytes=40 << 20),
    )(merged, far)
    asked = far[:, -16:-8].reshape(NZ * 8, 512)
    visual = lax.all_to_all(
        visual, ("seq_1", "seq_2"), split_axis=0, concat_axis=0, tiled=True
    ).reshape(LAYER * UNITS, 512)
    sent = call(
        attend_kernel,
        sds((NZ * 4 * GROUP, 2 * HD), bf16),
        (place, visual, asked, ranges),
        [SMEM] + [VMEM] * 3,
    )
    got = lax.all_to_all(
        sent.reshape(NZ, 4 * GROUP, 2 * HD), "seq_0", split_axis=0, concat_axis=0, tiled=True
    ).reshape(-1, 2 * HD)
    return call(answer_kernel, sds((2, 2 * GROUP * HD), bf16), (got, mixed, level))


def solution(mesh):
    torus = Mesh(
        mesh.devices.reshape(NZ, NY, NC, NX), ("seq_0", "seq_1", "seq_2", "head")
    )
    in_specs = (
        P(SEQ, None),
        P(),
        P(SEQ, None, "head"),
        P("head", SEQ),
        P(SEQ, None),
        P(),
        P(SEQ, None, "head"),
        P(SEQ, "head"),
        P(SEQ, None, None, "head"),
        P(SEQ),
        P(),
    )
    return jax.shard_map(
        on_device, mesh=torus, in_specs=in_specs, out_specs=P(SEQ, "head"), check_vma=False
    )
```

time: 200 us -> 188 us (0.940)
  blocking collectives: 91.1 us -> 78.1 us
  waiting for transfers between devices: 48.7 us -> 40.9 us
  starting transfers between devices: 21.6 us -> 24.8 us
  Pallas kernels: 14.7 us -> 17.6 us
    all_to_all x2 -> x0, waiting for transfers between devices: 29.2 us -> none  [the longest x1 18 us: on_device(): lax.all_to_all(sent.reshape(NZ, 4 * GROUP, 2 * HD), 'seq_0', split_axis=0...]
    all_to_all x1 -> x2, waiting for transfers between devices: 5.86 us -> 28.2 us  [copies_over(): return lax.all_to_all(copies, axes, split_axis=0, concat_axis=0, tiled=True)]
    all_to_all x1 -> x2, starting transfers between devices: 4.47 us -> 19.2 us  [copies_over(): return lax.all_to_all(copies, axes, split_axis=0, concat_axis=0, tiled=True)]
    all_to_all x1 -> x2, blocking collectives: 57 us -> 45.2 us  [the longest x1 30 us: on_device(): lax.all_to_all(sent.reshape(NZ, 4 * GROUP, 2 * HD), 'seq_0', split_axis=0...]
    all_to_all x2 -> x0, starting transfers between devices: 11.6 us -> none  [the longest x1 7.11 us: on_device(): lax.all_to_all(sent.reshape(NZ, 4 * GROUP, 2 * HD), 'seq_0', split_axis=0...]
    pallas_call x5 -> x6, Pallas kernels: 12.4 us -> 13.8 us  [call(): pl.pallas_call(body, out_shape=outs, in_specs=specs or [vm] * len(operand...]
    unnamed x25 -> x28, local copies, waits for them, and re-layouts: 6.15 us -> 6.14 us
  transfers between devices with their start and end apart: 6 -> 5, of which waited for: 5 -> 4; matrix products, arithmetic and copies ran while one was open for 1% -> 2% of each run, Pallas kernels for 4% -> 6%
where the time goes in v2:
time: 188 us; the launch traced here: 187 us
  blocking collectives  78.1 us (42%)
  waiting for transfers between devices  40.9 us (22%)
  starting transfers between devices  24.8 us (13%)
  Pallas kernels  17.6 us (9%)
  between operations  13.6 us (7%)
  local copies, waits for them, and re-layouts  10.5 us (6%)
    all_to_all x1, blocking collectives, on_device(): lax.all_to_all(sent.reshape(NZ, 4 * GROUP, 2 * HD), 'seq_0', split_axis=0...  30 us
    all_to_all x2, waiting for transfers between devices, copies_over(): return lax.all_to_all(copies, axes, split_axis=0, concat_axis=0, tiled=True)  28.2 us
    all_to_all x2, starting transfers between devices, copies_over(): return lax.all_to_all(copies, axes, split_axis=0, concat_axis=0, tiled=True)  19.2 us
    all_to_all x1, blocking collectives, on_device(): lax.all_to_all(weights, 'seq_1', split_axis=0, concat_axis=0, tiled=True)  19.2 us
    all_to_all x1, blocking collectives, on_device(): lax.all_to_all(partial.reshape(NX, UNITS, VD), 'head', split_axis=0, conc...  15.2 us
    pallas_call x6, Pallas kernels, call(): pl.pallas_call(body, out_shape=outs, in_specs=specs or [vm] * len(operand...  13.8 us
    all_gather x1, blocking collectives, on_device(): merged = lax.all_gather(merged, 'head', axis=0, tiled=True)  13.7 us
    all_to_all x1, waiting for transfers between devices, on_device(): lax.all_to_all(visual, ('seq_1', 'seq_2'), split_axis=0, concat_axis=0, t...  9.19 us
  transfers between devices with their start and end apart: 5, of which 4 were waited for; matrix products, arithmetic and copies ran while one was open for 2% of the time, Pallas kernels for 6%

profile of v2, /device:TPU:64, one launch (start us, length us, event | category | flops | bytes accessed | tf_op | source)
XLA Modules:
  0.0 187.2 jit_solution(9419371107675858937)
XLA Ops:
  6.5 0.0 copy-start.9
  6.5 0.0 copy-start.6
  6.6 0.8 copy.14
  7.4 0.7 broadcast_in_dim.21
  8.1 4.5 %all-to-all-start = ((bf16[8,40,512]{2,1,0:T(8,128)(2,1)}), bf16[8,40,512]{2,1,0:T(8,128)(2,1)S(1)}, u32[]{:S(2)}, u32[]{:S(2)}) async-start(bf16[8,40,512]{2,1,0:T(8,128)(2,1)} %broadcast_in_dim.21), calls=%async_computation | async-start | bytes 655360 | tf_op jit(solution)/shard_map/all_to_all | solution.py:47
  12.6 0.0 all-gather.3.cloned.1.call-start
  12.6 0.8 reshape.47
  13.5 0.7 reshape.57
  14.2 0.1 pad.9.clone
  14.3 0.1 pad.2.clone
  14.4 0.8 fusion.1
  15.2 5.7 %all-to-all-done = bf16[8,40,512]{2,1,0:T(8,128)(2,1)S(1)} async-done(((bf16[8,40,512]{2,1,0:T(8,128)(2,1)}), bf16[8,40,512]{2,1,0:T(8,128)(2,1)S(1)}, u32[]{:S(2)}, u32[]{:S(2)}) %all-to-all-start) | async-done | bytes 327712 | tf_op jit(solution)/shard_map/all_to_all | solution.py:47
  20.8 0.8 maximum_maximum_fusion
  21.7 0.0 all-gather.3.cloned.1.call-update
  21.7 0.8 broadcast_in_dim.22
  22.5 14.8 %all-to-all-start.1 = ((bf16[16,24,640]{2,1,0:T(8,128)(2,1)}), bf16[16,24,640]{2,1,0:T(8,128)(2,1)}, u32[]{:S(2)}, u32[]{:S(2)}) async-start(bf16[16,24,640]{2,1,0:T(8,128)(2,1)} %broadcast_in_dim.22), calls=%async_computation.1 | async-start | bytes 983040 | tf_op jit(solution)/shard_map/all_to_all | solution.py:47
  37.3 0.0 copy-done.9
  37.3 0.0 copy-done.8
  37.4 0.0 copy-done.10
  37.4 0.0 copy-done.11
  37.4 0.1 pad_add_fusion.place_ref
  37.5 0.0 copy-done.7
  37.5 0.0 copy-done.6
  37.5 1.1 copy-done.3
  38.6 4.6 %shard_map.109 = (bf16[256,1280]{1,0:T(8,128)(2,1)S(1)}, f32[64,1280]{1,0:T(8,128)S(1)}, f32[1,1280]{1,0:T(1,128)S(1)}, bf16[1280,1280]{1,0:T(8,128)(2,1)S(1)}, ...) custom-call(s32[2]{0:T(128)S(1)} %copy-done.6, s32[4]{0:T(128)S(1)} %pad_add_fusion.place_ref, ...), custom_call_target="tpu_custom_call" | custom-call | tf_op jit(solution)/shard_map/pallas_call | solution.py:52
  43.2 0.9 copy-done.1
  44.1 0.7 copy-done.4
  44.8 22.5 %all-to-all-done.1 = bf16[16,24,640]{2,1,0:T(8,128)(2,1)} async-done(((bf16[16,24,640]{2,1,0:T(8,128)(2,1)}), bf16[16,24,640]{2,1,0:T(8,128)(2,1)}, u32[]{:S(2)}, u32[]{:S(2)}) %all-to-all-start.1) | async-done | bytes 491552 | tf_op jit(solution)/shard_map/all_to_all | solution.py:47
  67.3 1.5 shard_map.110
  68.8 19.2 %all_to_all.30 = bf16[4,160,1280]{2,1,0:T(8,128)(2,1)S(1)} all-to-all(bf16[4,160,1280]{2,1,0:T(8,128)(2,1)S(1)} %shard_map.110), channel_id=1, replica_groups=mesh['seq_0'=16,'seq_1'=4,'seq_2'=2,'head'=4] {'seq_1'}, dimensions={0} | all-to-all | bytes 3276800 | tf_op jit(solution)/shard_map/all_to_all | solution.py:291
  88.0 2.0 %collective-permute-start = (bf16[640,1280]{1,0:T(8,128)(2,1)S(1)}, bf16[640,1280]{1,0:T(8,128)(2,1)S(1)}, u32[]{:S(2)}, u32[]{:S(2)}) collective-permute-start(bf16[640,1280]{1,0:T(8,128)(2,1)S(1)} %bitcast.21), channel_id=1, source_target_pairs={{0,4},{4,0},{1,5},{5,1},{2,6},{6,2},{3,7},{7,3},{8,12},{12,8},{9,1... | collective-permute-start | bytes 4915208 | tf_op jit(solution)/shard_map/ppermute | solution.py:292
  90.1 3.5 %collective-permute-done.other_ref = bf16[640,1280]{1,0:T(8,128)(2,1)S(1)} collective-permute-done((bf16[640,1280]{1,0:T(8,128)(2,1)S(1)}, bf16[640,1280]{1,0:T(8,128)(2,1)S(1)}, u32[]{:S(2)}, u32[]{:S(2)}) %collective-permute-start) | collective-permute-done | bytes 1638432 | tf_op jit(solution)/shard_map/ppermute | solution.py:292
  93.6 0.0 copy-done.2
  93.6 3.3 %shard_map.111 = bf16[256,1280]{1,0:T(8,128)(2,1)S(1)} custom-call(bf16[256,1280]{1,0:T(8,128)(2,1)S(1)} %copy-done.2, bf16[640,1280]{1,0:T(8,128)(2,1)S(1)} %bitcast.22, bf16[640,1280]{1,0:T(8,128)(2,1)S(1)} %collective-permute-done.other_ref, bf16[256,128]{1,0:T(8,128)(2,1)S(1)} %get-tuple-element.35.member_ref), custom_call_target="tpu_custom_call" | custom-call | tf_op jit(solution)/shard_map/pallas_call | solution.py:52
  96.9 15.2 %all_to_all.31 = bf16[4,64,1280]{2,1,0:T(8,128)(2,1)S(1)} all-to-all(bf16[4,64,1280]{2,1,0:T(8,128)(2,1)S(1)} %bitcast.25), channel_id=1, replica_groups=mesh['seq_0'=16,'seq_1'=4,'seq_2'=2,'head'=4] {'head'}, dimensions={0} | all-to-all | bytes 1310720 | tf_op jit(solution)/shard_map/all_to_all | solution.py:294
  112.1 0.0 copy-done.5
  112.1 1.2 shard_map.112
  113.3 13.7 %all_gather.9.merged_ref = bf16[256,1280]{1,0:T(8,128)(2,1)S(1)} all-gather(bf16[64,1280]{1,0:T(8,128)(2,1)S(1)} %shard_map.112), channel_id=1, replica_groups=mesh['seq_0'=16,'seq_1'=4,'seq_2'=2,'head'=4] {'head'}, dimensions={0}, use_global_device_ids=true | all-gather | bytes 819200 | tf_op jit(solution)/shard_map/all_gather | solution.py:298
  127.0 2.6 %copy-done = bf16[5376,512]{1,0:T(8,128)(2,1)S(1)} copy-done((bf16[5376,512]{1,0:T(8,128)(2,1)S(1)}, bf16[5376,512]{1,0:T(8,128)(2,1)}, u32[]{:S(2)}) %copy-start) | copy-done | bytes 5505048
  129.6 3.7 %shard_map.113 = bf16[8,64,512]{2,1,0:T(8,128)(2,1)} custom-call(bf16[256,1280]{1,0:T(8,128)(2,1)S(1)} %all_gather.9.merged_ref, bf16[16,336,512]{2,1,0:T(8,128)(2,1)S(1)} %bitcast.24), custom_call_target="tpu_custom_call" | custom-call | tf_op jit(solution)/shard_map/pallas_call | solution.py:299
  133.3 3.5 %all-to-all-start.4 = ((bf16[8,64,512]{2,1,0:T(8,128)(2,1)}), bf16[8,64,512]{2,1,0:T(8,128)(2,1)S(1)}, u32[]{:S(2)}, u32[]{:S(2)}) async-start(bf16[8,64,512]{2,1,0:T(8,128)(2,1)} %shard_map.113), calls=%async_computation.4 | async-start | bytes 1048576 | tf_op jit(solution)/shard_map/all_to_all | solution.py:308
  136.8 0.0 copy-done.12
  136.8 0.1 copy.13.range_ref
  137.0 0.9 slice_bitcast_fusion.asked_ref
  137.9 9.2 %all-to-all-done.4 = bf16[8,64,512]{2,1,0:T(8,128)(2,1)S(1)} async-done(((bf16[8,64,512]{2,1,0:T(8,128)(2,1)}), bf16[8,64,512]{2,1,0:T(8,128)(2,1)S(1)}, u32[]{:S(2)}, u32[]{:S(2)}) %all-to-all-start.4) | async-done | bytes 524320 | tf_op jit(solution)/shard_map/all_to_all | solution.py:308
  147.1 2.2 %shard_map.114 = bf16[512,256]{1,0:T(8,128)(2,1)S(1)} custom-call(s32[4]{0:T(128)S(1)} %pad_add_fusion.place_ref, bf16[512,512]{1,0:T(8,128)(2,1)S(1)} %bitcast.27, bf16[128,512]{1,0:T(8,128)(2,1)S(1)} %slice_bitcast_fusion.asked_ref, s32[256,2]{1,0:T(8,128)S(1)} %copy.13.range_ref), custom_call_target="tpu_custom_call" | custom-call | tf_op jit(solution)/shard_map/pallas_call | solution.py:52
  149.3 30.0 %all_to_all.32 = bf16[16,32,256]{2,1,0:T(8,128)(2,1)S(1)} all-to-all(bf16[16,32,256]{2,1,0:T(8,128)(2,1)S(1)} %bitcast.29), channel_id=1, replica_groups=mesh['seq_0'=16,'seq_1'=4,'seq_2'=2,'head'=4] {'seq_0'}, dimensions={0} | all-to-all | bytes 524288 | tf_op jit(solution)/shard_map/all_to_all | solution.py:317
  179.3 1.0 shard_map.115
  (19 shorter events, 0.1 us)
Async XLA Ops:
  6.5 30.8 %copy-start.9 = (bf16[2,2048]{1,0:T(2,128)(2,1)S(1)}, bf16[2,2048]{1,0:T(2,128)(2,1)}, u32[]{:S(2)}) copy-start(bf16[2,2048]{1,0:T(2,128)(2,1)} %param.18) | copy-start | bytes 24580
  6.5 30.8 %copy-start.8 = (bf16[2,64,2,256]{3,2,1,0:T(2,128)(2,1)S(1)}, bf16[2,64,2,256]{3,2,1,0:T(2,128)(2,1)}, u32[]{:S(2)}) copy-start(bf16[2,64,2,256]{3,2,1,0:T(2,128)(2,1)} %param.19) | copy-start | bytes 393220
  6.5 30.8 %copy-start.10 = (f32[1280]{0:T(1024)S(1)}, f32[1280]{0:T(1024)}, u32[]{:S(2)}) copy-start(f32[1280]{0:T(1024)} %param.12) | copy-start | bytes 15364
  6.5 30.8 %copy-start.11 = (f32[1280]{0:T(1024)S(1)}, f32[1280]{0:T(1024)}, u32[]{:S(2)}) copy-start(f32[1280]{0:T(1024)} %param.16) | copy-start | bytes 15364
  6.5 31.0 %copy-start.7 = (s32[1,64]{1,0:T(1,128)S(1)}, s32[1,64]{1,0:T(1,128)}, u32[]{:S(2)}) copy-start(s32[1,64]{1,0:T(1,128)} %window_ref.1) | copy-start | bytes 772
  6.5 30.9 %copy-start.6 = (s32[2]{0:T(128)S(1)}, s32[2]{0:T(128)}, u32[]{:S(2)}) copy-start(s32[2]{0:T(128)} %length_ref.1) | copy-start | bytes 28
  8.1 12.7 %all-to-all-start = ((bf16[8,40,512]{2,1,0:T(8,128)(2,1)}), bf16[8,40,512]{2,1,0:T(8,128)(2,1)S(1)}, u32[]{:S(2)}, u32[]{:S(2)}) async-start(bf16[8,40,512]{2,1,0:T(8,128)(2,1)} %broadcast_in_dim.21), calls=%async_computation | async-start | bytes 655360 | tf_op jit(solution)/shard_map/all_to_all | solution.py:47
  12.6 114.4 %all-gather.3.cloned.1.call-start = ((), (), s32[]{:S(2)}) async-start(), calls=%async_computation.6 | async-start | bytes 5849088 | tf_op jit(solution)/shard_map/all_gather | solution.py:268
  22.5 44.8 %all-to-all-start.1 = ((bf16[16,24,640]{2,1,0:T(8,128)(2,1)}), bf16[16,24,640]{2,1,0:T(8,128)(2,1)}, u32[]{:S(2)}, u32[]{:S(2)}) async-start(bf16[16,24,640]{2,1,0:T(8,128)(2,1)} %broadcast_in_dim.22), calls=%async_computation.1 | async-start | bytes 983040 | tf_op jit(solution)/shard_map/all_to_all | solution.py:47
  37.5 1.1 copy-start.3
  43.2 0.9 copy-start.1
  44.0 0.7 copy-start.4
  67.3 26.3 %copy-start.2 = (bf16[256,1280]{1,0:T(8,128)(2,1)S(1)}, bf16[256,1280]{1,0:T(8,128)(2,1)}, u32[]{:S(2)}) copy-start(bf16[256,1280]{1,0:T(8,128)(2,1)} %copy-done.1) | copy-start | bytes 1966084
  88.0 24.1 %copy-start.5 = (f32[64,1280]{1,0:T(8,128)S(1)}, f32[64,1280]{1,0:T(8,128)}, u32[]{:S(2)}) copy-start(f32[64,1280]{1,0:T(8,128)} %copy-done.4) | copy-start | bytes 983044
  88.0 5.5 %collective-permute-start = (bf16[640,1280]{1,0:T(8,128)(2,1)S(1)}, bf16[640,1280]{1,0:T(8,128)(2,1)S(1)}, u32[]{:S(2)}, u32[]{:S(2)}) collective-permute-start(bf16[640,1280]{1,0:T(8,128)(2,1)S(1)} %bitcast.21), channel_id=1, source_target_pairs={{0,4},{4,0},{1,5},{5,1},{2,6},{6,2},{3,7},{7,3},{8,12},{12,8},{9,1... | collective-permute-start | bytes 4915208 | tf_op jit(solution)/shard_map/ppermute | solution.py:292
  127.0 2.6 %copy-start = (bf16[5376,512]{1,0:T(8,128)(2,1)S(1)}, bf16[5376,512]{1,0:T(8,128)(2,1)}, u32[]{:S(2)}) copy-start(bf16[5376,512]{1,0:T(8,128)(2,1)} %all-gather.3.cloned.1.call-done) | copy-start | bytes 16515076
  129.6 7.3 %copy-start.12 = (s32[256,2]{0,1:T(2,128)S(1)}, s32[256,2]{0,1:T(2,128)}, u32[]{:S(2)}) copy-start(s32[256,2]{0,1:T(2,128)} %param.21) | copy-start | bytes 6148
  133.3 13.8 %all-to-all-start.4 = ((bf16[8,64,512]{2,1,0:T(8,128)(2,1)}), bf16[8,64,512]{2,1,0:T(8,128)(2,1)S(1)}, u32[]{:S(2)}, u32[]{:S(2)}) async-start(bf16[8,64,512]{2,1,0:T(8,128)(2,1)} %shard_map.113), calls=%async_computation.4 | async-start | bytes 1048576 | tf_op jit(solution)/shard_map/all_to_all | solution.py:308
Sparse Core Ops, SparseCore 0:
  21.8 99.8 all-gather.2

commit v3 on v2

--- a/solution.py
+++ b/solution.py
@@ -15,6 +15,7 @@
 NZ, NY, NC, NX = 16, 4, 2, 4
 ROWS = VD // (NZ * NY * NC)
 PACKED = 24
+SENT = 40
 COLS = VD // NX
 HEAD = VD // VH
 HEADS = COLS // HEAD
@@ -47,7 +48,7 @@
     return lax.all_to_all(copies, axes, split_axis=0, concat_axis=0, tiled=True)
 
 
-def call(body, outs, operands, specs=None, vmem=40 << 20):
+def call(body, outs, operands, specs=None, vmem=24 << 20):
     vm = pl.BlockSpec(memory_space=pltpu.VMEM)
     return pl.pallas_call(
         body,
@@ -64,14 +65,21 @@
 
 def prepare_kernel(
     length_ref, place_ref, patches_ref, gain_ref, merge_gain_ref, window_ref, asking_ref, suffix_ref,
-    normed_ref, source_ref, merge_ref, order_ref, member_ref, mixed_ref, level_ref,
+    normed_ref, source_ref, merge_ref, turn_ref, member_ref, mixed_ref, level_ref,
 ):
     shape = (VD, VD)
+    core, inner = place_ref[2], place_ref[1]
     row = iota((VD, 1), 0)
     z, y, c, r = row // (VD // NZ), row // (NC * ROWS) % NY, row // ROWS % NC, row % ROWS
-    target = ((c + place_ref[2]) % NC) * (VD // NC) + (y * NZ + z) * ROWS + r
+    target = ((c + core) % NC) * (VD // NC) + (y * NZ + z) * ROWS + r
     order = one_hot(iota(shape, 1) == target)
-    order_ref[...] = order
+    half, y, z, r = row // (VD // NC), row // (NZ * ROWS) % NY, row // ROWS % NZ, row % ROWS
+    natural = ((z * NY + y) * NC + (half + core) % NC) * ROWS + r
+    deep = 4 * ROWS
+    z, y, c, r = natural // (LAYER * deep), natural // (NC * deep) % NY, natural // deep % NC, natural % deep
+    away = (inner // NC - y + NY) % NY
+    target = ((c + core) % NC) * (VD // NC) + (z * NY + away) * deep + r
+    turn_ref[...] = one_hot(iota(shape, 1) == target)
     source = patches_ref[...].astype(f32)
     scale = lax.rsqrt(jnp.mean(source * source, axis=-1, keepdims=True) + 1e-06)
     normed = (source * scale * gain_ref[...]).astype(bf16)
@@ -149,30 +157,24 @@
     out_ref[:, half:] = dot_t(mixed, other_ref[:, 896:1280]).astype(bf16)
 
 
-def merge_kernel(got_ref, source_ref, gain_ref, order_ref, out_ref):
+def merge_kernel(got_ref, source_ref, gain_ref, turn_ref, out_ref):
     hidden = source_ref[...]
     for k in range(NX):
         hidden += got_ref[k * UNITS : (k + 1) * UNITS].astype(f32)
     scale = lax.rsqrt(jnp.mean(hidden * hidden, axis=-1, keepdims=True) + 1e-06)
     merged = (hidden * scale * gain_ref[...]).astype(bf16)
-    out_ref[...] = dot_t(merged, order_ref[...]).astype(bf16)
-
-
-def visual_kernel(merged_ref, weights_ref, out_ref, held_ref, sems):
-    rows = 4 * VD // NZ
-
-    def copy(k):
-        return pltpu.make_async_copy(
-            weights_ref.at[k, pl.ds(0, rows)], held_ref.at[pl.ds(k * rows, rows)], sems.at[k]
-        )
-
-    for k in range(NZ):
-        copy(k).start()
+    out_ref[...] = dot(merged, turn_ref[...]).astype(bf16)
+
+
+def visual_kernel(merged_ref, own_ref, other_ref, out_ref):
+    rows = 4 * NY * ROWS
+    half = VD // 2
     total = jnp.zeros((UNITS, 512), f32)
     for i in range(4):
-        for k in range(4):
-            copy(i * 4 + k).wait()
-        total += dot(merged_ref[i * UNITS : (i + 1) * UNITS], held_ref[i * VD : (i + 1) * VD])
+        merged = merged_ref[i * UNITS : (i + 1) * UNITS]
+        for part, ref in ((merged[:, :half], own_ref), (merged[:, half:], other_ref)):
+            weights = jnp.concatenate([ref[i * 4 + k, :rows] for k in range(4)], axis=0)
+            total += dot(part, weights)
     visual = total.astype(bf16)
     for k in range(LAYER):
         out_ref[k] = visual
@@ -205,23 +207,33 @@
     middle = (level - high).astype(bf16).astype(f32)
     low = level - high - middle
     lane = iota((1, HD), 1)
-    levels = jnp.where(lane == 0, high, jnp.where(lane == 1, middle, jnp.where(lane == 2, low, 0.0)))
-    sent = jnp.concatenate([mixed, levels], axis=1).astype(bf16)
-    shape = (count, count)
-    row, col = iota(shape, 0), iota(shape, 1)
-    head = row % 16
-    order = one_hot(col == (head % 4) * (NZ * 8) + row // 32 * 8 + row // 16 % 2 * 4 + head // 4)
-    out_ref[...] = dot(order, sent).astype(bf16)
+    place = row // 4 % 2 * 16 + row % 4 * 4 + row // (NZ * 8)
+    levels = jnp.where(
+        lane == place,
+        high,
+        jnp.where(lane == place + 32, middle, jnp.where(lane == place + 64, low, 0.0)),
+    )
+    shape = (NZ * SENT, count)
+    row, col = iota((NZ * SENT, 1), 0), iota(shape, 1)
+    z, at = row // SENT, row % SENT
+    head = at % 16
+    source = jnp.where(at < 32, (head % 4) * (NZ * 8) + z * 8 + at // 16 * 4 + head // 4, -1)
+    order = one_hot(col == source)
+    layers = one_hot(iota((1, count), 1) // 8 % NZ == jnp.where(at == 32, z, -1))
+    out_ref[...] = (dot(order, mixed.astype(bf16)) + dot(layers, levels.astype(bf16))).astype(bf16)
 
 
 def answer_kernel(got_ref, mixed_ref, level_ref, out_ref):
     count = mixed_ref.shape[0]
     highest, total = level_ref[:, 0:1], level_ref[:, 1:2]
+    got = got_ref[...].astype(f32)
+    shape = (count, HD)
+    mine = iota(shape, 1) % count == iota(shape, 0)
     levels = []
     top = highest
     for k in range(NZ):
-        parts = got_ref[k * count : (k + 1) * count, HD:].astype(f32)
-        level = parts[:, 0:1] + parts[:, 1:2] + parts[:, 2:3]
+        row = got[k * SENT + count : k * SENT + count + 1]
+        level = jnp.sum(jnp.where(mine, row, 0.0), axis=-1, keepdims=True)
         levels.append(level)
         top = jnp.maximum(top, level)
     share = jnp.exp(highest - top)
@@ -229,7 +241,7 @@
     total = total * share
     for k in range(NZ):
         share = jnp.exp(levels[k] - top)
-        mixed += got_ref[k * count : (k + 1) * count, :HD].astype(f32) * share
+        mixed += got[k * SENT : k * SENT + count] * share
         total += share
     mixed = mixed / total
     heads = count // 2
@@ -257,14 +269,14 @@
     inner = lax.axis_index(("seq_1", "seq_2"))
     place = jnp.stack([layer, inner, lax.axis_index("seq_2"), lax.axis_index("head")])
 
-    near = copies_over(w_kv.reshape(-1, 512), ("seq_1", "seq_2"), LAYER).reshape(-1, 512)
+    near = [w_kv.reshape(-1, 512)]
+    for away in range(1, NY):
+        near.append(lax.ppermute(near[0], "seq_1", [(k, (k + away) % NY) for k in range(NY)]))
     packed = jnp.concatenate([w_qkv.reshape(ROWS, 3 * COLS), w_out.T], axis=1)
     packed = jnp.concatenate(
         [packed[:, :640], packed[:, 640:], jnp.zeros((PACKED - 2 * ROWS, 640), bf16)], axis=0
     )
-    packed, near = barrier((packed, near))
-    asked = jnp.concatenate([queries.reshape(8, 512), jnp.zeros((8, 512), bf16)], axis=0)
-    near = jnp.concatenate([near, asked], axis=0)
+    near = jnp.concatenate([*near, queries.reshape(8, 512), jnp.zeros((8, 512), bf16)], axis=0)
     far = lax.all_gather(near, "seq_0", axis=0)
 
     prepared = call(
@@ -286,7 +298,7 @@
     )
     got = copies_over(packed, "seq_0", NZ).reshape(NZ * PACKED, 640)
     got, prepared, place, ranges = barrier((got, prepared, place, frame_range))
-    normed, source, merge, order, member, mixed, level = prepared
+    normed, source, merge, turn, member, mixed, level = prepared
     weights = call(compact_kernel, sds((NY, NZ * ROWS, VD), bf16), (got,))
     own = lax.all_to_all(weights, "seq_1", split_axis=0, concat_axis=0, tiled=True).reshape(VD // 2, VD)
     other = lax.ppermute(own, "seq_2", [(0, 1), (1, 0)])
@@ -294,29 +306,24 @@
     partial = lax.all_to_all(
         partial.reshape(NX, UNITS, VD), "head", split_axis=0, concat_axis=0, tiled=True
     ).reshape(FPATCH, VD)
-    merged = call(merge_kernel, sds((UNITS, VD), bf16), (partial, source, merge, order))
+    partial, far = barrier((partial, far))
+    far_other = lax.ppermute(far, "seq_2", [(0, 1), (1, 0)])
+    merged = call(merge_kernel, sds((UNITS, VD), bf16), (partial, source, merge, turn))
     merged = lax.all_gather(merged, "head", axis=0, tiled=True)
-    visual = pl.pallas_call(
-        visual_kernel,
-        out_shape=sds((LAYER, UNITS, 512), bf16),
-        in_specs=[VMEM, pl.BlockSpec(memory_space=pltpu.HBM)],
-        out_specs=VMEM,
-        scratch_shapes=[pltpu.VMEM((4 * VD, 512), bf16), pltpu.SemaphoreType.DMA((NZ,))],
-        compiler_params=pltpu.CompilerParams(vmem_limit_bytes=40 << 20),
-    )(merged, far)
+    visual = call(visual_kernel, sds((LAYER, UNITS, 512), bf16), (merged, far, far_other), vmem=24 << 20)
     asked = far[:, -16:-8].reshape(NZ * 8, 512)
     visual = lax.all_to_all(
         visual, ("seq_1", "seq_2"), split_axis=0, concat_axis=0, tiled=True
     ).reshape(LAYER * UNITS, 512)
     sent = call(
         attend_kernel,
-        sds((NZ * 4 * GROUP, 2 * HD), bf16),
+        sds((NZ * SENT, HD), bf16),
         (place, visual, asked, ranges),
         [SMEM] + [VMEM] * 3,
     )
     got = lax.all_to_all(
-        sent.reshape(NZ, 4 * GROUP, 2 * HD), "seq_0", split_axis=0, concat_axis=0, tiled=True
-    ).reshape(-1, 2 * HD)
+        sent.reshape(NZ, SENT, HD), "seq_0", split_axis=0, concat_axis=0, tiled=True
+    ).reshape(-1, HD)
     return call(answer_kernel, sds((2, 2 * GROUP * HD), bf16), (got, mixed, level))
 
 

time: 188 us -> 186 us (0.989)
  the two profiles are of different devices: /device:TPU:64 before, /device:TPU:1 now
where the time goes in v3:
time: 186 us; the launch traced here: 182 us
  blocking collectives  63.8 us (34%)
  starting transfers between devices  51.5 us (28%)
  waiting for transfers between devices  19.4 us (10%)
  Pallas kernels  19.3 us (10%)
  local copies, waits for them, and re-layouts  14.1 us (8%)
  between operations  13.5 us (7%)
    all_to_all x1, blocking collectives, on_device(): lax.all_to_all(sent.reshape(NZ, SENT, HD), 'seq_0', split_axis=0, concat_...  21.8 us
    pallas_call x7, Pallas kernels, call(): pl.pallas_call(body, out_shape=outs, in_specs=specs or [vm] * len(operand...  19.3 us
    all_to_all x1, blocking collectives, on_device(): lax.all_to_all(weights, 'seq_1', split_axis=0, concat_axis=0, tiled=True)  16.4 us
    all_to_all x1, starting transfers between devices, copies_over(): return lax.all_to_all(copies, axes, split_axis=0, concat_axis=0, tiled=True)  14.7 us
    all_to_all x1, blocking collectives, on_device(): lax.all_to_all(partial.reshape(NX, UNITS, VD), 'head', split_axis=0, conc...  14 us
    ppermute x1, starting transfers between devices, on_device(): other = lax.ppermute(own, 'seq_2', [(0, 1), (1, 0)])  13.5 us
    ppermute x3, starting transfers between devices, on_device(): lax.ppermute(near[0], 'seq_1', [(k, (k + away) % NY) for k in range(NY)])  11.5 us
    all_gather x1, blocking collectives, on_device(): merged = lax.all_gather(merged, 'head', axis=0, tiled=True)  11.5 us
  transfers between devices with their start and end apart: 8, of which 4 were waited for; matrix products, arithmetic and copies ran while one was open for 4% of the time, Pallas kernels for 7%

profile of v3, /device:TPU:1, one launch (start us, length us, event | category | flops | bytes accessed | tf_op | source)
XLA Modules:
  0.0 182.5 jit_solution(3348832555935590855)
XLA Ops:
  6.5 0.0 all-gather.3.cloned.1.call-start
  6.5 0.8 copy.15
  7.3 4.0 %collective-permute-start.1 = (bf16[40,512]{1,0:T(8,128)(2,1)S(1)}, bf16[40,512]{1,0:T(8,128)(2,1)S(1)}, u32[]{:S(2)}, u32[]{:S(2)}) collective-permute-start(bf16[40,512]{1,0:T(8,128)(2,1)S(1)} %bitcast.31), channel_id=1, source_target_pairs={{0,8},{8,16},{16,24},{24,0},{1,9},{9,17},{17,25},{25,1},{2,10},{10... | collective-permute-start | bytes 122888 | tf_op jit(solution)/shard_map/ppermute | solution.py:274
  11.4 4.5 %collective-permute-start.2 = (bf16[40,512]{1,0:T(8,128)(2,1)S(1)}, bf16[40,512]{1,0:T(8,128)(2,1)S(1)}, u32[]{:S(2)}, u32[]{:S(2)}) collective-permute-start(bf16[40,512]{1,0:T(8,128)(2,1)S(1)} %bitcast.32), channel_id=1, source_target_pairs={{0,16},{8,24},{16,0},{24,8},{1,17},{9,25},{17,1},{25,9},{2,18},{10... | collective-permute-start | bytes 122888 | tf_op jit(solution)/shard_map/ppermute | solution.py:274
  15.9 3.0 %collective-permute-start.3 = (bf16[40,512]{1,0:T(8,128)(2,1)S(1)}, bf16[40,512]{1,0:T(8,128)(2,1)S(1)}, u32[]{:S(2)}, u32[]{:S(2)}) collective-permute-start(bf16[40,512]{1,0:T(8,128)(2,1)S(1)} %bitcast.33), channel_id=1, source_target_pairs={{0,24},{8,0},{16,8},{24,16},{1,25},{9,1},{17,9},{25,17},{2,26},{10... | collective-permute-start | bytes 122888 | tf_op jit(solution)/shard_map/ppermute | solution.py:274
  18.9 0.8 reshape.46
  19.7 0.7 reshape.56
  20.5 0.1 pad.6.clone
  20.5 0.0 collective-permute-done.1
  20.5 0.0 collective-permute-done.2
  20.6 0.3 collective-permute-done.3
  20.9 0.7 copy-done.9
  21.6 0.0 all-gather.3.cloned.1.call-update
  21.6 0.8 fusion.1
  22.4 0.8 broadcast_in_dim.13
  23.2 14.7 %all-to-all-start = ((bf16[16,24,640]{2,1,0:T(8,128)(2,1)}), bf16[16,24,640]{2,1,0:T(8,128)(2,1)}, u32[]{:S(2)}, u32[]{:S(2)}) async-start(bf16[16,24,640]{2,1,0:T(8,128)(2,1)} %broadcast_in_dim.13), calls=%async_computation | async-start | bytes 983040 | tf_op jit(solution)/shard_map/all_to_all | solution.py:48
  37.9 0.7 reshape.50.asking_ref
  38.7 0.7 reshape.48.gain_ref
  39.4 0.7 reshape.49.merge_gain_ref
  40.1 0.9 copy.14
  41.0 0.1 pad_add_fusion.place_ref
  41.1 1.1 copy-done.4
  42.2 0.7 copy-done.7
  42.8 0.7 copy-done.8
  43.5 7.9 %shard_map.109 = (bf16[256,1280]{1,0:T(8,128)(2,1)S(1)}, f32[64,1280]{1,0:T(8,128)S(1)}, f32[1,1280]{1,0:T(1,128)S(1)}, bf16[1280,1280]{1,0:T(8,128)(2,1)S(1)}, ...) custom-call(s32[2]{0:T(128)S(1)} %copy-done.7, s32[4]{0:T(128)S(1)} %pad_add_fusion.place_ref, ...), custom_call_target="tpu_custom_call" | custom-call | tf_op jit(solution)/shard_map/pallas_call | solution.py:53
  51.3 0.9 copy-done.2
  52.2 0.7 copy-done.5
  52.9 7.5 %all-to-all-done = bf16[16,24,640]{2,1,0:T(8,128)(2,1)} async-done(((bf16[16,24,640]{2,1,0:T(8,128)(2,1)}), bf16[16,24,640]{2,1,0:T(8,128)(2,1)}, u32[]{:S(2)}, u32[]{:S(2)}) %all-to-all-start) | async-done | bytes 491552 | tf_op jit(solution)/shard_map/all_to_all | solution.py:48
  60.5 1.5 shard_map.110
  62.0 16.4 %all_to_all.25 = bf16[4,160,1280]{2,1,0:T(8,128)(2,1)S(1)} all-to-all(bf16[4,160,1280]{2,1,0:T(8,128)(2,1)S(1)} %shard_map.110), channel_id=1, replica_groups=mesh['seq_0'=16,'seq_1'=4,'seq_2'=2,'head'=4] {'seq_1'}, dimensions={0} | all-to-all | bytes 3276800 | tf_op jit(solution)/shard_map/all_to_all | solution.py:303
  78.4 13.5 %collective-permute-start = (bf16[640,1280]{1,0:T(8,128)(2,1)S(1)}, bf16[640,1280]{1,0:T(8,128)(2,1)S(1)}, u32[]{:S(2)}, u32[]{:S(2)}) collective-permute-start(bf16[640,1280]{1,0:T(8,128)(2,1)S(1)} %bitcast.20), channel_id=1, source_target_pairs={{0,4},{4,0},{1,5},{5,1},{2,6},{6,2},{3,7},{7,3},{8,12},{12,8},{9,1... | collective-permute-start | bytes 4915208 | tf_op jit(solution)/shard_map/ppermute | solution.py:304
  91.9 3.1 %collective-permute-done.other_ref = bf16[640,1280]{1,0:T(8,128)(2,1)S(1)} collective-permute-done((bf16[640,1280]{1,0:T(8,128)(2,1)S(1)}, bf16[640,1280]{1,0:T(8,128)(2,1)S(1)}, u32[]{:S(2)}, u32[]{:S(2)}) %collective-permute-start) | collective-permute-done | bytes 1638432 | tf_op jit(solution)/shard_map/ppermute | solution.py:304
  95.0 3.3 %shard_map.111 = bf16[256,1280]{1,0:T(8,128)(2,1)S(1)} custom-call(bf16[256,1280]{1,0:T(8,128)(2,1)S(1)} %copy-done.3, bf16[640,1280]{1,0:T(8,128)(2,1)S(1)} %bitcast.21, bf16[640,1280]{1,0:T(8,128)(2,1)S(1)} %collective-permute-done.other_ref, bf16[256,128]{1,0:T(8,128)(2,1)S(1)} %get-tuple-element.34.member_ref), custom_call_target="tpu_custom_call" | custom-call | tf_op jit(solution)/shard_map/pallas_call | solution.py:53
  98.3 14.0 %all_to_all.26 = bf16[4,64,1280]{2,1,0:T(8,128)(2,1)} all-to-all(bf16[4,64,1280]{2,1,0:T(8,128)(2,1)S(1)} %bitcast.25), channel_id=1, replica_groups=mesh['seq_0'=16,'seq_1'=4,'seq_2'=2,'head'=4] {'head'}, dimensions={0} | all-to-all | bytes 1310720 | tf_op jit(solution)/shard_map/all_to_all | solution.py:306
  112.4 5.6 %collective-permute-start.4 = (bf16[16,176,512]{2,1,0:T(8,128)(2,1)}, bf16[16,176,512]{2,1,0:T(8,128)(2,1)S(1)}, u32[]{:S(2)}, u32[]{:S(2)}) collective-permute-start(bf16[16,176,512]{2,1,0:T(8,128)(2,1)} %bitcast.22), channel_id=1, source_target_pairs={{0,4},{4,0},{1,5},{5,1},{2,6},{6,2},{3,7},{7,3},{8,12},{12,8},{9,1... | collective-permute-start | bytes 8650760 | tf_op jit(solution)/shard_map/ppermute | solution.py:310
  118.0 1.1 copy-done.1
  119.1 1.0 copy-done.6
  120.0 0.8 shard_map.112
  120.8 11.5 %all_gather.11.merged_ref = bf16[256,1280]{1,0:T(8,128)(2,1)S(1)} all-gather(bf16[64,1280]{1,0:T(8,128)(2,1)S(1)} %shard_map.112), channel_id=1, replica_groups=mesh['seq_0'=16,'seq_1'=4,'seq_2'=2,'head'=4] {'head'}, dimensions={0}, use_global_device_ids=true | all-gather | bytes 819200 | tf_op jit(solution)/shard_map/all_gather | solution.py:312
  132.3 0.0 collective-permute-done.4.other_ref
  132.4 1.8 %shard_map.113 = bf16[8,64,512]{2,1,0:T(8,128)(2,1)} custom-call(bf16[256,1280]{1,0:T(8,128)(2,1)S(1)} %all_gather.11.merged_ref, bf16[16,176,512]{2,1,0:T(8,128)(2,1)S(1)} %bitcast.24, bf16[16,176,512]{2,1,0:T(8,128)(2,1)S(1)} %collective-permute-done.4.other_ref), custom_call_target="tpu_custom_call" | custom-call | tf_op jit(solution)/shard_map/pallas_call | solution.py:53
  134.2 6.2 %all-to-all-start.3 = ((bf16[8,64,512]{2,1,0:T(8,128)(2,1)}), bf16[8,64,512]{2,1,0:T(8,128)(2,1)S(1)}, u32[]{:S(2)}, u32[]{:S(2)}) async-start(bf16[8,64,512]{2,1,0:T(8,128)(2,1)} %shard_map.113), calls=%async_computation.3 | async-start | bytes 1048576 | tf_op jit(solution)/shard_map/all_to_all | solution.py:315
  140.4 0.1 copy.13.range_ref
  140.5 0.9 slice_bitcast_fusion.asked_ref
  141.5 8.4 %all-to-all-done.3 = bf16[8,64,512]{2,1,0:T(8,128)(2,1)S(1)} async-done(((bf16[8,64,512]{2,1,0:T(8,128)(2,1)}), bf16[8,64,512]{2,1,0:T(8,128)(2,1)S(1)}, u32[]{:S(2)}, u32[]{:S(2)}) %all-to-all-start.3) | async-done | bytes 524320 | tf_op jit(solution)/shard_map/all_to_all | solution.py:315
  149.9 2.9 %shard_map.114 = bf16[640,128]{1,0:T(8,128)(2,1)S(1)} custom-call(s32[4]{0:T(128)S(1)} %pad_add_fusion.place_ref, bf16[512,512]{1,0:T(8,128)(2,1)S(1)} %bitcast.27, bf16[128,512]{1,0:T(8,128)(2,1)S(1)} %slice_bitcast_fusion.asked_ref, s32[256,2]{1,0:T(8,128)S(1)} %copy.13.range_ref), custom_call_target="tpu_custom_call" | custom-call | tf_op jit(solution)/shard_map/pallas_call | solution.py:53
  152.8 21.8 %all_to_all.27 = bf16[16,40,128]{2,1,0:T(8,128)(2,1)S(1)} all-to-all(bf16[16,40,128]{2,1,0:T(8,128)(2,1)S(1)} %bitcast.28), channel_id=1, replica_groups=mesh['seq_0'=16,'seq_1'=4,'seq_2'=2,'head'=4] {'seq_0'}, dimensions={0} | all-to-all | bytes 327680 | tf_op jit(solution)/shard_map/all_to_all | solution.py:324
  174.6 1.1 shard_map.115
  (23 shorter events, 0.1 us)
Async XLA Ops:
  6.5 105.8 %all-gather.3.cloned.1.call-start = ((), (), s32[]{:S(2)}) async-start(), calls=%async_computation.5 | async-start | bytes 3063808 | tf_op jit(solution)/shard_map/all_gather | solution.py:280
  7.3 13.2 %collective-permute-start.1 = (bf16[40,512]{1,0:T(8,128)(2,1)S(1)}, bf16[40,512]{1,0:T(8,128)(2,1)S(1)}, u32[]{:S(2)}, u32[]{:S(2)}) collective-permute-start(bf16[40,512]{1,0:T(8,128)(2,1)S(1)} %bitcast.31), channel_id=1, source_target_pairs={{0,8},{8,16},{16,24},{24,0},{1,9},{9,17},{17,25},{25,1},{2,10},{10... | collective-permute-start | bytes 122888 | tf_op jit(solution)/shard_map/ppermute | solution.py:274
  11.4 9.2 %collective-permute-start.2 = (bf16[40,512]{1,0:T(8,128)(2,1)S(1)}, bf16[40,512]{1,0:T(8,128)(2,1)S(1)}, u32[]{:S(2)}, u32[]{:S(2)}) collective-permute-start(bf16[40,512]{1,0:T(8,128)(2,1)S(1)} %bitcast.32), channel_id=1, source_target_pairs={{0,16},{8,24},{16,0},{24,8},{1,17},{9,25},{17,1},{25,9},{2,18},{10... | collective-permute-start | bytes 122888 | tf_op jit(solution)/shard_map/ppermute | solution.py:274
  15.9 5.0 %collective-permute-start.3 = (bf16[40,512]{1,0:T(8,128)(2,1)S(1)}, bf16[40,512]{1,0:T(8,128)(2,1)S(1)}, u32[]{:S(2)}, u32[]{:S(2)}) collective-permute-start(bf16[40,512]{1,0:T(8,128)(2,1)S(1)} %bitcast.33), channel_id=1, source_target_pairs={{0,24},{8,0},{16,8},{24,16},{1,25},{9,1},{17,9},{25,17},{2,26},{10... | collective-permute-start | bytes 122888 | tf_op jit(solution)/shard_map/ppermute | solution.py:274
  20.9 0.7 copy-start.9
  23.2 37.2 %all-to-all-start = ((bf16[16,24,640]{2,1,0:T(8,128)(2,1)}), bf16[16,24,640]{2,1,0:T(8,128)(2,1)}, u32[]{:S(2)}, u32[]{:S(2)}) async-start(bf16[16,24,640]{2,1,0:T(8,128)(2,1)} %broadcast_in_dim.13), calls=%async_computation | async-start | bytes 983040 | tf_op jit(solution)/shard_map/all_to_all | solution.py:48
  41.1 1.1 copy-start.4
  42.2 0.7 copy-start.7
  42.8 0.7 copy-start.8
  51.3 0.9 copy-start.2
  52.2 0.7 copy-start.5
  60.5 34.6 %copy-start.3 = (bf16[256,1280]{1,0:T(8,128)(2,1)S(1)}, bf16[256,1280]{1,0:T(8,128)(2,1)}, u32[]{:S(2)}) copy-start(bf16[256,1280]{1,0:T(8,128)(2,1)} %copy-done.2) | copy-start | bytes 1966084
  78.4 16.6 %collective-permute-start = (bf16[640,1280]{1,0:T(8,128)(2,1)S(1)}, bf16[640,1280]{1,0:T(8,128)(2,1)S(1)}, u32[]{:S(2)}, u32[]{:S(2)}) collective-permute-start(bf16[640,1280]{1,0:T(8,128)(2,1)S(1)} %bitcast.20), channel_id=1, source_target_pairs={{0,4},{4,0},{1,5},{5,1},{2,6},{6,2},{3,7},{7,3},{8,12},{12,8},{9,1... | collective-permute-start | bytes 4915208 | tf_op jit(solution)/shard_map/ppermute | solution.py:304
  112.4 20.0 %copy-start = (bf16[2816,512]{1,0:T(8,128)(2,1)S(1)}, bf16[2816,512]{1,0:T(8,128)(2,1)}, u32[]{:S(2)}) copy-start(bf16[2816,512]{1,0:T(8,128)(2,1)} %all-gather.3.cloned.1.call-done) | copy-start | bytes 8650756
  112.4 20.0 %collective-permute-start.4 = (bf16[16,176,512]{2,1,0:T(8,128)(2,1)}, bf16[16,176,512]{2,1,0:T(8,128)(2,1)S(1)}, u32[]{:S(2)}, u32[]{:S(2)}) collective-permute-start(bf16[16,176,512]{2,1,0:T(8,128)(2,1)} %bitcast.22), channel_id=1, source_target_pairs={{0,4},{4,0},{1,5},{5,1},{2,6},{6,2},{3,7},{7,3},{8,12},{12,8},{9,1... | collective-permute-start | bytes 8650760 | tf_op jit(solution)/shard_map/ppermute | solution.py:310
  118.0 1.1 copy-start.1
  119.1 1.0 copy-start.6
  132.3 8.1 %copy-start.10 = (s32[256,2]{0,1:T(2,128)S(1)}, s32[256,2]{0,1:T(2,128)}, u32[]{:S(2)}) copy-start(s32[256,2]{0,1:T(2,128)} %param.21) | copy-start | bytes 6148
  134.2 15.7 %all-to-all-start.3 = ((bf16[8,64,512]{2,1,0:T(8,128)(2,1)}), bf16[8,64,512]{2,1,0:T(8,128)(2,1)S(1)}, u32[]{:S(2)}, u32[]{:S(2)}) async-start(bf16[8,64,512]{2,1,0:T(8,128)(2,1)} %shard_map.113), calls=%async_computation.3 | async-start | bytes 1048576 | tf_op jit(solution)/shard_map/all_to_all | solution.py:315
Sparse Core Ops, SparseCore 0:
  21.7 86.0 all-gather.2

commit v4 on v3

--- a/solution.py
+++ b/solution.py
@@ -63,41 +63,47 @@
 SMEM = pl.BlockSpec(memory_space=pltpu.SMEM)
 
 
-def prepare_kernel(
-    length_ref, place_ref, patches_ref, gain_ref, merge_gain_ref, window_ref, asking_ref, suffix_ref,
-    normed_ref, source_ref, merge_ref, turn_ref, member_ref, mixed_ref, level_ref,
-):
-    shape = (VD, VD)
-    core, inner = place_ref[2], place_ref[1]
-    row = iota((VD, 1), 0)
-    z, y, c, r = row // (VD // NZ), row // (NC * ROWS) % NY, row // ROWS % NC, row % ROWS
+def places():
+    at = iota((VD, 1), 0)
+    return at // (NY * NC * ROWS), at // (NC * ROWS) % NY, at // ROWS % NC, at % ROWS
+
+
+def prepare_kernel(place_ref, patches_ref, gain_ref, window_ref, normed_ref, member_ref):
+    core = place_ref[2]
+    z, y, c, r = places()
     target = ((c + core) % NC) * (VD // NC) + (y * NZ + z) * ROWS + r
-    order = one_hot(iota(shape, 1) == target)
-    half, y, z, r = row // (VD // NC), row // (NZ * ROWS) % NY, row // ROWS % NZ, row % ROWS
-    natural = ((z * NY + y) * NC + (half + core) % NC) * ROWS + r
-    deep = 4 * ROWS
-    z, y, c, r = natural // (LAYER * deep), natural // (NC * deep) % NY, natural // deep % NC, natural % deep
-    away = (inner // NC - y + NY) % NY
-    target = ((c + core) % NC) * (VD // NC) + (z * NY + away) * deep + r
-    turn_ref[...] = one_hot(iota(shape, 1) == target)
+    order = one_hot(iota((VD, VD), 1) == target)
     source = patches_ref[...].astype(f32)
     scale = lax.rsqrt(jnp.mean(source * source, axis=-1, keepdims=True) + 1e-06)
     normed = (source * scale * gain_ref[...]).astype(bf16)
     normed_ref[...] = dot(normed, order).astype(bf16)
+    member = one_hot(window_ref[...] == iota((FPATCH, UNITS), 0) // 4)
+    shape = (UNITS, 128)
+    member_ref[...] = dot(member, one_hot(iota(shape, 0) // (WIN // 4) == iota(shape, 1))).astype(bf16)
+
+
+def residual_kernel(place_ref, patches_ref, gain_ref, source_ref, gains_ref, turn_ref):
+    core = place_ref[2]
+    z, y, c, r = places()
+    target = ((y // 2 + core) % NC) * (VD // NC) + ((c * 2 + y % 2) * NZ + z) * ROWS + r
+    order = one_hot(iota((VD, VD), 1) == target)
     shape = (UNITS, FPATCH)
     pick = one_hot(iota(shape, 1) == iota(shape, 0) * 4 + place_ref[3])
     source_ref[...] = dot(dot(pick, patches_ref[...]).astype(bf16), order)
-    gain = merge_gain_ref[...]
+    gain = gain_ref[...]
     high = gain.astype(bf16).astype(f32)
     middle = (gain - high).astype(bf16).astype(f32)
     low = gain - high - middle
     part = iota((8, 1), 0)
     parts = jnp.where(part == 0, high, jnp.where(part == 1, middle, jnp.where(part == 2, low, 0.0)))
-    merge_ref[...] = jnp.sum(dot(parts.astype(bf16), order), axis=0, keepdims=True)
-    member = one_hot(window_ref[...] == iota((FPATCH, UNITS), 0) // 4)
-    shape = (UNITS, 128)
-    member_ref[...] = dot(member, one_hot(iota(shape, 0) // (WIN // 4) == iota(shape, 1))).astype(bf16)
-
+    gains_ref[...] = jnp.sum(dot(parts.astype(bf16), order), axis=0, keepdims=True)
+    half = VD // 2
+    row = iota((half, 1), 0)
+    c, y, z, r = row // (2 * NZ * ROWS), row // (NZ * ROWS) % 2, row // ROWS % NZ, row % ROWS
+    turn_ref[...] = one_hot(iota((half, half), 1) == ((z * 2 + y) * NC + c) * ROWS + r)
+
+
+def suffix_kernel(length_ref, asking_ref, suffix_ref, mixed_ref, level_ref):
     asking = asking_ref[...]
     count = asking.shape[0]
     span = suffix_ref.shape[0] // 2
@@ -114,8 +120,7 @@
     total = jnp.sum(weights, axis=-1, keepdims=True)
     weights = weights.astype(bf16)
     mixed_ref[...] = jnp.where(even, dot(weights, suffix_ref[:, 256:384]), dot(weights, suffix_ref[:, 384:512]))
-    lane = iota((1, HD), 1)
-    level_ref[...] = jnp.where(lane == 0, highest, total)
+    level_ref[...] = jnp.where(iota((1, HD), 1) == 0, highest, total)
 
 
 def compact_kernel(got_ref, weights_ref):
@@ -129,7 +134,7 @@
             weights_ref[k, :, half * 640 : (half + 1) * 640] = weights
 
 
-def vision_kernel(normed_ref, own_ref, other_ref, member_ref, out_ref):
+def vision_kernel(place_ref, normed_ref, own_ref, other_ref, member_ref, out_ref):
     wide = 1024
     half = VD // 2
     projected = dot(normed_ref[:, :half], own_ref[:, :wide]) + dot(normed_ref[:, half:], other_ref[:, :wide])
@@ -153,8 +158,16 @@
     shape = (FPATCH, FPATCH)
     row, col = iota(shape, 0), iota(shape, 1)
     mixed = dot(one_hot(col == (row % UNITS) * 4 + row // UNITS), mixed).astype(bf16)
-    out_ref[:, :half] = dot_t(mixed, own_ref[:, 896:1280]).astype(bf16)
-    out_ref[:, half:] = dot_t(mixed, other_ref[:, 896:1280]).astype(bf16)
+
+    def project(core):
+        pair = (own_ref, other_ref) if core == 0 else (other_ref, own_ref)
+        for part in range(2):
+            rows = slice((part ^ core) * half // 2, ((part ^ core) + 1) * half // 2)
+            weights = jnp.concatenate([ref[rows, 896:1280] for ref in pair], axis=0)
+            out_ref[:, part * half : (part + 1) * half] = dot_t(mixed, weights).astype(bf16)
+
+    for core in range(NC):
+        pl.when(place_ref[2] == core)(lambda core=core: project(core))
 
 
 def merge_kernel(got_ref, source_ref, gain_ref, turn_ref, out_ref):
@@ -163,7 +176,10 @@
         hidden += got_ref[k * UNITS : (k + 1) * UNITS].astype(f32)
     scale = lax.rsqrt(jnp.mean(hidden * hidden, axis=-1, keepdims=True) + 1e-06)
     merged = (hidden * scale * gain_ref[...]).astype(bf16)
-    out_ref[...] = dot(merged, turn_ref[...]).astype(bf16)
+    half = VD // 2
+    for part in range(2):
+        at = slice(part * half, (part + 1) * half)
+        out_ref[:, at] = dot(merged[:, at], turn_ref[...]).astype(bf16)
 
 
 def visual_kernel(merged_ref, own_ref, other_ref, out_ref):
@@ -269,46 +285,44 @@
     inner = lax.axis_index(("seq_1", "seq_2"))
     place = jnp.stack([layer, inner, lax.axis_index("seq_2"), lax.axis_index("head")])
 
-    near = [w_kv.reshape(-1, 512)]
-    for away in range(1, NY):
-        near.append(lax.ppermute(near[0], "seq_1", [(k, (k + away) % NY) for k in range(NY)]))
+    near = copies_over(w_kv.reshape(-1, 512), "seq_1", NY).reshape(-1, 512)
     packed = jnp.concatenate([w_qkv.reshape(ROWS, 3 * COLS), w_out.T], axis=1)
     packed = jnp.concatenate(
         [packed[:, :640], packed[:, 640:], jnp.zeros((PACKED - 2 * ROWS, 640), bf16)], axis=0
     )
-    near = jnp.concatenate([*near, queries.reshape(8, 512), jnp.zeros((8, 512), bf16)], axis=0)
+    packed, near = barrier((packed, near))
+    near = jnp.concatenate([near, queries.reshape(8, 512), jnp.zeros((8, 512), bf16)], axis=0)
     far = lax.all_gather(near, "seq_0", axis=0)
-
-    prepared = call(
+    got = lax.all_gather(packed, "seq_0", axis=0, tiled=True)
+    weights = call(compact_kernel, sds((NY, NZ * ROWS, VD), bf16), (got,))
+
+    weights, patches, place, norm_gain, window_order = barrier((weights, patches, place, norm_gain, window_order))
+    normed, member = call(
         prepare_kernel,
-        (
-            sds((FPATCH, VD), bf16),
-            sds((UNITS, VD), f32),
-            sds((1, VD), f32),
-            sds((VD, VD), bf16),
-            sds((FPATCH, 128), bf16),
-            sds((4 * GROUP, HD), f32),
-            sds((4 * GROUP, HD), f32),
-        ),
-        (
-            question_lengths, place, patches, norm_gain.reshape(1, VD), merge_gain.reshape(1, VD),
-            window_order, queries.reshape(4 * GROUP, HD), suffix_kv.reshape(-1, 512),
-        ),
-        [SMEM] * 2 + [VMEM] * 6,
-    )
-    got = copies_over(packed, "seq_0", NZ).reshape(NZ * PACKED, 640)
-    got, prepared, place, ranges = barrier((got, prepared, place, frame_range))
-    normed, source, merge, turn, member, mixed, level = prepared
-    weights = call(compact_kernel, sds((NY, NZ * ROWS, VD), bf16), (got,))
+        (sds((FPATCH, VD), bf16), sds((FPATCH, 128), bf16)),
+        (place, patches, norm_gain.reshape(1, VD), window_order),
+        [SMEM] + [VMEM] * 3,
+    )
     own = lax.all_to_all(weights, "seq_1", split_axis=0, concat_axis=0, tiled=True).reshape(VD // 2, VD)
+    own, normed, member = barrier((own, normed, member))
     other = lax.ppermute(own, "seq_2", [(0, 1), (1, 0)])
-    partial = call(vision_kernel, sds((FPATCH, VD), bf16), (normed, own, other, member))
+    partial = call(
+        vision_kernel, sds((FPATCH, VD), bf16), (place, normed, own, other, member), [SMEM] + [VMEM] * 4
+    )
+
+    partial, patches, place, merge_gain = barrier((partial, patches, place, merge_gain))
+    source, gains, turn = call(
+        residual_kernel,
+        (sds((UNITS, VD), f32), sds((1, VD), f32), sds((VD // 2, VD // 2), bf16)),
+        (place, patches, merge_gain.reshape(1, VD)),
+        [SMEM] + [VMEM] * 2,
+    )
     partial = lax.all_to_all(
         partial.reshape(NX, UNITS, VD), "head", split_axis=0, concat_axis=0, tiled=True
     ).reshape(FPATCH, VD)
-    partial, far = barrier((partial, far))
+    partial, far, source, gains, turn = barrier((partial, far, source, gains, turn))
     far_other = lax.ppermute(far, "seq_2", [(0, 1), (1, 0)])
-    merged = call(merge_kernel, sds((UNITS, VD), bf16), (partial, source, merge, turn))
+    merged = call(merge_kernel, sds((UNITS, VD), bf16), (partial, source, gains, turn))
     merged = lax.all_gather(merged, "head", axis=0, tiled=True)
     visual = call(visual_kernel, sds((LAYER, UNITS, 512), bf16), (merged, far, far_other), vmem=24 << 20)
     asked = far[:, -16:-8].reshape(NZ * 8, 512)
@@ -318,12 +332,19 @@
     sent = call(
         attend_kernel,
         sds((NZ * SENT, HD), bf16),
-        (place, visual, asked, ranges),
+        (place, visual, asked, frame_range),
         [SMEM] + [VMEM] * 3,
     )
+    sent, queries, suffix_kv, question_lengths = barrier((sent, queries, suffix_kv, question_lengths))
     got = lax.all_to_all(
         sent.reshape(NZ, SENT, HD), "seq_0", split_axis=0, concat_axis=0, tiled=True
     ).reshape(-1, HD)
+    mixed, level = call(
+        suffix_kernel,
+        (sds((4 * GROUP, HD), f32), sds((4 * GROUP, HD), f32)),
+        (question_lengths, queries.reshape(4 * GROUP, HD), suffix_kv.reshape(-1, 512)),
+        [SMEM] + [VMEM] * 2,
+    )
     return call(answer_kernel, sds((2, 2 * GROUP * HD), bf16), (got, mixed, level))
 
 

time: 186 us -> 172 us (0.925)
  waiting for transfers between devices: 19.4 us -> 41.4 us
  blocking collectives: 63.8 us -> 45 us
  starting transfers between devices: 51.5 us -> 40.2 us
  local copies, waits for them, and re-layouts: 14.1 us -> 6.13 us
  Pallas kernels: 19.3 us -> 21.4 us
    all_to_all x3 -> x0, blocking collectives: 52.3 us -> none  [the longest x1 21.8 us: on_device(): lax.all_to_all(sent.reshape(NZ, SENT, HD), 'seq_0', split_axis=0, concat_...]
    all_gather x0 -> x1, blocking collectives: none -> 33.6 us  [on_device(): got = lax.all_gather(packed, 'seq_0', axis=0, tiled=True)]
    all_to_all x0 -> x3, waiting for transfers between devices: none -> 27.4 us  [the longest x1 11.2 us: on_device(): lax.all_to_all(sent.reshape(NZ, SENT, HD), 'seq_0', split_axis=0, concat_...]
    all_to_all x0 -> x3, starting transfers between devices: none -> 13.3 us  [the longest x1 5.86 us: on_device(): lax.all_to_all(sent.reshape(NZ, SENT, HD), 'seq_0', split_axis=0, concat_...]
    ppermute x3 -> x0, starting transfers between devices: 11.5 us -> none  [on_device(): lax.ppermute(near[0], 'seq_1', [(k, (k + away) % NY) for k in range(NY)])]
    all_to_all x1, starting transfers between devices: 14.7 us -> 5.01 us  [copies_over(): return lax.all_to_all(copies, axes, split_axis=0, concat_axis=0, tiled=True)]
    unnamed x29 -> x21, local copies, waits for them, and re-layouts: 8.46 us -> 2.78 us
    all_to_all x1, waiting for transfers between devices: 7.53 us -> 2.48 us  [copies_over(): return lax.all_to_all(copies, axes, split_axis=0, concat_axis=0, tiled=True)]
  transfers between devices with their start and end apart: 8 -> 8, of which waited for: 4 -> 6; matrix products, arithmetic and copies ran while one was open for 4% -> 2% of each run, Pallas kernels for 7% -> 9%
where the time goes in v4:
time: 172 us; the launch traced here: 169 us
  blocking collectives  45 us (26%)
  waiting for transfers between devices  41.4 us (24%)
  starting transfers between devices  40.2 us (23%)
  Pallas kernels  21.4 us (12%)
  between operations  13.6 us (8%)
  local copies, waits for them, and re-layouts  6.13 us (4%)
    all_gather x1, blocking collectives, on_device(): got = lax.all_gather(packed, 'seq_0', axis=0, tiled=True)  33.6 us
    pallas_call x9, Pallas kernels, call(): pl.pallas_call(body, out_shape=outs, in_specs=specs or [vm] * len(operand...  21.4 us
    ppermute x1, starting transfers between devices, on_device(): other = lax.ppermute(own, 'seq_2', [(0, 1), (1, 0)])  12.5 us
    all_gather x1, blocking collectives, on_device(): merged = lax.all_gather(merged, 'head', axis=0, tiled=True)  11.4 us
    all_to_all x1, waiting for transfers between devices, on_device(): lax.all_to_all(sent.reshape(NZ, SENT, HD), 'seq_0', split_axis=0, concat_...  11.2 us
    all_to_all x1, waiting for transfers between devices, on_device(): lax.all_to_all(weights, 'seq_1', split_axis=0, concat_axis=0, tiled=True)  10 us
    all_to_all x1, waiting for transfers between devices, on_device(): lax.all_to_all(visual, ('seq_1', 'seq_2'), split_axis=0, concat_axis=0, t...  8.43 us
    all_to_all x1, waiting for transfers between devices, on_device(): lax.all_to_all(partial.reshape(NX, UNITS, VD), 'head', split_axis=0, conc...  6.13 us
  transfers between devices with their start and end apart: 8, of which 6 were waited for; matrix products, arithmetic and copies ran while one was open for 2% of the time, Pallas kernels for 9%

profile of v4, /device:TPU:1, one launch (start us, length us, event | category | flops | bytes accessed | tf_op | source)
XLA Modules:
  0.0 169.4 jit_solution(7096855514906082148)
XLA Ops:
  6.5 0.8 copy.14
  7.3 0.7 broadcast_in_dim.15
  8.0 5.0 %all-to-all-start = ((bf16[4,40,512]{2,1,0:T(8,128)(2,1)}), bf16[4,40,512]{2,1,0:T(8,128)(2,1)S(1)}, u32[]{:S(2)}, u32[]{:S(2)}) async-start(bf16[4,40,512]{2,1,0:T(8,128)(2,1)} %broadcast_in_dim.15), calls=%async_computation | async-start | bytes 327680 | tf_op jit(solution)/shard_map/all_to_all | solution.py:48
  13.0 0.0 all-gather.3.cloned.1.call-start
  13.0 0.8 reshape.43
  13.9 0.7 reshape.49
  14.6 0.1 pad.9.clone
  14.7 0.1 pad.2.clone
  14.7 0.8 fusion.1
  15.5 2.5 %all-to-all-done = bf16[4,40,512]{2,1,0:T(8,128)(2,1)S(1)} async-done(((bf16[4,40,512]{2,1,0:T(8,128)(2,1)}), bf16[4,40,512]{2,1,0:T(8,128)(2,1)S(1)}, u32[]{:S(2)}, u32[]{:S(2)}) %all-to-all-start) | async-done | bytes 163872 | tf_op jit(solution)/shard_map/all_to_all | solution.py:48
  18.0 0.8 maximum_maximum_fusion
  18.8 0.0 all-gather.3.cloned.1.call-update
  18.8 0.1 pad_add_fusion.place_ref
  18.9 0.0 copy-start.6
  18.9 33.6 %all_gather.12.got_ref = bf16[384,640]{1,0:T(8,128)(2,1)S(1)} all-gather(bf16[24,640]{1,0:T(8,128)(2,1)S(1)} %fusion.1), channel_id=1, replica_groups=mesh['seq_0'=16,'seq_1'=4,'seq_2'=2,'head'=4] {'seq_0'}, dimensions={0}, use_global_device_ids=true | all-gather | bytes 522240 | tf_op jit(solution)/shard_map/all_gather | solution.py:296
  52.5 1.6 shard_map.109
  54.1 3.6 %all-to-all-start.1 = ((bf16[4,160,1280]{2,1,0:T(8,128)(2,1)}), bf16[4,160,1280]{2,1,0:T(8,128)(2,1)S(1)}, u32[]{:S(2)}, u32[]{:S(2)}) async-start(bf16[4,160,1280]{2,1,0:T(8,128)(2,1)} %shard_map.109), calls=%async_computation.1 | async-start | bytes 3276800 | tf_op jit(solution)/shard_map/all_to_all | solution.py:306
  57.7 0.0 copy-done.6
  57.7 0.0 copy-done.1
  57.8 0.0 copy-done.2
  57.8 2.9 %shard_map.110 = (bf16[256,1280]{1,0:T(8,128)(2,1)S(1)}, bf16[256,128]{1,0:T(8,128)(2,1)S(1)}) custom-call(s32[4]{0:T(128)S(1)} %pad_add_fusion.place_ref, bf16[256,1280]{1,0:T(8,128)(2,1)S(1)} %copy-done.1, f32[1,1280]{1,0:T(1,128)S(1)} %reshape.46.gain_ref, s32[1,64]{1,0:T(1,128)S(1)} %copy-done.2), custom_call_target="tpu_custom_call" | custom-call | tf_op jit(solution)/shard_map/pallas_call | solution.py:53
  60.6 10.0 %all-to-all-done.1 = bf16[4,160,1280]{2,1,0:T(8,128)(2,1)S(1)} async-done(((bf16[4,160,1280]{2,1,0:T(8,128)(2,1)}), bf16[4,160,1280]{2,1,0:T(8,128)(2,1)S(1)}, u32[]{:S(2)}, u32[]{:S(2)}) %all-to-all-start.1) | async-done | bytes 1638432 | tf_op jit(solution)/shard_map/all_to_all | solution.py:306
  70.6 12.5 %collective-permute-start = (bf16[640,1280]{1,0:T(8,128)(2,1)S(1)}, bf16[640,1280]{1,0:T(8,128)(2,1)S(1)}, u32[]{:S(2)}, u32[]{:S(2)}) collective-permute-start(bf16[640,1280]{1,0:T(8,128)(2,1)S(1)} %bitcast.20), channel_id=1, source_target_pairs={{0,4},{4,0},{1,5},{5,1},{2,6},{6,2},{3,7},{7,3},{8,12},{12,8},{9,1... | collective-permute-start | bytes 4915208 | tf_op jit(solution)/shard_map/ppermute | solution.py:308
  83.1 3.1 %collective-permute-done.other_ref = bf16[640,1280]{1,0:T(8,128)(2,1)S(1)} collective-permute-done((bf16[640,1280]{1,0:T(8,128)(2,1)S(1)}, bf16[640,1280]{1,0:T(8,128)(2,1)S(1)}, u32[]{:S(2)}, u32[]{:S(2)}) %collective-permute-start) | collective-permute-done | bytes 1638432 | tf_op jit(solution)/shard_map/ppermute | solution.py:308
  86.2 4.8 %shard_map.111 = bf16[256,1280]{1,0:T(8,128)(2,1)} custom-call(s32[4]{0:T(128)S(1)} %pad_add_fusion.place_ref, bf16[256,1280]{1,0:T(8,128)(2,1)S(1)} %get-tuple-element.43.normed_ref, bf16[640,1280]{1,0:T(8,128)(2,1)S(1)} %bitcast.21, bf16[640,1280]{1,0:T(8,128)(2,1)S(1)} %collective-permute-done.other_ref, bf16[256,128]{1,0:T(8,128)(2,1)S(1)} %get-tuple-element.45.member_ref), custom_call_target="tpu_custom_call" | custom-call | tf_op jit(solution)/shard_map/pallas_call | solution.py:53
  91.1 3.9 %all-to-all-start.2 = ((bf16[4,64,1280]{2,1,0:T(8,128)(2,1)}), bf16[4,64,1280]{2,1,0:T(8,128)(2,1)S(1)}, u32[]{:S(2)}, u32[]{:S(2)}) async-start(bf16[4,64,1280]{2,1,0:T(8,128)(2,1)} %bitcast.7), calls=%async_computation.2 | async-start | bytes 1310720 | tf_op jit(solution)/shard_map/all_to_all | solution.py:320
  95.0 0.0 copy-done.7
  95.0 4.2 %shard_map.112 = (f32[64,1280]{1,0:T(8,128)S(1)}, f32[1,1280]{1,0:T(1,128)S(1)}, bf16[640,640]{1,0:T(8,128)(2,1)S(1)}) custom-call(s32[4]{0:T(128)S(1)} %pad_add_fusion.place_ref, bf16[256,1280]{1,0:T(8,128)(2,1)S(1)} %copy-done.1, f32[1,1280]{1,0:T(1,128)S(1)} %reshape.50.gain_ref), custom_call_target="tpu_custom_call" | custom-call | tf_op jit(solution)/shard_map/pallas_call | solution.py:53
  99.2 6.1 %all-to-all-done.2 = bf16[4,64,1280]{2,1,0:T(8,128)(2,1)S(1)} async-done(((bf16[4,64,1280]{2,1,0:T(8,128)(2,1)}), bf16[4,64,1280]{2,1,0:T(8,128)(2,1)S(1)}, u32[]{:S(2)}, u32[]{:S(2)}) %all-to-all-start.2) | async-done | bytes 655392 | tf_op jit(solution)/shard_map/all_to_all | solution.py:320
  105.3 3.4 %collective-permute-start.1 = (bf16[16,176,512]{2,1,0:T(8,128)(2,1)}, bf16[16,176,512]{2,1,0:T(8,128)(2,1)S(1)}, u32[]{:S(2)}, u32[]{:S(2)}) collective-permute-start(bf16[16,176,512]{2,1,0:T(8,128)(2,1)} %bitcast.22), channel_id=1, source_target_pairs={{0,4},{4,0},{1,5},{5,1},{2,6},{6,2},{3,7},{7,3},{8,12},{12,8},{9,1... | collective-permute-start | bytes 8650760 | tf_op jit(solution)/shard_map/ppermute | solution.py:324
  108.7 0.5 shard_map.113
  109.2 11.4 %all_gather.15.merged_ref = bf16[256,1280]{1,0:T(8,128)(2,1)S(1)} all-gather(bf16[64,1280]{1,0:T(8,128)(2,1)S(1)} %shard_map.113), channel_id=1, replica_groups=mesh['seq_0'=16,'seq_1'=4,'seq_2'=2,'head'=4] {'head'}, dimensions={0}, use_global_device_ids=true | all-gather | bytes 819200 | tf_op jit(solution)/shard_map/all_gather | solution.py:326
  120.6 0.0 collective-permute-done.1.other_ref
  120.6 1.8 %copy-done = bf16[2816,512]{1,0:T(8,128)(2,1)S(1)} copy-done((bf16[2816,512]{1,0:T(8,128)(2,1)S(1)}, bf16[2816,512]{1,0:T(8,128)(2,1)}, u32[]{:S(2)}) %copy-start) | copy-done | bytes 2883608
  122.5 1.9 %shard_map.114 = bf16[8,64,512]{2,1,0:T(8,128)(2,1)} custom-call(bf16[256,1280]{1,0:T(8,128)(2,1)S(1)} %all_gather.15.merged_ref, bf16[16,176,512]{2,1,0:T(8,128)(2,1)S(1)} %bitcast.24, bf16[16,176,512]{2,1,0:T(8,128)(2,1)S(1)} %collective-permute-done.1.other_ref), custom_call_target="tpu_custom_call" | custom-call | tf_op jit(solution)/shard_map/pallas_call | solution.py:53
  124.3 6.0 %all-to-all-start.3 = ((bf16[8,64,512]{2,1,0:T(8,128)(2,1)}), bf16[8,64,512]{2,1,0:T(8,128)(2,1)S(1)}, u32[]{:S(2)}, u32[]{:S(2)}) async-start(bf16[8,64,512]{2,1,0:T(8,128)(2,1)} %shard_map.114), calls=%async_computation.3 | async-start | bytes 1048576 | tf_op jit(solution)/shard_map/all_to_all | solution.py:329
  130.3 0.0 copy-done.8
  130.3 0.1 copy.13.range_ref
  130.5 0.9 slice_bitcast_fusion.asked_ref
  131.4 8.4 %all-to-all-done.3 = bf16[8,64,512]{2,1,0:T(8,128)(2,1)S(1)} async-done(((bf16[8,64,512]{2,1,0:T(8,128)(2,1)}), bf16[8,64,512]{2,1,0:T(8,128)(2,1)S(1)}, u32[]{:S(2)}, u32[]{:S(2)}) %all-to-all-start.3) | async-done | bytes 524320 | tf_op jit(solution)/shard_map/all_to_all | solution.py:329
  139.8 3.6 %shard_map.115 = bf16[640,128]{1,0:T(8,128)(2,1)} custom-call(s32[4]{0:T(128)S(1)} %pad_add_fusion.place_ref, bf16[512,512]{1,0:T(8,128)(2,1)S(1)} %bitcast.26, bf16[128,512]{1,0:T(8,128)(2,1)S(1)} %slice_bitcast_fusion.asked_ref, s32[256,2]{1,0:T(8,128)S(1)} %copy.13.range_ref), custom_call_target="tpu_custom_call" | custom-call | tf_op jit(solution)/shard_map/pallas_call | solution.py:53
  143.4 5.9 %all-to-all-start.4 = ((bf16[16,40,128]{2,1,0:T(8,128)(2,1)}), bf16[16,40,128]{2,1,0:T(8,128)(2,1)S(1)}, u32[]{:S(2)}, u32[]{:S(2)}) async-start(bf16[16,40,128]{2,1,0:T(8,128)(2,1)} %bitcast.12), calls=%async_computation.4 | async-start | bytes 327680 | tf_op jit(solution)/shard_map/all_to_all | solution.py:339
  149.2 0.0 copy-done.5
  149.3 0.0 copy-done.4
  149.3 0.0 copy-done.3
  149.3 0.9 shard_map.116
  150.2 11.2 %all-to-all-done.4 = bf16[16,40,128]{2,1,0:T(8,128)(2,1)S(1)} async-done(((bf16[16,40,128]{2,1,0:T(8,128)(2,1)}), bf16[16,40,128]{2,1,0:T(8,128)(2,1)S(1)}, u32[]{:S(2)}, u32[]{:S(2)}) %all-to-all-start.4) | async-done | bytes 163872 | tf_op jit(solution)/shard_map/all_to_all | solution.py:339
  161.4 1.1 shard_map.117
  (16 shorter events, 0.1 us)
Async XLA Ops:
  8.0 10.0 %all-to-all-start = ((bf16[4,40,512]{2,1,0:T(8,128)(2,1)}), bf16[4,40,512]{2,1,0:T(8,128)(2,1)S(1)}, u32[]{:S(2)}, u32[]{:S(2)}) async-start(bf16[4,40,512]{2,1,0:T(8,128)(2,1)} %broadcast_in_dim.15), calls=%async_computation | async-start | bytes 327680 | tf_op jit(solution)/shard_map/all_to_all | solution.py:48
  13.0 92.3 %all-gather.3.cloned.1.call-start = ((), (), s32[]{:S(2)}) async-start(), calls=%async_computation.5 | async-start | bytes 3063808 | tf_op jit(solution)/shard_map/all_gather | solution.py:295
  18.9 38.8 %copy-start.6 = (f32[1280]{0:T(1024)S(1)}, f32[1280]{0:T(1024)}, u32[]{:S(2)}) copy-start(f32[1280]{0:T(1024)} %param.12) | copy-start | bytes 15364
  18.9 38.9 %copy-start.1 = (bf16[256,1280]{1,0:T(8,128)(2,1)S(1)}, bf16[256,1280]{1,0:T(8,128)(2,1)}, u32[]{:S(2)}) copy-start(bf16[256,1280]{1,0:T(8,128)(2,1)} %patches_ref.1) | copy-start | bytes 1966084
  18.9 38.9 %copy-start.2 = (s32[1,64]{1,0:T(1,128)S(1)}, s32[1,64]{1,0:T(1,128)}, u32[]{:S(2)}) copy-start(s32[1,64]{1,0:T(1,128)} %window_ref) | copy-start | bytes 772
  54.1 16.5 %all-to-all-start.1 = ((bf16[4,160,1280]{2,1,0:T(8,128)(2,1)}), bf16[4,160,1280]{2,1,0:T(8,128)(2,1)S(1)}, u32[]{:S(2)}, u32[]{:S(2)}) async-start(bf16[4,160,1280]{2,1,0:T(8,128)(2,1)} %shard_map.109), calls=%async_computation.1 | async-start | bytes 3276800 | tf_op jit(solution)/shard_map/all_to_all | solution.py:306
  70.6 24.3 %copy-start.7 = (f32[1280]{0:T(1024)S(1)}, f32[1280]{0:T(1024)}, u32[]{:S(2)}) copy-start(f32[1280]{0:T(1024)} %param.16) | copy-start | bytes 15364
  70.6 15.6 %collective-permute-start = (bf16[640,1280]{1,0:T(8,128)(2,1)S(1)}, bf16[640,1280]{1,0:T(8,128)(2,1)S(1)}, u32[]{:S(2)}, u32[]{:S(2)}) collective-permute-start(bf16[640,1280]{1,0:T(8,128)(2,1)S(1)} %bitcast.20), channel_id=1, source_target_pairs={{0,4},{4,0},{1,5},{5,1},{2,6},{6,2},{3,7},{7,3},{8,12},{12,8},{9,1... | collective-permute-start | bytes 4915208 | tf_op jit(solution)/shard_map/ppermute | solution.py:308
  91.1 14.2 %all-to-all-start.2 = ((bf16[4,64,1280]{2,1,0:T(8,128)(2,1)}), bf16[4,64,1280]{2,1,0:T(8,128)(2,1)S(1)}, u32[]{:S(2)}, u32[]{:S(2)}) async-start(bf16[4,64,1280]{2,1,0:T(8,128)(2,1)} %bitcast.7), calls=%async_computation.2 | async-start | bytes 1310720 | tf_op jit(solution)/shard_map/all_to_all | solution.py:320
  105.3 15.4 %collective-permute-start.1 = (bf16[16,176,512]{2,1,0:T(8,128)(2,1)}, bf16[16,176,512]{2,1,0:T(8,128)(2,1)S(1)}, u32[]{:S(2)}, u32[]{:S(2)}) collective-permute-start(bf16[16,176,512]{2,1,0:T(8,128)(2,1)} %bitcast.22), channel_id=1, source_target_pairs={{0,4},{4,0},{1,5},{5,1},{2,6},{6,2},{3,7},{7,3},{8,12},{12,8},{9,1... | collective-permute-start | bytes 8650760 | tf_op jit(solution)/shard_map/ppermute | solution.py:324
  120.6 1.8 %copy-start = (bf16[2816,512]{1,0:T(8,128)(2,1)S(1)}, bf16[2816,512]{1,0:T(8,128)(2,1)}, u32[]{:S(2)}) copy-start(bf16[2816,512]{1,0:T(8,128)(2,1)} %all-gather.3.cloned.1.call-done) | copy-start | bytes 8650756
  122.5 7.9 %copy-start.8 = (s32[256,2]{0,1:T(2,128)S(1)}, s32[256,2]{0,1:T(2,128)}, u32[]{:S(2)}) copy-start(s32[256,2]{0,1:T(2,128)} %param.21) | copy-start | bytes 6148
  122.5 26.8 %copy-start.5 = (bf16[2,2048]{1,0:T(2,128)(2,1)S(1)}, bf16[2,2048]{1,0:T(2,128)(2,1)}, u32[]{:S(2)}) copy-start(bf16[2,2048]{1,0:T(2,128)(2,1)} %param.18) | copy-start | bytes 24580
  122.5 26.8 %copy-start.4 = (bf16[2,64,2,256]{3,2,1,0:T(2,128)(2,1)S(1)}, bf16[2,64,2,256]{3,2,1,0:T(2,128)(2,1)}, u32[]{:S(2)}) copy-start(bf16[2,64,2,256]{3,2,1,0:T(2,128)(2,1)} %param.19) | copy-start | bytes 393220
  124.3 25.0 %copy-start.3 = (s32[2]{0:T(128)S(1)}, s32[2]{0:T(128)}, u32[]{:S(2)}) copy-start(s32[2]{0:T(128)} %length_ref) | copy-start | bytes 28
  124.3 15.5 %all-to-all-start.3 = ((bf16[8,64,512]{2,1,0:T(8,128)(2,1)}), bf16[8,64,512]{2,1,0:T(8,128)(2,1)S(1)}, u32[]{:S(2)}, u32[]{:S(2)}) async-start(bf16[8,64,512]{2,1,0:T(8,128)(2,1)} %shard_map.114), calls=%async_computation.3 | async-start | bytes 1048576 | tf_op jit(solution)/shard_map/all_to_all | solution.py:329
  143.4 18.1 %all-to-all-start.4 = ((bf16[16,40,128]{2,1,0:T(8,128)(2,1)}), bf16[16,40,128]{2,1,0:T(8,128)(2,1)S(1)}, u32[]{:S(2)}, u32[]{:S(2)}) async-start(bf16[16,40,128]{2,1,0:T(8,128)(2,1)} %bitcast.12), calls=%async_computation.4 | async-start | bytes 327680 | tf_op jit(solution)/shard_map/all_to_all | solution.py:339
Sparse Core Ops, SparseCore 0:
  18.9 71.9 all-gather.2

commit v5 on v4

--- a/solution.py
+++ b/solution.py
@@ -15,7 +15,6 @@
 NZ, NY, NC, NX = 16, 4, 2, 4
 ROWS = VD // (NZ * NY * NC)
 PACKED = 24
-SENT = 40
 COLS = VD // NX
 HEAD = VD // VH
 HEADS = COLS // HEAD
@@ -43,11 +42,6 @@
     return jnp.where(condition, 1.0, 0.0).astype(bf16)
 
 
-def copies_over(value, axes, count):
-    copies = jnp.broadcast_to(value[None], (count, *value.shape))
-    return lax.all_to_all(copies, axes, split_axis=0, concat_axis=0, tiled=True)
-
-
 def call(body, outs, operands, specs=None, vmem=24 << 20):
     vm = pl.BlockSpec(memory_space=pltpu.VMEM)
     return pl.pallas_call(
@@ -63,16 +57,20 @@
 SMEM = pl.BlockSpec(memory_space=pltpu.SMEM)
 
 
+def near_kernel(weights_ref, out_ref):
+    for part in range(2):
+        rows = weights_ref[:, part, :]
+        for k in range(NY):
+            out_ref[k, :, part * 256 : (part + 1) * 256] = rows
+
+
 def places():
     at = iota((VD, 1), 0)
     return at // (NY * NC * ROWS), at // (NC * ROWS) % NY, at // ROWS % NC, at % ROWS
 
 
 def prepare_kernel(place_ref, patches_ref, gain_ref, window_ref, normed_ref, member_ref):
-    core = place_ref[2]
-    z, y, c, r = places()
-    target = ((c + core) % NC) * (VD // NC) + (y * NZ + z) * ROWS + r
-    order = one_hot(iota((VD, VD), 1) == target)
+    order = one_hot(iota((VD, VD), 1) == gathered(place_ref[2]))
     source = patches_ref[...].astype(f32)
     scale = lax.rsqrt(jnp.mean(source * source, axis=-1, keepdims=True) + 1e-06)
     normed = (source * scale * gain_ref[...]).astype(bf16)
@@ -82,14 +80,17 @@
     member_ref[...] = dot(member, one_hot(iota(shape, 0) // (WIN // 4) == iota(shape, 1))).astype(bf16)
 
 
-def residual_kernel(place_ref, patches_ref, gain_ref, source_ref, gains_ref, turn_ref):
+def gathered(core):
+    z, y, c, r = places()
+    return ((c + core) % NC) * (VD // NC) + (y * NZ + z) * ROWS + r
+
+
+def residual_kernel(place_ref, patches_ref, gain_ref, turn_ref, gains_ref):
     core = place_ref[2]
-    z, y, c, r = places()
-    target = ((y // 2 + core) % NC) * (VD // NC) + ((c * 2 + y % 2) * NZ + z) * ROWS + r
-    order = one_hot(iota((VD, VD), 1) == target)
+    order = one_hot(iota((VD, VD), 1) == gathered(core))
     shape = (UNITS, FPATCH)
     pick = one_hot(iota(shape, 1) == iota(shape, 0) * 4 + place_ref[3])
-    source_ref[...] = dot(dot(pick, patches_ref[...]).astype(bf16), order)
+    turn_ref[VD:] = dot(dot(pick, patches_ref[...]).astype(bf16), order).astype(bf16)
     gain = gain_ref[...]
     high = gain.astype(bf16).astype(f32)
     middle = (gain - high).astype(bf16).astype(f32)
@@ -97,19 +98,23 @@
     part = iota((8, 1), 0)
     parts = jnp.where(part == 0, high, jnp.where(part == 1, middle, jnp.where(part == 2, low, 0.0)))
     gains_ref[...] = jnp.sum(dot(parts.astype(bf16), order), axis=0, keepdims=True)
-    half = VD // 2
-    row = iota((half, 1), 0)
-    c, y, z, r = row // (2 * NZ * ROWS), row // (NZ * ROWS) % 2, row // ROWS % NZ, row % ROWS
-    turn_ref[...] = one_hot(iota((half, half), 1) == ((z * 2 + y) * NC + c) * ROWS + r)
+    row = iota((VD, 1), 0)
+    c, y, z, r = row // (VD // NC), row // (NZ * ROWS) % NY, row // ROWS % NZ, row % ROWS
+    target = ((y // 2 + core) % NC) * (VD // NC) + ((z * 2 + y % 2) * NC + (c + core) % NC) * ROWS + r
+    turn_ref[:VD] = one_hot(iota((VD, VD), 1) == target)
+
+
+def side_by_side(value):
+    return jnp.concatenate([value[:, b * HD : (b + 1) * HD] for b in range(4)], axis=0)
 
 
 def suffix_kernel(length_ref, asking_ref, suffix_ref, mixed_ref, level_ref):
-    asking = asking_ref[...]
+    asking = side_by_side(asking_ref[...])
     count = asking.shape[0]
     span = suffix_ref.shape[0] // 2
     row = iota((count, 1), 0)
-    even = (row // GROUP) % 2 == 0
-    second = row // (2 * GROUP)
+    even = row % 4 < 2
+    second = row // 4 % 2
     scores = jnp.where(even, dot_t(asking, suffix_ref[:, 0:128]), dot_t(asking, suffix_ref[:, 128:256]))
     col = iota((1, 2 * span), 1)
     length = jnp.where(second == 0, length_ref[0], length_ref[1])
@@ -134,7 +139,7 @@
             weights_ref[k, :, half * 640 : (half + 1) * 640] = weights
 
 
-def vision_kernel(place_ref, normed_ref, own_ref, other_ref, member_ref, out_ref):
+def vision_kernel(normed_ref, own_ref, other_ref, member_ref, out_ref):
     wide = 1024
     half = VD // 2
     projected = dot(normed_ref[:, :half], own_ref[:, :wide]) + dot(normed_ref[:, half:], other_ref[:, :wide])
@@ -158,28 +163,17 @@
     shape = (FPATCH, FPATCH)
     row, col = iota(shape, 0), iota(shape, 1)
     mixed = dot(one_hot(col == (row % UNITS) * 4 + row // UNITS), mixed).astype(bf16)
-
-    def project(core):
-        pair = (own_ref, other_ref) if core == 0 else (other_ref, own_ref)
-        for part in range(2):
-            rows = slice((part ^ core) * half // 2, ((part ^ core) + 1) * half // 2)
-            weights = jnp.concatenate([ref[rows, 896:1280] for ref in pair], axis=0)
-            out_ref[:, part * half : (part + 1) * half] = dot_t(mixed, weights).astype(bf16)
-
-    for core in range(NC):
-        pl.when(place_ref[2] == core)(lambda core=core: project(core))
-
-
-def merge_kernel(got_ref, source_ref, gain_ref, turn_ref, out_ref):
-    hidden = source_ref[...]
+    out_ref[:, :half] = dot_t(mixed, own_ref[:, 896:1280]).astype(bf16)
+    out_ref[:, half:] = dot_t(mixed, other_ref[:, 896:1280]).astype(bf16)
+
+
+def merge_kernel(got_ref, gain_ref, turn_ref, out_ref):
+    hidden = turn_ref[VD:].astype(f32)
     for k in range(NX):
         hidden += got_ref[k * UNITS : (k + 1) * UNITS].astype(f32)
     scale = lax.rsqrt(jnp.mean(hidden * hidden, axis=-1, keepdims=True) + 1e-06)
     merged = (hidden * scale * gain_ref[...]).astype(bf16)
-    half = VD // 2
-    for part in range(2):
-        at = slice(part * half, (part + 1) * half)
-        out_ref[:, at] = dot(merged[:, at], turn_ref[...]).astype(bf16)
+    out_ref[...] = dot(merged, turn_ref[:VD]).astype(bf16)
 
 
 def visual_kernel(merged_ref, own_ref, other_ref, out_ref):
@@ -200,8 +194,7 @@
     layer, inner = place_ref[0], place_ref[1]
     count = NZ * 4 * GROUP
     tokens = LAYER * UNITS
-    asked = asked_ref[...]
-    asking = jnp.concatenate([asked[:, b * HD : (b + 1) * HD] for b in range(4)], axis=0)
+    asking = side_by_side(asked_ref[...])
     row = iota((count, 1), 0)
     even = row % 4 < 2
     question = ((row // 8) % NZ * LAYER + inner) * 2 + (row // 4) % 2
@@ -223,47 +216,42 @@
     middle = (level - high).astype(bf16).astype(f32)
     low = level - high - middle
     lane = iota((1, HD), 1)
-    place = row // 4 % 2 * 16 + row % 4 * 4 + row // (NZ * 8)
+    block = row // (NZ * 8)
     levels = jnp.where(
-        lane == place,
-        high,
-        jnp.where(lane == place + 32, middle, jnp.where(lane == place + 64, low, 0.0)),
-    )
-    shape = (NZ * SENT, count)
-    row, col = iota((NZ * SENT, 1), 0), iota(shape, 1)
-    z, at = row // SENT, row % SENT
-    head = at % 16
-    source = jnp.where(at < 32, (head % 4) * (NZ * 8) + z * 8 + at // 16 * 4 + head // 4, -1)
-    order = one_hot(col == source)
-    layers = one_hot(iota((1, count), 1) // 8 % NZ == jnp.where(at == 32, z, -1))
-    out_ref[...] = (dot(order, mixed.astype(bf16)) + dot(layers, levels.astype(bf16))).astype(bf16)
+        lane == block, high, jnp.where(lane == block + 4, middle, jnp.where(lane == block + 8, low, 0.0))
+    )
+    blocks = [slice(b * NZ * 8, (b + 1) * NZ * 8) for b in range(4)]
+    for b in range(4):
+        out_ref[:, b * HD : (b + 1) * HD] = mixed[blocks[b]].astype(bf16)
+    out_ref[:, 4 * HD :] = sum(levels[at] for at in blocks).astype(bf16)
 
 
 def answer_kernel(got_ref, mixed_ref, level_ref, out_ref):
-    count = mixed_ref.shape[0]
-    highest, total = level_ref[:, 0:1], level_ref[:, 1:2]
     got = got_ref[...].astype(f32)
-    shape = (count, HD)
-    mine = iota(shape, 1) % count == iota(shape, 0)
-    levels = []
-    top = highest
-    for k in range(NZ):
-        row = got[k * SENT + count : k * SENT + count + 1]
-        level = jnp.sum(jnp.where(mine, row, 0.0), axis=-1, keepdims=True)
-        levels.append(level)
-        top = jnp.maximum(top, level)
-    share = jnp.exp(highest - top)
-    mixed = mixed_ref[...] * share
-    total = total * share
-    for k in range(NZ):
-        share = jnp.exp(levels[k] - top)
-        mixed += got[k * SENT : k * SENT + count] * share
-        total += share
-    mixed = mixed / total
-    heads = count // 2
-    for h in range(heads):
-        pair = jnp.concatenate([mixed[h : h + 1], mixed[heads + h : heads + h + 1]], axis=0)
-        out_ref[:, h * HD : (h + 1) * HD] = pair.astype(bf16)
+    count = 8
+    lane = iota((1, HD), 1)
+    answers = []
+    for b in range(4):
+        at = slice(b * count, (b + 1) * count)
+        highest, total = level_ref[at, 0:1], level_ref[at, 1:2]
+        mine = (lane < 12) & (lane % 4 == b)
+        level = jnp.sum(jnp.where(mine, got[:, 4 * HD :], 0.0), axis=-1, keepdims=True)
+        levels = [level[k * count : (k + 1) * count] for k in range(NZ)]
+        top = highest
+        for k in range(NZ):
+            top = jnp.maximum(top, levels[k])
+        share = jnp.exp(highest - top)
+        mixed = mixed_ref[at] * share
+        total = total * share
+        for k in range(NZ):
+            share = jnp.exp(levels[k] - top)
+            mixed += got[k * count : (k + 1) * count, b * HD : (b + 1) * HD] * share
+            total += share
+        answers.append(mixed / total)
+    answers = jnp.concatenate(answers, axis=1)
+    for a in range(4):
+        pair = jnp.concatenate([answers[a : a + 1], answers[4 + a : 5 + a]], axis=0)
+        out_ref[:, a * 512 : (a + 1) * 512] = pair.astype(bf16)
 
 
 def on_device(
@@ -285,7 +273,8 @@
     inner = lax.axis_index(("seq_1", "seq_2"))
     place = jnp.stack([layer, inner, lax.axis_index("seq_2"), lax.axis_index("head")])
 
-    near = copies_over(w_kv.reshape(-1, 512), "seq_1", NY).reshape(-1, 512)
+    near = call(near_kernel, sds((NY, 4 * ROWS, 512), bf16), (w_kv,))
+    near = lax.all_to_all(near, "seq_1", split_axis=0, concat_axis=0, tiled=True).reshape(-1, 512)
     packed = jnp.concatenate([w_qkv.reshape(ROWS, 3 * COLS), w_out.T], axis=1)
     packed = jnp.concatenate(
         [packed[:, :640], packed[:, 640:], jnp.zeros((PACKED - 2 * ROWS, 640), bf16)], axis=0
@@ -307,22 +296,22 @@
     own, normed, member = barrier((own, normed, member))
     other = lax.ppermute(own, "seq_2", [(0, 1), (1, 0)])
     partial = call(
-        vision_kernel, sds((FPATCH, VD), bf16), (place, normed, own, other, member), [SMEM] + [VMEM] * 4
+        vision_kernel, sds((FPATCH, VD), bf16), (normed, own, other, member)
     )
 
     partial, patches, place, merge_gain = barrier((partial, patches, place, merge_gain))
-    source, gains, turn = call(
+    turn, gains = call(
         residual_kernel,
-        (sds((UNITS, VD), f32), sds((1, VD), f32), sds((VD // 2, VD // 2), bf16)),
+        (sds((VD + UNITS, VD), bf16), sds((1, VD), f32)),
         (place, patches, merge_gain.reshape(1, VD)),
         [SMEM] + [VMEM] * 2,
     )
     partial = lax.all_to_all(
         partial.reshape(NX, UNITS, VD), "head", split_axis=0, concat_axis=0, tiled=True
     ).reshape(FPATCH, VD)
-    partial, far, source, gains, turn = barrier((partial, far, source, gains, turn))
+    partial, far, gains, turn = barrier((partial, far, gains, turn))
     far_other = lax.ppermute(far, "seq_2", [(0, 1), (1, 0)])
-    merged = call(merge_kernel, sds((UNITS, VD), bf16), (partial, source, gains, turn))
+    merged = call(merge_kernel, sds((UNITS, VD), bf16), (partial, gains, turn))
     merged = lax.all_gather(merged, "head", axis=0, tiled=True)
     visual = call(visual_kernel, sds((LAYER, UNITS, 512), bf16), (merged, far, far_other), vmem=24 << 20)
     asked = far[:, -16:-8].reshape(NZ * 8, 512)
@@ -331,18 +320,18 @@
     ).reshape(LAYER * UNITS, 512)
     sent = call(
         attend_kernel,
-        sds((NZ * SENT, HD), bf16),
+        sds((NZ * 8, 5 * HD), bf16),
         (place, visual, asked, frame_range),
         [SMEM] + [VMEM] * 3,
     )
     sent, queries, suffix_kv, question_lengths = barrier((sent, queries, suffix_kv, question_lengths))
     got = lax.all_to_all(
-        sent.reshape(NZ, SENT, HD), "seq_0", split_axis=0, concat_axis=0, tiled=True
-    ).reshape(-1, HD)
+        sent.reshape(NZ, 8, 5 * HD), "seq_0", split_axis=0, concat_axis=0, tiled=True
+    ).reshape(-1, 5 * HD)
     mixed, level = call(
         suffix_kernel,
         (sds((4 * GROUP, HD), f32), sds((4 * GROUP, HD), f32)),
-        (question_lengths, queries.reshape(4 * GROUP, HD), suffix_kv.reshape(-1, 512)),
+        (question_lengths, queries.reshape(8, 512), suffix_kv.reshape(-1, 512)),
         [SMEM] + [VMEM] * 2,
     )
     return call(answer_kernel, sds((2, 2 * GROUP * HD), bf16), (got, mixed, level))

time: 172 us -> 171 us (level)
  waiting for transfers between devices: 41.4 us -> 39.2 us
  Pallas kernels: 21.4 us -> 23.3 us
    all_to_all x1, waiting for transfers between devices: 6.13 us -> 3.94 us  [on_device(): lax.all_to_all(partial.reshape(NX, UNITS, VD), 'head', split_axis=0, conc...]
    pallas_call x9 -> x10, Pallas kernels: 21.4 us -> 23.3 us  [call(): pl.pallas_call(body, out_shape=outs, in_specs=specs or [vm] * len(operand...]
  transfers between devices with their start and end apart: 8 -> 8, of which waited for: 6 -> 6; matrix products, arithmetic and copies ran while one was open for 2% -> 2% of each run, Pallas kernels for 9% -> 10%
where the time goes in v5:
time: 171 us; the launch traced here: 168 us
  blocking collectives  45 us (26%)
  starting transfers between devices  40.7 us (24%)
  waiting for transfers between devices  39.2 us (23%)
  Pallas kernels  23.3 us (14%)
  between operations  13.6 us (8%)
  local copies, waits for them, and re-layouts  4.71 us (3%)
    all_gather x1, blocking collectives, on_device(): got = lax.all_gather(packed, 'seq_0', axis=0, tiled=True)  33.6 us
    pallas_call x10, Pallas kernels, call(): pl.pallas_call(body, out_shape=outs, in_specs=specs or [vm] * len(operand...  23.3 us
    ppermute x1, starting transfers between devices, on_device(): other = lax.ppermute(own, 'seq_2', [(0, 1), (1, 0)])  12.5 us
    all_gather x1, blocking collectives, on_device(): merged = lax.all_gather(merged, 'head', axis=0, tiled=True)  11.4 us
    all_to_all x1, waiting for transfers between devices, on_device(): lax.all_to_all(sent.reshape(NZ, 8, 5 * HD), 'seq_0', split_axis=0, concat...  11.2 us
    all_to_all x1, waiting for transfers between devices, on_device(): lax.all_to_all(weights, 'seq_1', split_axis=0, concat_axis=0, tiled=True)  10 us
    all_to_all x1, waiting for transfers between devices, on_device(): lax.all_to_all(visual, ('seq_1', 'seq_2'), split_axis=0, concat_axis=0, t...  8.43 us
    all_to_all x1, starting transfers between devices, on_device(): lax.all_to_all(visual, ('seq_1', 'seq_2'), split_axis=0, concat_axis=0, t...  5.96 us
  transfers between devices with their start and end apart: 8, of which 6 were waited for; matrix products, arithmetic and copies ran while one was open for 2% of the time, Pallas kernels for 10%

profile of v5, /device:TPU:1, one launch (start us, length us, event | category | flops | bytes accessed | tf_op | source)
XLA Modules:
  0.0 168.2 jit_solution(14295564407726683776)
XLA Ops:
  6.5 0.8 copy-done.3
  7.3 0.8 shard_map.109
  8.1 5.0 %all-to-all-start = ((bf16[4,40,512]{2,1,0:T(8,128)(2,1)}), bf16[4,40,512]{2,1,0:T(8,128)(2,1)S(1)}, u32[]{:S(2)}, u32[]{:S(2)}) async-start(bf16[4,40,512]{2,1,0:T(8,128)(2,1)} %shard_map.109), calls=%async_computation | async-start | bytes 327680 | tf_op jit(solution)/shard_map/all_to_all | solution.py:277
  13.1 0.0 all-gather.3.cloned.1.call-start
  13.1 0.8 reshape.42
  13.9 0.7 reshape.48
  14.7 0.1 pad.9.clone
  14.7 0.1 pad.2.clone
  14.8 0.8 fusion.1
  15.6 2.5 %all-to-all-done = bf16[4,40,512]{2,1,0:T(8,128)(2,1)S(1)} async-done(((bf16[4,40,512]{2,1,0:T(8,128)(2,1)}), bf16[4,40,512]{2,1,0:T(8,128)(2,1)S(1)}, u32[]{:S(2)}, u32[]{:S(2)}) %all-to-all-start) | async-done | bytes 163872 | tf_op jit(solution)/shard_map/all_to_all | solution.py:277
  18.1 0.8 maximum_maximum_fusion
  18.9 0.0 all-gather.3.cloned.1.call-update
  18.9 0.1 pad_add_fusion.place_ref
  19.0 33.6 %all_gather.12.got_ref = bf16[384,640]{1,0:T(8,128)(2,1)S(1)} all-gather(bf16[24,640]{1,0:T(8,128)(2,1)S(1)} %fusion.1), channel_id=1, replica_groups=mesh['seq_0'=16,'seq_1'=4,'seq_2'=2,'head'=4] {'seq_0'}, dimensions={0}, use_global_device_ids=true | all-gather | bytes 522240 | tf_op jit(solution)/shard_map/all_gather | solution.py:285
  52.6 1.6 shard_map.110
  54.2 3.6 %all-to-all-start.1 = ((bf16[4,160,1280]{2,1,0:T(8,128)(2,1)}), bf16[4,160,1280]{2,1,0:T(8,128)(2,1)S(1)}, u32[]{:S(2)}, u32[]{:S(2)}) async-start(bf16[4,160,1280]{2,1,0:T(8,128)(2,1)} %shard_map.110), calls=%async_computation.1 | async-start | bytes 3276800 | tf_op jit(solution)/shard_map/all_to_all | solution.py:295
  57.8 0.0 copy-done.8
  57.8 0.0 copy-done.1
  57.8 0.0 copy-done.4
  57.9 2.9 %shard_map.111 = (bf16[256,1280]{1,0:T(8,128)(2,1)S(1)}, bf16[256,128]{1,0:T(8,128)(2,1)S(1)}) custom-call(s32[4]{0:T(128)S(1)} %pad_add_fusion.place_ref, bf16[256,1280]{1,0:T(8,128)(2,1)S(1)} %copy-done.1, f32[1,1280]{1,0:T(1,128)S(1)} %reshape.45.gain_ref, s32[1,64]{1,0:T(1,128)S(1)} %copy-done.4), custom_call_target="tpu_custom_call" | custom-call | tf_op jit(solution)/shard_map/pallas_call | solution.py:47
  60.7 10.0 %all-to-all-done.1 = bf16[4,160,1280]{2,1,0:T(8,128)(2,1)S(1)} async-done(((bf16[4,160,1280]{2,1,0:T(8,128)(2,1)}), bf16[4,160,1280]{2,1,0:T(8,128)(2,1)S(1)}, u32[]{:S(2)}, u32[]{:S(2)}) %all-to-all-start.1) | async-done | bytes 1638432 | tf_op jit(solution)/shard_map/all_to_all | solution.py:295
  70.7 12.5 %collective-permute-start = (bf16[640,1280]{1,0:T(8,128)(2,1)S(1)}, bf16[640,1280]{1,0:T(8,128)(2,1)S(1)}, u32[]{:S(2)}, u32[]{:S(2)}) collective-permute-start(bf16[640,1280]{1,0:T(8,128)(2,1)S(1)} %bitcast.18), channel_id=1, source_target_pairs={{0,4},{4,0},{1,5},{5,1},{2,6},{6,2},{3,7},{7,3},{8,12},{12,8},{9,1... | collective-permute-start | bytes 4915208 | tf_op jit(solution)/shard_map/ppermute | solution.py:297
  83.2 3.1 %collective-permute-done.other_ref = bf16[640,1280]{1,0:T(8,128)(2,1)S(1)} collective-permute-done((bf16[640,1280]{1,0:T(8,128)(2,1)S(1)}, bf16[640,1280]{1,0:T(8,128)(2,1)S(1)}, u32[]{:S(2)}, u32[]{:S(2)}) %collective-permute-start) | collective-permute-done | bytes 1638432 | tf_op jit(solution)/shard_map/ppermute | solution.py:297
  86.3 4.1 %shard_map.112 = bf16[256,1280]{1,0:T(8,128)(2,1)} custom-call(bf16[256,1280]{1,0:T(8,128)(2,1)S(1)} %get-tuple-element.41.normed_ref, bf16[640,1280]{1,0:T(8,128)(2,1)S(1)} %bitcast.19, bf16[640,1280]{1,0:T(8,128)(2,1)S(1)} %collective-permute-done.other_ref, bf16[256,128]{1,0:T(8,128)(2,1)S(1)} %get-tuple-element.43.member_ref), custom_call_target="tpu_custom_call" | custom-call | tf_op jit(solution)/shard_map/pallas_call | solution.py:47
  90.4 4.2 %all-to-all-start.2 = ((bf16[4,64,1280]{2,1,0:T(8,128)(2,1)}), bf16[4,64,1280]{2,1,0:T(8,128)(2,1)}, u32[]{:S(2)}, u32[]{:S(2)}) async-start(bf16[4,64,1280]{2,1,0:T(8,128)(2,1)} %bitcast.7), calls=%async_computation.2 | async-start | bytes 1310720 | tf_op jit(solution)/shard_map/all_to_all | solution.py:309
  94.6 0.0 copy-done.9
  94.6 0.0 copy-start.2
  94.7 1.1 copy-done.2
  95.7 5.6 %shard_map.113 = (bf16[1344,1280]{1,0:T(8,128)(2,1)S(1)}, f32[1,1280]{1,0:T(1,128)S(1)}) custom-call(s32[4]{0:T(128)S(1)} %pad_add_fusion.place_ref, bf16[256,1280]{1,0:T(8,128)(2,1)S(1)} %copy-done.2, f32[1,1280]{1,0:T(1,128)S(1)} %reshape.49.gain_ref), custom_call_target="tpu_custom_call" | custom-call | tf_op jit(solution)/shard_map/pallas_call | solution.py:47
  101.3 3.9 %all-to-all-done.2 = bf16[4,64,1280]{2,1,0:T(8,128)(2,1)} async-done(((bf16[4,64,1280]{2,1,0:T(8,128)(2,1)}), bf16[4,64,1280]{2,1,0:T(8,128)(2,1)}, u32[]{:S(2)}, u32[]{:S(2)}) %all-to-all-start.2) | async-done | bytes 655392 | tf_op jit(solution)/shard_map/all_to_all | solution.py:309
  105.3 3.6 %collective-permute-start.1 = (bf16[16,176,512]{2,1,0:T(8,128)(2,1)}, bf16[16,176,512]{2,1,0:T(8,128)(2,1)S(1)}, u32[]{:S(2)}, u32[]{:S(2)}) collective-permute-start(bf16[16,176,512]{2,1,0:T(8,128)(2,1)} %bitcast.20), channel_id=1, source_target_pairs={{0,4},{4,0},{1,5},{5,1},{2,6},{6,2},{3,7},{7,3},{8,12},{12,8},{9,1... | collective-permute-start | bytes 8650760 | tf_op jit(solution)/shard_map/ppermute | solution.py:313
  108.9 1.9 %shard_map.114 = bf16[64,1280]{1,0:T(8,128)(2,1)S(1)} custom-call(bf16[256,1280]{1,0:T(8,128)(2,1)} %bitcast.8.got_ref, f32[1,1280]{1,0:T(1,128)S(1)} %get-tuple-element.52.gain_ref, bf16[1344,1280]{1,0:T(8,128)(2,1)S(1)} %get-tuple-element.53.turn_ref), custom_call_target="tpu_custom_call" | custom-call | tf_op jit(solution)/shard_map/pallas_call | solution.py:47
  110.8 11.4 %all_gather.15.merged_ref = bf16[256,1280]{1,0:T(8,128)(2,1)S(1)} all-gather(bf16[64,1280]{1,0:T(8,128)(2,1)S(1)} %shard_map.114), channel_id=1, replica_groups=mesh['seq_0'=16,'seq_1'=4,'seq_2'=2,'head'=4] {'head'}, dimensions={0}, use_global_device_ids=true | all-gather | bytes 819200 | tf_op jit(solution)/shard_map/all_gather | solution.py:315
  122.2 0.0 collective-permute-done.1.other_ref
  122.2 0.0 copy-done
  122.2 1.9 %shard_map.115 = bf16[8,64,512]{2,1,0:T(8,128)(2,1)} custom-call(bf16[256,1280]{1,0:T(8,128)(2,1)S(1)} %all_gather.15.merged_ref, bf16[16,176,512]{2,1,0:T(8,128)(2,1)S(1)} %bitcast.22, bf16[16,176,512]{2,1,0:T(8,128)(2,1)S(1)} %collective-permute-done.1.other_ref), custom_call_target="tpu_custom_call" | custom-call | tf_op jit(solution)/shard_map/pallas_call | solution.py:47
  124.1 6.0 %all-to-all-start.3 = ((bf16[8,64,512]{2,1,0:T(8,128)(2,1)}), bf16[8,64,512]{2,1,0:T(8,128)(2,1)S(1)}, u32[]{:S(2)}, u32[]{:S(2)}) async-start(bf16[8,64,512]{2,1,0:T(8,128)(2,1)} %shard_map.115), calls=%async_computation.3 | async-start | bytes 1048576 | tf_op jit(solution)/shard_map/all_to_all | solution.py:318
  130.1 0.0 copy-done.10
  130.1 0.1 copy.13.range_ref
  130.2 0.9 slice_bitcast_fusion.asked_ref
  131.1 8.4 %all-to-all-done.3 = bf16[8,64,512]{2,1,0:T(8,128)(2,1)S(1)} async-done(((bf16[8,64,512]{2,1,0:T(8,128)(2,1)}), bf16[8,64,512]{2,1,0:T(8,128)(2,1)S(1)}, u32[]{:S(2)}, u32[]{:S(2)}) %all-to-all-start.3) | async-done | bytes 524320 | tf_op jit(solution)/shard_map/all_to_all | solution.py:318
  139.6 2.6 %shard_map.116 = bf16[128,640]{1,0:T(8,128)(2,1)} custom-call(s32[4]{0:T(128)S(1)} %pad_add_fusion.place_ref, bf16[512,512]{1,0:T(8,128)(2,1)S(1)} %bitcast.23, bf16[128,512]{1,0:T(8,128)(2,1)S(1)} %slice_bitcast_fusion.asked_ref, s32[256,2]{1,0:T(8,128)S(1)} %copy.13.range_ref), custom_call_target="tpu_custom_call" | custom-call | tf_op jit(solution)/shard_map/pallas_call | solution.py:47
  142.1 5.9 %all-to-all-start.4 = ((bf16[16,8,640]{2,1,0:T(8,128)(2,1)}), bf16[16,8,640]{2,1,0:T(8,128)(2,1)S(1)}, u32[]{:S(2)}, u32[]{:S(2)}) async-start(bf16[16,8,640]{2,1,0:T(8,128)(2,1)} %bitcast.12), calls=%async_computation.4 | async-start | bytes 327680 | tf_op jit(solution)/shard_map/all_to_all | solution.py:328
  148.0 0.0 copy-done.7
  148.1 0.0 copy-done.5
  148.1 0.9 shard_map.117
  149.0 11.2 %all-to-all-done.4 = bf16[16,8,640]{2,1,0:T(8,128)(2,1)S(1)} async-done(((bf16[16,8,640]{2,1,0:T(8,128)(2,1)}), bf16[16,8,640]{2,1,0:T(8,128)(2,1)S(1)}, u32[]{:S(2)}, u32[]{:S(2)}) %all-to-all-start.4) | async-done | bytes 163872 | tf_op jit(solution)/shard_map/all_to_all | solution.py:328
  160.2 1.1 shard_map.118
  (19 shorter events, 0.1 us)
Async XLA Ops:
  6.5 0.8 copy-start.3
  8.1 10.0 %all-to-all-start = ((bf16[4,40,512]{2,1,0:T(8,128)(2,1)}), bf16[4,40,512]{2,1,0:T(8,128)(2,1)S(1)}, u32[]{:S(2)}, u32[]{:S(2)}) async-start(bf16[4,40,512]{2,1,0:T(8,128)(2,1)} %shard_map.109), calls=%async_computation | async-start | bytes 327680 | tf_op jit(solution)/shard_map/all_to_all | solution.py:277
  13.1 92.2 %all-gather.3.cloned.1.call-start = ((), (), s32[]{:S(2)}) async-start(), calls=%async_computation.5 | async-start | bytes 3063808 | tf_op jit(solution)/shard_map/all_gather | solution.py:284
  19.0 38.8 %copy-start.8 = (f32[1280]{0:T(1024)S(1)}, f32[1280]{0:T(1024)}, u32[]{:S(2)}) copy-start(f32[1280]{0:T(1024)} %param.12) | copy-start | bytes 15364
  19.0 38.9 %copy-start.1 = (bf16[256,1280]{1,0:T(8,128)(2,1)S(1)}, bf16[256,1280]{1,0:T(8,128)(2,1)}, u32[]{:S(2)}) copy-start(bf16[256,1280]{1,0:T(8,128)(2,1)} %patches_ref.1) | copy-start | bytes 1966084
  19.0 38.9 %copy-start.4 = (s32[1,64]{1,0:T(1,128)S(1)}, s32[1,64]{1,0:T(1,128)}, u32[]{:S(2)}) copy-start(s32[1,64]{1,0:T(1,128)} %window_ref) | copy-start | bytes 772
  54.2 16.5 %all-to-all-start.1 = ((bf16[4,160,1280]{2,1,0:T(8,128)(2,1)}), bf16[4,160,1280]{2,1,0:T(8,128)(2,1)S(1)}, u32[]{:S(2)}, u32[]{:S(2)}) async-start(bf16[4,160,1280]{2,1,0:T(8,128)(2,1)} %shard_map.110), calls=%async_computation.1 | async-start | bytes 3276800 | tf_op jit(solution)/shard_map/all_to_all | solution.py:295
  70.7 23.9 %copy-start.9 = (f32[1280]{0:T(1024)S(1)}, f32[1280]{0:T(1024)}, u32[]{:S(2)}) copy-start(f32[1280]{0:T(1024)} %param.16) | copy-start | bytes 15364
  70.7 15.6 %collective-permute-start = (bf16[640,1280]{1,0:T(8,128)(2,1)S(1)}, bf16[640,1280]{1,0:T(8,128)(2,1)S(1)}, u32[]{:S(2)}, u32[]{:S(2)}) collective-permute-start(bf16[640,1280]{1,0:T(8,128)(2,1)S(1)} %bitcast.18), channel_id=1, source_target_pairs={{0,4},{4,0},{1,5},{5,1},{2,6},{6,2},{3,7},{7,3},{8,12},{12,8},{9,1... | collective-permute-start | bytes 4915208 | tf_op jit(solution)/shard_map/ppermute | solution.py:297
  90.4 14.8 %all-to-all-start.2 = ((bf16[4,64,1280]{2,1,0:T(8,128)(2,1)}), bf16[4,64,1280]{2,1,0:T(8,128)(2,1)}, u32[]{:S(2)}, u32[]{:S(2)}) async-start(bf16[4,64,1280]{2,1,0:T(8,128)(2,1)} %bitcast.7), calls=%async_computation.2 | async-start | bytes 1310720 | tf_op jit(solution)/shard_map/all_to_all | solution.py:309
  94.6 1.1 copy-start.2
  105.3 16.9 %copy-start = (bf16[2816,512]{1,0:T(8,128)(2,1)S(1)}, bf16[2816,512]{1,0:T(8,128)(2,1)}, u32[]{:S(2)}) copy-start(bf16[2816,512]{1,0:T(8,128)(2,1)} %all-gather.3.cloned.1.call-done) | copy-start | bytes 8650756
  105.3 16.9 %collective-permute-start.1 = (bf16[16,176,512]{2,1,0:T(8,128)(2,1)}, bf16[16,176,512]{2,1,0:T(8,128)(2,1)S(1)}, u32[]{:S(2)}, u32[]{:S(2)}) collective-permute-start(bf16[16,176,512]{2,1,0:T(8,128)(2,1)} %bitcast.20), channel_id=1, source_target_pairs={{0,4},{4,0},{1,5},{5,1},{2,6},{6,2},{3,7},{7,3},{8,12},{12,8},{9,1... | collective-permute-start | bytes 8650760 | tf_op jit(solution)/shard_map/ppermute | solution.py:313
  122.2 7.9 %copy-start.10 = (s32[256,2]{0,1:T(2,128)S(1)}, s32[256,2]{0,1:T(2,128)}, u32[]{:S(2)}) copy-start(s32[256,2]{0,1:T(2,128)} %param.21) | copy-start | bytes 6148
  122.2 25.8 %copy-start.7 = (bf16[2,2048]{1,0:T(2,128)(2,1)S(1)}, bf16[2,2048]{1,0:T(2,128)(2,1)}, u32[]{:S(2)}) copy-start(bf16[2,2048]{1,0:T(2,128)(2,1)} %param.18) | copy-start | bytes 24580
  122.2 25.9 %copy-start.6 = (bf16[2,64,2,256]{3,2,1,0:T(2,128)(2,1)S(1)}, bf16[2,64,2,256]{3,2,1,0:T(2,128)(2,1)}, u32[]{:S(2)}) copy-start(bf16[2,64,2,256]{3,2,1,0:T(2,128)(2,1)} %param.19) | copy-start | bytes 393220
  124.1 24.0 %copy-start.5 = (s32[2]{0:T(128)S(1)}, s32[2]{0:T(128)}, u32[]{:S(2)}) copy-start(s32[2]{0:T(128)} %length_ref) | copy-start | bytes 28
  124.1 15.5 %all-to-all-start.3 = ((bf16[8,64,512]{2,1,0:T(8,128)(2,1)}), bf16[8,64,512]{2,1,0:T(8,128)(2,1)S(1)}, u32[]{:S(2)}, u32[]{:S(2)}) async-start(bf16[8,64,512]{2,1,0:T(8,128)(2,1)} %shard_map.115), calls=%async_computation.3 | async-start | bytes 1048576 | tf_op jit(solution)/shard_map/all_to_all | solution.py:318
  142.1 18.1 %all-to-all-start.4 = ((bf16[16,8,640]{2,1,0:T(8,128)(2,1)}), bf16[16,8,640]{2,1,0:T(8,128)(2,1)S(1)}, u32[]{:S(2)}, u32[]{:S(2)}) async-start(bf16[16,8,640]{2,1,0:T(8,128)(2,1)} %bitcast.12), calls=%async_computation.4 | async-start | bytes 327680 | tf_op jit(solution)/shard_map/all_to_all | solution.py:328
Sparse Core Ops, SparseCore 0:
  19.0 71.9 all-gather.2

commit v6 on v5

--- a/solution.py
+++ b/solution.py
@@ -57,13 +57,6 @@
 SMEM = pl.BlockSpec(memory_space=pltpu.SMEM)
 
 
-def near_kernel(weights_ref, out_ref):
-    for part in range(2):
-        rows = weights_ref[:, part, :]
-        for k in range(NY):
-            out_ref[k, :, part * 256 : (part + 1) * 256] = rows
-
-
 def places():
     at = iota((VD, 1), 0)
     return at // (NY * NC * ROWS), at // (NC * ROWS) % NY, at // ROWS % NC, at % ROWS
@@ -87,10 +80,15 @@
 
 def residual_kernel(place_ref, patches_ref, gain_ref, turn_ref, gains_ref):
     core = place_ref[2]
-    order = one_hot(iota((VD, VD), 1) == gathered(core))
+    half = VD // 2
+    z, y, c, r = places()
+    target = (y // 2) * half + (((c + core) % NC * 2 + y % 2) * NZ + z) * ROWS + r
+    order = one_hot(iota((VD, VD), 1) == target)
     shape = (UNITS, FPATCH)
     pick = one_hot(iota(shape, 1) == iota(shape, 0) * 4 + place_ref[3])
-    turn_ref[VD:] = dot(dot(pick, patches_ref[...]).astype(bf16), order).astype(bf16)
+    source = dot(dot(pick, patches_ref[...]).astype(bf16), order).astype(bf16)
+    turn_ref[half : half + UNITS] = source[:, :half]
+    turn_ref[half + UNITS :] = source[:, half:]
     gain = gain_ref[...]
     high = gain.astype(bf16).astype(f32)
     middle = (gain - high).astype(bf16).astype(f32)
@@ -98,10 +96,10 @@
     part = iota((8, 1), 0)
     parts = jnp.where(part == 0, high, jnp.where(part == 1, middle, jnp.where(part == 2, low, 0.0)))
     gains_ref[...] = jnp.sum(dot(parts.astype(bf16), order), axis=0, keepdims=True)
-    row = iota((VD, 1), 0)
-    c, y, z, r = row // (VD // NC), row // (NZ * ROWS) % NY, row // ROWS % NZ, row % ROWS
-    target = ((y // 2 + core) % NC) * (VD // NC) + ((z * 2 + y % 2) * NC + (c + core) % NC) * ROWS + r
-    turn_ref[:VD] = one_hot(iota((VD, VD), 1) == target)
+    row = iota((half, 1), 0)
+    c, y, z, r = row // (2 * NZ * ROWS), row // (NZ * ROWS) % 2, row // ROWS % NZ, row % ROWS
+    target = ((z * 2 + y) * NC + (c + core) % NC) * ROWS + r
+    turn_ref[:half] = one_hot(iota((half, half), 1) == target)
 
 
 def side_by_side(value):
@@ -140,9 +138,8 @@
 
 
 def vision_kernel(normed_ref, own_ref, other_ref, member_ref, out_ref):
-    wide = 1024
     half = VD // 2
-    projected = dot(normed_ref[:, :half], own_ref[:, :wide]) + dot(normed_ref[:, half:], other_ref[:, :wide])
+    projected = dot(normed_ref[:, :half], own_ref[:, :1024]) + dot(normed_ref[:, half:], other_ref[:, :1024])
     projected = projected.astype(bf16).astype(f32)
     query = pltpu.roll(projected[:, 0:384], 64, 1)
     key = projected[:, 256:640].astype(bf16)
@@ -163,17 +160,24 @@
     shape = (FPATCH, FPATCH)
     row, col = iota(shape, 0), iota(shape, 1)
     mixed = dot(one_hot(col == (row % UNITS) * 4 + row // UNITS), mixed).astype(bf16)
-    out_ref[:, :half] = dot_t(mixed, own_ref[:, 896:1280]).astype(bf16)
-    out_ref[:, half:] = dot_t(mixed, other_ref[:, 896:1280]).astype(bf16)
-
-
-def merge_kernel(got_ref, gain_ref, turn_ref, out_ref):
-    hidden = turn_ref[VD:].astype(f32)
+    for part in range(2):
+        rows = slice(part * half // 2, (part + 1) * half // 2)
+        weights = jnp.concatenate([own_ref[rows, 896:1280], other_ref[rows, 896:1280]], axis=0)
+        out_ref[:, part * half : (part + 1) * half] = dot_t(mixed, weights).astype(bf16)
+
+
+def merge_kernel(place_ref, got_ref, gain_ref, turn_ref, out_ref):
+    half = VD // 2
+    hidden = jnp.concatenate([turn_ref[half : half + UNITS], turn_ref[half + UNITS :]], axis=1).astype(f32)
     for k in range(NX):
         hidden += got_ref[k * UNITS : (k + 1) * UNITS].astype(f32)
     scale = lax.rsqrt(jnp.mean(hidden * hidden, axis=-1, keepdims=True) + 1e-06)
     merged = (hidden * scale * gain_ref[...]).astype(bf16)
-    out_ref[...] = dot(merged, turn_ref[:VD]).astype(bf16)
+    left = dot(merged[:, :half], turn_ref[:half])
+    right = dot(merged[:, half:], turn_ref[:half])
+    first = place_ref[2] == 0
+    out_ref[:, :half] = jnp.where(first, left, right).astype(bf16)
+    out_ref[:, half:] = jnp.where(first, right, left).astype(bf16)
 
 
 def visual_kernel(merged_ref, own_ref, other_ref, out_ref):
@@ -273,7 +277,7 @@
     inner = lax.axis_index(("seq_1", "seq_2"))
     place = jnp.stack([layer, inner, lax.axis_index("seq_2"), lax.axis_index("head")])
 
-    near = call(near_kernel, sds((NY, 4 * ROWS, 512), bf16), (w_kv,))
+    near = jnp.broadcast_to(w_kv[None], (NY, *w_kv.shape))
     near = lax.all_to_all(near, "seq_1", split_axis=0, concat_axis=0, tiled=True).reshape(-1, 512)
     packed = jnp.concatenate([w_qkv.reshape(ROWS, 3 * COLS), w_out.T], axis=1)
     packed = jnp.concatenate(
@@ -302,7 +306,7 @@
     partial, patches, place, merge_gain = barrier((partial, patches, place, merge_gain))
     turn, gains = call(
         residual_kernel,
-        (sds((VD + UNITS, VD), bf16), sds((1, VD), f32)),
+        (sds((VD // 2 + 2 * UNITS, VD // 2), bf16), sds((1, VD), f32)),
         (place, patches, merge_gain.reshape(1, VD)),
         [SMEM] + [VMEM] * 2,
     )
@@ -311,7 +315,7 @@
     ).reshape(FPATCH, VD)
     partial, far, gains, turn = barrier((partial, far, gains, turn))
     far_other = lax.ppermute(far, "seq_2", [(0, 1), (1, 0)])
-    merged = call(merge_kernel, sds((UNITS, VD), bf16), (partial, gains, turn))
+    merged = call(merge_kernel, sds((UNITS, VD), bf16), (place, partial, gains, turn), [SMEM] + [VMEM] * 3)
     merged = lax.all_gather(merged, "head", axis=0, tiled=True)
     visual = call(visual_kernel, sds((LAYER, UNITS, 512), bf16), (merged, far, far_other), vmem=24 << 20)
     asked = far[:, -16:-8].reshape(NZ * 8, 512)

time: 171 us -> 172 us (level)
  Pallas kernels: 23.3 us -> 20.4 us
  waiting for transfers between devices: 39.2 us -> 41.3 us
    pallas_call x10 -> x9, Pallas kernels: 23.3 us -> 20.4 us  [call(): pl.pallas_call(body, out_shape=outs, in_specs=specs or [vm] * len(operand...]
    all_to_all x1, waiting for transfers between devices: 3.94 us -> 5.99 us  [on_device(): lax.all_to_all(partial.reshape(NX, UNITS, VD), 'head', split_axis=0, conc...]
  transfers between devices with their start and end apart: 8 -> 8, of which waited for: 6 -> 6; matrix products, arithmetic and copies ran while one was open for 2% -> 2% of each run, Pallas kernels for 10% -> 9%
where the time goes in v6:
time: 172 us; the launch traced here: 168 us
  blocking collectives  45 us (26%)
  waiting for transfers between devices  41.3 us (24%)
  starting transfers between devices  40.2 us (23%)
  Pallas kernels  20.4 us (12%)
  between operations  13.6 us (8%)
  local copies, waits for them, and re-layouts  6.21 us (4%)
    all_gather x1, blocking collectives, on_device(): got = lax.all_gather(packed, 'seq_0', axis=0, tiled=True)  33.6 us
    pallas_call x9, Pallas kernels, call(): pl.pallas_call(body, out_shape=outs, in_specs=specs or [vm] * len(operand...  20.4 us
    ppermute x1, starting transfers between devices, on_device(): other = lax.ppermute(own, 'seq_2', [(0, 1), (1, 0)])  12.5 us
    all_gather x1, blocking collectives, on_device(): merged = lax.all_gather(merged, 'head', axis=0, tiled=True)  11.4 us
    all_to_all x1, waiting for transfers between devices, on_device(): lax.all_to_all(sent.reshape(NZ, 8, 5 * HD), 'seq_0', split_axis=0, concat...  11.2 us
    all_to_all x1, waiting for transfers between devices, on_device(): lax.all_to_all(weights, 'seq_1', split_axis=0, concat_axis=0, tiled=True)  10 us
    all_to_all x1, waiting for transfers between devices, on_device(): lax.all_to_all(visual, ('seq_1', 'seq_2'), split_axis=0, concat_axis=0, t...  8.43 us
    all_to_all x1, waiting for transfers between devices, on_device(): lax.all_to_all(partial.reshape(NX, UNITS, VD), 'head', split_axis=0, conc...  5.99 us
  transfers between devices with their start and end apart: 8, of which 6 were waited for; matrix products, arithmetic and copies ran while one was open for 2% of the time, Pallas kernels for 9%

profile of v6, /device:TPU:1, one launch (start us, length us, event | category | flops | bytes accessed | tf_op | source)
XLA Modules:
  0.0 168.4 jit_solution(2156182553343499439)
XLA Ops:
  6.5 1.5 broadcast_in_dim.13
  8.1 5.0 %all-to-all-start = ((bf16[4,40,2,256]{3,2,1,0:T(2,128)(2,1)}), bf16[4,40,2,256]{3,2,1,0:T(2,128)(2,1)S(1)}, u32[]{:S(2)}, u32[]{:S(2)}) async-start(bf16[4,40,2,256]{3,2,1,0:T(2,128)(2,1)} %broadcast_in_dim.13), calls=%async_computation | async-start | bytes 327680 | tf_op jit(solution)/shard_map/all_to_all | solution.py:281
  13.1 0.0 all-gather.3.cloned.1.call-start
  13.1 0.8 reshape.43
  13.9 0.7 reshape.49
  14.7 0.1 pad.9.clone
  14.7 0.1 pad.2.clone
  14.8 0.8 fusion.1
  15.6 2.5 %all-to-all-done = bf16[4,40,2,256]{3,2,1,0:T(2,128)(2,1)S(1)} async-done(((bf16[4,40,2,256]{3,2,1,0:T(2,128)(2,1)}), bf16[4,40,2,256]{3,2,1,0:T(2,128)(2,1)S(1)}, u32[]{:S(2)}, u32[]{:S(2)}) %all-to-all-start) | async-done | bytes 163872 | tf_op jit(solution)/shard_map/all_to_all | solution.py:281
  18.1 0.8 maximum_maximum_fusion
  18.9 0.0 all-gather.3.cloned.1.call-update
  18.9 0.1 pad_add_fusion.place_ref
  19.0 0.0 copy-start.6
  19.0 0.0 copy-start.1
  19.0 33.6 %all_gather.12.got_ref = bf16[384,640]{1,0:T(8,128)(2,1)S(1)} all-gather(bf16[24,640]{1,0:T(8,128)(2,1)S(1)} %fusion.1), channel_id=1, replica_groups=mesh['seq_0'=16,'seq_1'=4,'seq_2'=2,'head'=4] {'seq_0'}, dimensions={0}, use_global_device_ids=true | all-gather | bytes 522240 | tf_op jit(solution)/shard_map/all_gather | solution.py:289
  52.6 1.6 shard_map.109
  54.2 3.6 %all-to-all-start.1 = ((bf16[4,160,1280]{2,1,0:T(8,128)(2,1)}), bf16[4,160,1280]{2,1,0:T(8,128)(2,1)S(1)}, u32[]{:S(2)}, u32[]{:S(2)}) async-start(bf16[4,160,1280]{2,1,0:T(8,128)(2,1)} %shard_map.109), calls=%async_computation.1 | async-start | bytes 3276800 | tf_op jit(solution)/shard_map/all_to_all | solution.py:299
  57.8 0.0 copy-done.6
  57.8 0.0 copy-done.1
  57.8 0.0 copy-done.2
  57.8 2.9 %shard_map.110 = (bf16[256,1280]{1,0:T(8,128)(2,1)S(1)}, bf16[256,128]{1,0:T(8,128)(2,1)S(1)}) custom-call(s32[4]{0:T(128)S(1)} %pad_add_fusion.place_ref, bf16[256,1280]{1,0:T(8,128)(2,1)S(1)} %copy-done.1, f32[1,1280]{1,0:T(1,128)S(1)} %reshape.46.gain_ref, s32[1,64]{1,0:T(1,128)S(1)} %copy-done.2), custom_call_target="tpu_custom_call" | custom-call | tf_op jit(solution)/shard_map/pallas_call | solution.py:47
  60.7 10.0 %all-to-all-done.1 = bf16[4,160,1280]{2,1,0:T(8,128)(2,1)S(1)} async-done(((bf16[4,160,1280]{2,1,0:T(8,128)(2,1)}), bf16[4,160,1280]{2,1,0:T(8,128)(2,1)S(1)}, u32[]{:S(2)}, u32[]{:S(2)}) %all-to-all-start.1) | async-done | bytes 1638432 | tf_op jit(solution)/shard_map/all_to_all | solution.py:299
  70.7 12.5 %collective-permute-start = (bf16[640,1280]{1,0:T(8,128)(2,1)S(1)}, bf16[640,1280]{1,0:T(8,128)(2,1)S(1)}, u32[]{:S(2)}, u32[]{:S(2)}) collective-permute-start(bf16[640,1280]{1,0:T(8,128)(2,1)S(1)} %bitcast.20), channel_id=1, source_target_pairs={{0,4},{4,0},{1,5},{5,1},{2,6},{6,2},{3,7},{7,3},{8,12},{12,8},{9,1... | collective-permute-start | bytes 4915208 | tf_op jit(solution)/shard_map/ppermute | solution.py:301
  83.2 3.1 %collective-permute-done.other_ref = bf16[640,1280]{1,0:T(8,128)(2,1)S(1)} collective-permute-done((bf16[640,1280]{1,0:T(8,128)(2,1)S(1)}, bf16[640,1280]{1,0:T(8,128)(2,1)S(1)}, u32[]{:S(2)}, u32[]{:S(2)}) %collective-permute-start) | collective-permute-done | bytes 1638432 | tf_op jit(solution)/shard_map/ppermute | solution.py:301
  86.3 4.1 %shard_map.111 = bf16[256,1280]{1,0:T(8,128)(2,1)} custom-call(bf16[256,1280]{1,0:T(8,128)(2,1)S(1)} %get-tuple-element.41.normed_ref, bf16[640,1280]{1,0:T(8,128)(2,1)S(1)} %bitcast.21, bf16[640,1280]{1,0:T(8,128)(2,1)S(1)} %collective-permute-done.other_ref, bf16[256,128]{1,0:T(8,128)(2,1)S(1)} %get-tuple-element.43.member_ref), custom_call_target="tpu_custom_call" | custom-call | tf_op jit(solution)/shard_map/pallas_call | solution.py:47
  90.5 3.9 %all-to-all-start.2 = ((bf16[4,64,1280]{2,1,0:T(8,128)(2,1)}), bf16[4,64,1280]{2,1,0:T(8,128)(2,1)S(1)}, u32[]{:S(2)}, u32[]{:S(2)}) async-start(bf16[4,64,1280]{2,1,0:T(8,128)(2,1)} %bitcast.6), calls=%async_computation.2 | async-start | bytes 1310720 | tf_op jit(solution)/shard_map/all_to_all | solution.py:313
  94.3 0.0 copy-done.7
  94.4 4.3 %shard_map.112 = (bf16[768,640]{1,0:T(8,128)(2,1)S(1)}, f32[1,1280]{1,0:T(1,128)S(1)}) custom-call(s32[4]{0:T(128)S(1)} %pad_add_fusion.place_ref, bf16[256,1280]{1,0:T(8,128)(2,1)S(1)} %copy-done.1, f32[1,1280]{1,0:T(1,128)S(1)} %reshape.50.gain_ref), custom_call_target="tpu_custom_call" | custom-call | tf_op jit(solution)/shard_map/pallas_call | solution.py:47
  98.7 6.0 %all-to-all-done.2 = bf16[4,64,1280]{2,1,0:T(8,128)(2,1)S(1)} async-done(((bf16[4,64,1280]{2,1,0:T(8,128)(2,1)}), bf16[4,64,1280]{2,1,0:T(8,128)(2,1)S(1)}, u32[]{:S(2)}, u32[]{:S(2)}) %all-to-all-start.2) | async-done | bytes 655392 | tf_op jit(solution)/shard_map/all_to_all | solution.py:313
  104.7 3.4 %collective-permute-start.1 = (bf16[16,176,512]{2,1,0:T(8,128)(2,1)}, bf16[16,176,512]{2,1,0:T(8,128)(2,1)S(1)}, u32[]{:S(2)}, u32[]{:S(2)}) collective-permute-start(bf16[16,176,512]{2,1,0:T(8,128)(2,1)} %bitcast.22), channel_id=1, source_target_pairs={{0,4},{4,0},{1,5},{5,1},{2,6},{6,2},{3,7},{7,3},{8,12},{12,8},{9,1... | collective-permute-start | bytes 8650760 | tf_op jit(solution)/shard_map/ppermute | solution.py:317
  108.1 1.1 shard_map.113
  109.2 11.4 %all_gather.15.merged_ref = bf16[256,1280]{1,0:T(8,128)(2,1)S(1)} all-gather(bf16[64,1280]{1,0:T(8,128)(2,1)S(1)} %shard_map.113), channel_id=1, replica_groups=mesh['seq_0'=16,'seq_1'=4,'seq_2'=2,'head'=4] {'head'}, dimensions={0}, use_global_device_ids=true | all-gather | bytes 819200 | tf_op jit(solution)/shard_map/all_gather | solution.py:319
  120.6 0.0 collective-permute-done.1.other_ref
  120.6 1.8 %copy-done = bf16[2816,512]{1,0:T(8,128)(2,1)S(1)} copy-done((bf16[2816,512]{1,0:T(8,128)(2,1)S(1)}, bf16[2816,512]{1,0:T(8,128)(2,1)}, u32[]{:S(2)}) %copy-start) | copy-done | bytes 2883608
  122.4 1.9 %shard_map.114 = bf16[8,64,512]{2,1,0:T(8,128)(2,1)} custom-call(bf16[256,1280]{1,0:T(8,128)(2,1)S(1)} %all_gather.15.merged_ref, bf16[16,176,512]{2,1,0:T(8,128)(2,1)S(1)} %bitcast.24, bf16[16,176,512]{2,1,0:T(8,128)(2,1)S(1)} %collective-permute-done.1.other_ref), custom_call_target="tpu_custom_call" | custom-call | tf_op jit(solution)/shard_map/pallas_call | solution.py:47
  124.3 6.0 %all-to-all-start.3 = ((bf16[8,64,512]{2,1,0:T(8,128)(2,1)}), bf16[8,64,512]{2,1,0:T(8,128)(2,1)S(1)}, u32[]{:S(2)}, u32[]{:S(2)}) async-start(bf16[8,64,512]{2,1,0:T(8,128)(2,1)} %shard_map.114), calls=%async_computation.3 | async-start | bytes 1048576 | tf_op jit(solution)/shard_map/all_to_all | solution.py:322
  130.2 0.0 copy-done.8
  130.2 0.1 copy.13.range_ref
  130.4 0.9 slice_bitcast_fusion.asked_ref
  131.3 8.4 %all-to-all-done.3 = bf16[8,64,512]{2,1,0:T(8,128)(2,1)S(1)} async-done(((bf16[8,64,512]{2,1,0:T(8,128)(2,1)}), bf16[8,64,512]{2,1,0:T(8,128)(2,1)S(1)}, u32[]{:S(2)}, u32[]{:S(2)}) %all-to-all-start.3) | async-done | bytes 524320 | tf_op jit(solution)/shard_map/all_to_all | solution.py:322
  139.7 2.6 %shard_map.115 = bf16[128,640]{1,0:T(8,128)(2,1)} custom-call(s32[4]{0:T(128)S(1)} %pad_add_fusion.place_ref, bf16[512,512]{1,0:T(8,128)(2,1)S(1)} %bitcast.26, bf16[128,512]{1,0:T(8,128)(2,1)S(1)} %slice_bitcast_fusion.asked_ref, s32[256,2]{1,0:T(8,128)S(1)} %copy.13.range_ref), custom_call_target="tpu_custom_call" | custom-call | tf_op jit(solution)/shard_map/pallas_call | solution.py:47
  142.3 5.9 %all-to-all-start.4 = ((bf16[16,8,640]{2,1,0:T(8,128)(2,1)}), bf16[16,8,640]{2,1,0:T(8,128)(2,1)S(1)}, u32[]{:S(2)}, u32[]{:S(2)}) async-start(bf16[16,8,640]{2,1,0:T(8,128)(2,1)} %bitcast.11), calls=%async_computation.4 | async-start | bytes 327680 | tf_op jit(solution)/shard_map/all_to_all | solution.py:332
  148.2 0.0 copy-done.5
  148.3 0.0 copy-done.4
  148.3 0.0 copy-done.3
  148.3 0.9 shard_map.116
  149.2 11.2 %all-to-all-done.4 = bf16[16,8,640]{2,1,0:T(8,128)(2,1)S(1)} async-done(((bf16[16,8,640]{2,1,0:T(8,128)(2,1)}), bf16[16,8,640]{2,1,0:T(8,128)(2,1)S(1)}, u32[]{:S(2)}, u32[]{:S(2)}) %all-to-all-start.4) | async-done | bytes 163872 | tf_op jit(solution)/shard_map/all_to_all | solution.py:332
  160.4 1.1 shard_map.117
  (16 shorter events, 0.1 us)
Async XLA Ops:
  8.1 10.0 %all-to-all-start = ((bf16[4,40,2,256]{3,2,1,0:T(2,128)(2,1)}), bf16[4,40,2,256]{3,2,1,0:T(2,128)(2,1)S(1)}, u32[]{:S(2)}, u32[]{:S(2)}) async-start(bf16[4,40,2,256]{3,2,1,0:T(2,128)(2,1)} %broadcast_in_dim.13), calls=%async_computation | async-start | bytes 327680 | tf_op jit(solution)/shard_map/all_to_all | solution.py:281
  13.1 91.6 %all-gather.3.cloned.1.call-start = ((), (), s32[]{:S(2)}) async-start(), calls=%async_computation.5 | async-start | bytes 3063808 | tf_op jit(solution)/shard_map/all_gather | solution.py:288
  19.0 38.8 %copy-start.6 = (f32[1280]{0:T(1024)S(1)}, f32[1280]{0:T(1024)}, u32[]{:S(2)}) copy-start(f32[1280]{0:T(1024)} %param.12) | copy-start | bytes 15364
  19.0 38.8 %copy-start.1 = (bf16[256,1280]{1,0:T(8,128)(2,1)S(1)}, bf16[256,1280]{1,0:T(8,128)(2,1)}, u32[]{:S(2)}) copy-start(bf16[256,1280]{1,0:T(8,128)(2,1)} %patches_ref.1) | copy-start | bytes 1966084
  19.0 38.9 %copy-start.2 = (s32[1,64]{1,0:T(1,128)S(1)}, s32[1,64]{1,0:T(1,128)}, u32[]{:S(2)}) copy-start(s32[1,64]{1,0:T(1,128)} %window_ref) | copy-start | bytes 772
  54.2 16.5 %all-to-all-start.1 = ((bf16[4,160,1280]{2,1,0:T(8,128)(2,1)}), bf16[4,160,1280]{2,1,0:T(8,128)(2,1)S(1)}, u32[]{:S(2)}, u32[]{:S(2)}) async-start(bf16[4,160,1280]{2,1,0:T(8,128)(2,1)} %shard_map.109), calls=%async_computation.1 | async-start | bytes 3276800 | tf_op jit(solution)/shard_map/all_to_all | solution.py:299
  70.7 23.6 %copy-start.7 = (f32[1280]{0:T(1024)S(1)}, f32[1280]{0:T(1024)}, u32[]{:S(2)}) copy-start(f32[1280]{0:T(1024)} %param.16) | copy-start | bytes 15364
  70.7 15.6 %collective-permute-start = (bf16[640,1280]{1,0:T(8,128)(2,1)S(1)}, bf16[640,1280]{1,0:T(8,128)(2,1)S(1)}, u32[]{:S(2)}, u32[]{:S(2)}) collective-permute-start(bf16[640,1280]{1,0:T(8,128)(2,1)S(1)} %bitcast.20), channel_id=1, source_target_pairs={{0,4},{4,0},{1,5},{5,1},{2,6},{6,2},{3,7},{7,3},{8,12},{12,8},{9,1... | collective-permute-start | bytes 4915208 | tf_op jit(solution)/shard_map/ppermute | solution.py:301
  90.5 14.2 %all-to-all-start.2 = ((bf16[4,64,1280]{2,1,0:T(8,128)(2,1)}), bf16[4,64,1280]{2,1,0:T(8,128)(2,1)S(1)}, u32[]{:S(2)}, u32[]{:S(2)}) async-start(bf16[4,64,1280]{2,1,0:T(8,128)(2,1)} %bitcast.6), calls=%async_computation.2 | async-start | bytes 1310720 | tf_op jit(solution)/shard_map/all_to_all | solution.py:313
  104.7 15.9 %collective-permute-start.1 = (bf16[16,176,512]{2,1,0:T(8,128)(2,1)}, bf16[16,176,512]{2,1,0:T(8,128)(2,1)S(1)}, u32[]{:S(2)}, u32[]{:S(2)}) collective-permute-start(bf16[16,176,512]{2,1,0:T(8,128)(2,1)} %bitcast.22), channel_id=1, source_target_pairs={{0,4},{4,0},{1,5},{5,1},{2,6},{6,2},{3,7},{7,3},{8,12},{12,8},{9,1... | collective-permute-start | bytes 8650760 | tf_op jit(solution)/shard_map/ppermute | solution.py:317
  120.6 1.8 %copy-start = (bf16[2816,512]{1,0:T(8,128)(2,1)S(1)}, bf16[2816,512]{1,0:T(8,128)(2,1)}, u32[]{:S(2)}) copy-start(bf16[2816,512]{1,0:T(8,128)(2,1)} %all-gather.3.cloned.1.call-done) | copy-start | bytes 8650756
  122.4 7.8 %copy-start.8 = (s32[256,2]{0,1:T(2,128)S(1)}, s32[256,2]{0,1:T(2,128)}, u32[]{:S(2)}) copy-start(s32[256,2]{0,1:T(2,128)} %param.21) | copy-start | bytes 6148
  122.4 25.8 %copy-start.5 = (bf16[2,2048]{1,0:T(2,128)(2,1)S(1)}, bf16[2,2048]{1,0:T(2,128)(2,1)}, u32[]{:S(2)}) copy-start(bf16[2,2048]{1,0:T(2,128)(2,1)} %param.18) | copy-start | bytes 24580
  122.4 25.9 %copy-start.4 = (bf16[2,64,2,256]{3,2,1,0:T(2,128)(2,1)S(1)}, bf16[2,64,2,256]{3,2,1,0:T(2,128)(2,1)}, u32[]{:S(2)}) copy-start(bf16[2,64,2,256]{3,2,1,0:T(2,128)(2,1)} %param.19) | copy-start | bytes 393220
  124.3 24.0 %copy-start.3 = (s32[2]{0:T(128)S(1)}, s32[2]{0:T(128)}, u32[]{:S(2)}) copy-start(s32[2]{0:T(128)} %length_ref) | copy-start | bytes 28
  124.3 15.5 %all-to-all-start.3 = ((bf16[8,64,512]{2,1,0:T(8,128)(2,1)}), bf16[8,64,512]{2,1,0:T(8,128)(2,1)S(1)}, u32[]{:S(2)}, u32[]{:S(2)}) async-start(bf16[8,64,512]{2,1,0:T(8,128)(2,1)} %shard_map.114), calls=%async_computation.3 | async-start | bytes 1048576 | tf_op jit(solution)/shard_map/all_to_all | solution.py:322
  142.3 18.1 %all-to-all-start.4 = ((bf16[16,8,640]{2,1,0:T(8,128)(2,1)}), bf16[16,8,640]{2,1,0:T(8,128)(2,1)S(1)}, u32[]{:S(2)}, u32[]{:S(2)}) async-start(bf16[16,8,640]{2,1,0:T(8,128)(2,1)} %bitcast.11), calls=%async_computation.4 | async-start | bytes 327680 | tf_op jit(solution)/shard_map/all_to_all | solution.py:332
Sparse Core Ops, SparseCore 0:
  19.0 71.9 all-gather.2

commit v7 on v6

--- a/solution.py
+++ b/solution.py
@@ -22,6 +22,7 @@
 GROUP = 8
 LAYER = NY * NC
 NEGATIVE = -1e30
+TURNS = (("seq_0", "seq_2"), [[z * NC + (z + group) % NC for z in range(NZ)] for group in range(NC)])
 f32 = jnp.float32
 bf16 = jnp.bfloat16
 
@@ -63,7 +64,7 @@
 
 
 def prepare_kernel(place_ref, patches_ref, gain_ref, window_ref, normed_ref, member_ref):
-    order = one_hot(iota((VD, VD), 1) == gathered(place_ref[2]))
+    order = one_hot(iota((VD, VD), 1) == gathered(place_ref[2] + place_ref[0]))
     source = patches_ref[...].astype(f32)
     scale = lax.rsqrt(jnp.mean(source * source, axis=-1, keepdims=True) + 1e-06)
     normed = (source * scale * gain_ref[...]).astype(bf16)
@@ -73,16 +74,16 @@
     member_ref[...] = dot(member, one_hot(iota(shape, 0) // (WIN // 4) == iota(shape, 1))).astype(bf16)
 
 
-def gathered(core):
+def gathered(group):
     z, y, c, r = places()
-    return ((c + core) % NC) * (VD // NC) + (y * NZ + z) * ROWS + r
+    return ((c + z + group) % NC) * (VD // NC) + (y * NZ + z) * ROWS + r
 
 
 def residual_kernel(place_ref, patches_ref, gain_ref, turn_ref, gains_ref):
-    core = place_ref[2]
+    group = place_ref[2] + place_ref[0]
     half = VD // 2
     z, y, c, r = places()
-    target = (y // 2) * half + (((c + core) % NC * 2 + y % 2) * NZ + z) * ROWS + r
+    target = (y // 2) * half + (((c + z + group) % NC * 2 + y % 2) * NZ + z) * ROWS + r
     order = one_hot(iota((VD, VD), 1) == target)
     shape = (UNITS, FPATCH)
     pick = one_hot(iota(shape, 1) == iota(shape, 0) * 4 + place_ref[3])
@@ -98,7 +99,7 @@
     gains_ref[...] = jnp.sum(dot(parts.astype(bf16), order), axis=0, keepdims=True)
     row = iota((half, 1), 0)
     c, y, z, r = row // (2 * NZ * ROWS), row // (NZ * ROWS) % 2, row // ROWS % NZ, row % ROWS
-    target = ((z * 2 + y) * NC + (c + core) % NC) * ROWS + r
+    target = ((z * 2 + y) * NC + (c + z + group) % NC) * ROWS + r
     turn_ref[:half] = one_hot(iota((half, half), 1) == target)
 
 
@@ -175,7 +176,7 @@
     merged = (hidden * scale * gain_ref[...]).astype(bf16)
     left = dot(merged[:, :half], turn_ref[:half])
     right = dot(merged[:, half:], turn_ref[:half])
-    first = place_ref[2] == 0
+    first = (iota((1, half), 1) // (4 * NY * ROWS) + place_ref[2] + place_ref[0]) % NC == 0
     out_ref[:, :half] = jnp.where(first, left, right).astype(bf16)
     out_ref[:, half:] = jnp.where(first, right, left).astype(bf16)
 
@@ -196,12 +197,14 @@
 
 def attend_kernel(place_ref, visual_ref, asked_ref, range_ref, out_ref):
     layer, inner = place_ref[0], place_ref[1]
+    group = place_ref[2] + layer
     count = NZ * 4 * GROUP
     tokens = LAYER * UNITS
     asking = side_by_side(asked_ref[...])
     row = iota((count, 1), 0)
     even = row % 4 < 2
-    question = ((row // 8) % NZ * LAYER + inner) * 2 + (row // 4) % 2
+    z = row // 8 % NZ
+    question = (z * LAYER + inner // NC * NC + (z + group) % NC) * 2 + row // 4 % 2
     pick = one_hot(iota((count, 256), 1) == question)
     bounds = dot(pick, range_ref[...].astype(f32).astype(bf16))
     lower, upper = bounds[:, 0:1], bounds[:, 1:2]
@@ -285,8 +288,8 @@
     )
     packed, near = barrier((packed, near))
     near = jnp.concatenate([near, queries.reshape(8, 512), jnp.zeros((8, 512), bf16)], axis=0)
-    far = lax.all_gather(near, "seq_0", axis=0)
-    got = lax.all_gather(packed, "seq_0", axis=0, tiled=True)
+    far = lax.all_gather(near, TURNS[0], axis=0, axis_index_groups=TURNS[1])
+    got = lax.all_gather(packed, TURNS[0], axis=0, axis_index_groups=TURNS[1], tiled=True)
     weights = call(compact_kernel, sds((NY, NZ * ROWS, VD), bf16), (got,))
 
     weights, patches, place, norm_gain, window_order = barrier((weights, patches, place, norm_gain, window_order))
@@ -330,7 +333,7 @@
     )
     sent, queries, suffix_kv, question_lengths = barrier((sent, queries, suffix_kv, question_lengths))
     got = lax.all_to_all(
-        sent.reshape(NZ, 8, 5 * HD), "seq_0", split_axis=0, concat_axis=0, tiled=True
+        sent.reshape(NZ, 8, 5 * HD), TURNS[0], split_axis=0, concat_axis=0, axis_index_groups=TURNS[1], tiled=True
     ).reshape(-1, 5 * HD)
     mixed, level = call(
         suffix_kernel,

time: 172 us -> 176 us (1.023)
  waiting for transfers between devices: 41.3 us -> 51.6 us
  starting transfers between devices: 40.2 us -> 30.8 us
  blocking collectives: 45 us -> 49.6 us
    ppermute x1, starting transfers between devices: 12.5 us -> 2.04 us  [on_device(): other = lax.ppermute(own, 'seq_2', [(0, 1), (1, 0)])]
    all_to_all x1, waiting for transfers between devices: 10 us -> 17.8 us  [on_device(): lax.all_to_all(weights, 'seq_1', split_axis=0, concat_axis=0, tiled=True)]
    all_gather x1, blocking collectives: 33.6 us -> 38.2 us  [on_device(): lax.all_gather(packed, TURNS[0], axis=0, axis_index_groups=TURNS[1], tile...]
    all_to_all x1, waiting for transfers between devices: 11.2 us -> 13.2 us  [on_device(): lax.all_to_all(sent.reshape(NZ, 8, 5 * HD), TURNS[0], split_axis=0, conca...]
where the time goes in v7:
time: 176 us; the launch traced here: 174 us
  waiting for transfers between devices  51.6 us (29%)
  blocking collectives  49.6 us (28%)
  starting transfers between devices  30.8 us (18%)
  Pallas kernels  20.7 us (12%)
  between operations  13.6 us (8%)
  local copies, waits for them, and re-layouts  6.21 us (4%)
    all_gather x1, blocking collectives, on_device(): lax.all_gather(packed, TURNS[0], axis=0, axis_index_groups=TURNS[1], tile...  38.2 us
    pallas_call x9, Pallas kernels, call(): pl.pallas_call(body, out_shape=outs, in_specs=specs or [vm] * len(operand...  20.7 us
    all_to_all x1, waiting for transfers between devices, on_device(): lax.all_to_all(weights, 'seq_1', split_axis=0, concat_axis=0, tiled=True)  17.8 us
    all_to_all x1, waiting for transfers between devices, on_device(): lax.all_to_all(sent.reshape(NZ, 8, 5 * HD), TURNS[0], split_axis=0, conca...  13.2 us
    all_gather x1, blocking collectives, on_device(): merged = lax.all_gather(merged, 'head', axis=0, tiled=True)  11.4 us
    all_to_all x1, waiting for transfers between devices, on_device(): lax.all_to_all(visual, ('seq_1', 'seq_2'), split_axis=0, concat_axis=0, t...  8.43 us
    all_to_all x1, starting transfers between devices, on_device(): lax.all_to_all(sent.reshape(NZ, 8, 5 * HD), TURNS[0], split_axis=0, conca...  7.41 us
    all_to_all x1, waiting for transfers between devices, on_device(): lax.all_to_all(partial.reshape(NX, UNITS, VD), 'head', split_axis=0, conc...  6.19 us
  transfers between devices with their start and end apart: 8, of which 6 were waited for; matrix products, arithmetic and copies ran while one was open for 2% of the time, Pallas kernels for 9%

profile of v7, /device:TPU:1, one launch (start us, length us, event | category | flops | bytes accessed | tf_op | source)
XLA Modules:
  0.0 174.1 jit_solution(15023759594466875094)
XLA Ops:
  6.5 1.5 broadcast_in_dim.13
  8.1 5.0 %all-to-all-start = ((bf16[4,40,2,256]{3,2,1,0:T(2,128)(2,1)}), bf16[4,40,2,256]{3,2,1,0:T(2,128)(2,1)S(1)}, u32[]{:S(2)}, u32[]{:S(2)}) async-start(bf16[4,40,2,256]{3,2,1,0:T(2,128)(2,1)} %broadcast_in_dim.13), calls=%async_computation | async-start | bytes 327680 | tf_op jit(solution)/shard_map/all_to_all | solution.py:284
  13.1 0.0 all-gather.3.cloned.1.call-start
  13.1 0.8 reshape.43
  13.9 0.7 reshape.49
  14.7 0.1 pad.9.clone
  14.7 0.1 pad.2.clone
  14.8 0.8 fusion.1
  15.6 2.5 %all-to-all-done = bf16[4,40,2,256]{3,2,1,0:T(2,128)(2,1)S(1)} async-done(((bf16[4,40,2,256]{3,2,1,0:T(2,128)(2,1)}), bf16[4,40,2,256]{3,2,1,0:T(2,128)(2,1)S(1)}, u32[]{:S(2)}, u32[]{:S(2)}) %all-to-all-start) | async-done | bytes 163872 | tf_op jit(solution)/shard_map/all_to_all | solution.py:284
  18.1 0.8 maximum_maximum_fusion
  18.9 0.0 all-gather.3.cloned.1.call-update
  18.9 0.1 pad_add_fusion.place_ref
  19.0 0.0 copy-start.1
  19.0 0.0 copy-start.2
  19.0 38.2 %all_gather.12.got_ref = bf16[384,640]{1,0:T(8,128)(2,1)S(1)} all-gather(bf16[24,640]{1,0:T(8,128)(2,1)S(1)} %fusion.1), channel_id=1, replica_groups={{0,36,64,100,128,164,192,228,256,292,320,356,384,420,448,484},{4,32,68,..., dimensions={0}, use_global_device_ids=true | all-gather | bytes 522240 | tf_op jit(solution)/shard_map/all_gather | solution.py:292
  57.2 1.6 shard_map.109
  58.8 3.6 %all-to-all-start.1 = ((bf16[4,160,1280]{2,1,0:T(8,128)(2,1)}), bf16[4,160,1280]{2,1,0:T(8,128)(2,1)S(1)}, u32[]{:S(2)}, u32[]{:S(2)}) async-start(bf16[4,160,1280]{2,1,0:T(8,128)(2,1)} %shard_map.109), calls=%async_computation.1 | async-start | bytes 3276800 | tf_op jit(solution)/shard_map/all_to_all | solution.py:302
  62.4 0.0 copy-done.6
  62.4 0.0 copy-done.1
  62.4 0.0 copy-done.2
  62.4 2.9 %shard_map.110 = (bf16[256,1280]{1,0:T(8,128)(2,1)S(1)}, bf16[256,128]{1,0:T(8,128)(2,1)S(1)}) custom-call(s32[4]{0:T(128)S(1)} %pad_add_fusion.place_ref, bf16[256,1280]{1,0:T(8,128)(2,1)S(1)} %copy-done.1, f32[1,1280]{1,0:T(1,128)S(1)} %reshape.46.gain_ref, s32[1,64]{1,0:T(1,128)S(1)} %copy-done.2), custom_call_target="tpu_custom_call" | custom-call | tf_op jit(solution)/shard_map/pallas_call | solution.py:48
  65.3 17.8 %all-to-all-done.1 = bf16[4,160,1280]{2,1,0:T(8,128)(2,1)S(1)} async-done(((bf16[4,160,1280]{2,1,0:T(8,128)(2,1)}), bf16[4,160,1280]{2,1,0:T(8,128)(2,1)S(1)}, u32[]{:S(2)}, u32[]{:S(2)}) %all-to-all-start.1) | async-done | bytes 1638432 | tf_op jit(solution)/shard_map/all_to_all | solution.py:302
  83.2 2.0 %collective-permute-start = (bf16[640,1280]{1,0:T(8,128)(2,1)S(1)}, bf16[640,1280]{1,0:T(8,128)(2,1)S(1)}, u32[]{:S(2)}, u32[]{:S(2)}) collective-permute-start(bf16[640,1280]{1,0:T(8,128)(2,1)S(1)} %bitcast.20), channel_id=1, source_target_pairs={{0,4},{4,0},{1,5},{5,1},{2,6},{6,2},{3,7},{7,3},{8,12},{12,8},{9,1... | collective-permute-start | bytes 4915208 | tf_op jit(solution)/shard_map/ppermute | solution.py:304
  85.2 3.5 %collective-permute-done.other_ref = bf16[640,1280]{1,0:T(8,128)(2,1)S(1)} collective-permute-done((bf16[640,1280]{1,0:T(8,128)(2,1)S(1)}, bf16[640,1280]{1,0:T(8,128)(2,1)S(1)}, u32[]{:S(2)}, u32[]{:S(2)}) %collective-permute-start) | collective-permute-done | bytes 1638432 | tf_op jit(solution)/shard_map/ppermute | solution.py:304
  88.7 4.1 %shard_map.111 = bf16[256,1280]{1,0:T(8,128)(2,1)} custom-call(bf16[256,1280]{1,0:T(8,128)(2,1)S(1)} %get-tuple-element.41.normed_ref, bf16[640,1280]{1,0:T(8,128)(2,1)S(1)} %bitcast.21, bf16[640,1280]{1,0:T(8,128)(2,1)S(1)} %collective-permute-done.other_ref, bf16[256,128]{1,0:T(8,128)(2,1)S(1)} %get-tuple-element.43.member_ref), custom_call_target="tpu_custom_call" | custom-call | tf_op jit(solution)/shard_map/pallas_call | solution.py:48
  92.8 3.6 %all-to-all-start.2 = ((bf16[4,64,1280]{2,1,0:T(8,128)(2,1)}), bf16[4,64,1280]{2,1,0:T(8,128)(2,1)S(1)}, u32[]{:S(2)}, u32[]{:S(2)}) async-start(bf16[4,64,1280]{2,1,0:T(8,128)(2,1)} %bitcast.6), calls=%async_computation.2 | async-start | bytes 1310720 | tf_op jit(solution)/shard_map/all_to_all | solution.py:316
  96.4 0.0 copy-done.7
  96.4 4.4 %shard_map.112 = (bf16[768,640]{1,0:T(8,128)(2,1)S(1)}, f32[1,1280]{1,0:T(1,128)S(1)}) custom-call(s32[4]{0:T(128)S(1)} %pad_add_fusion.place_ref, bf16[256,1280]{1,0:T(8,128)(2,1)S(1)} %copy-done.1, f32[1,1280]{1,0:T(1,128)S(1)} %reshape.50.gain_ref), custom_call_target="tpu_custom_call" | custom-call | tf_op jit(solution)/shard_map/pallas_call | solution.py:48
  100.8 6.2 %all-to-all-done.2 = bf16[4,64,1280]{2,1,0:T(8,128)(2,1)S(1)} async-done(((bf16[4,64,1280]{2,1,0:T(8,128)(2,1)}), bf16[4,64,1280]{2,1,0:T(8,128)(2,1)S(1)}, u32[]{:S(2)}, u32[]{:S(2)}) %all-to-all-start.2) | async-done | bytes 655392 | tf_op jit(solution)/shard_map/all_to_all | solution.py:316
  107.0 3.2 %collective-permute-start.1 = (bf16[16,176,512]{2,1,0:T(8,128)(2,1)}, bf16[16,176,512]{2,1,0:T(8,128)(2,1)S(1)}, u32[]{:S(2)}, u32[]{:S(2)}) collective-permute-start(bf16[16,176,512]{2,1,0:T(8,128)(2,1)} %bitcast.22), channel_id=1, source_target_pairs={{0,4},{4,0},{1,5},{5,1},{2,6},{6,2},{3,7},{7,3},{8,12},{12,8},{9,1... | collective-permute-start | bytes 8650760 | tf_op jit(solution)/shard_map/ppermute | solution.py:320
  110.2 1.1 shard_map.113
  111.2 11.4 %all_gather.15.merged_ref = bf16[256,1280]{1,0:T(8,128)(2,1)S(1)} all-gather(bf16[64,1280]{1,0:T(8,128)(2,1)S(1)} %shard_map.113), channel_id=1, replica_groups=mesh['seq_0'=16,'seq_1'=4,'seq_2'=2,'head'=4] {'head'}, dimensions={0}, use_global_device_ids=true | all-gather | bytes 819200 | tf_op jit(solution)/shard_map/all_gather | solution.py:322
  122.6 0.0 collective-permute-done.1.other_ref
  122.6 1.8 %copy-done = bf16[2816,512]{1,0:T(8,128)(2,1)S(1)} copy-done((bf16[2816,512]{1,0:T(8,128)(2,1)S(1)}, bf16[2816,512]{1,0:T(8,128)(2,1)}, u32[]{:S(2)}) %copy-start) | copy-done | bytes 2883608
  124.5 1.9 %shard_map.114 = bf16[8,64,512]{2,1,0:T(8,128)(2,1)} custom-call(bf16[256,1280]{1,0:T(8,128)(2,1)S(1)} %all_gather.15.merged_ref, bf16[16,176,512]{2,1,0:T(8,128)(2,1)S(1)} %bitcast.24, bf16[16,176,512]{2,1,0:T(8,128)(2,1)S(1)} %collective-permute-done.1.other_ref), custom_call_target="tpu_custom_call" | custom-call | tf_op jit(solution)/shard_map/pallas_call | solution.py:48
  126.3 6.0 %all-to-all-start.3 = ((bf16[8,64,512]{2,1,0:T(8,128)(2,1)}), bf16[8,64,512]{2,1,0:T(8,128)(2,1)S(1)}, u32[]{:S(2)}, u32[]{:S(2)}) async-start(bf16[8,64,512]{2,1,0:T(8,128)(2,1)} %shard_map.114), calls=%async_computation.3 | async-start | bytes 1048576 | tf_op jit(solution)/shard_map/all_to_all | solution.py:325
  132.3 0.0 copy-done.8
  132.3 0.1 copy.13.range_ref
  132.5 0.9 slice_bitcast_fusion.asked_ref
  133.4 8.4 %all-to-all-done.3 = bf16[8,64,512]{2,1,0:T(8,128)(2,1)S(1)} async-done(((bf16[8,64,512]{2,1,0:T(8,128)(2,1)}), bf16[8,64,512]{2,1,0:T(8,128)(2,1)S(1)}, u32[]{:S(2)}, u32[]{:S(2)}) %all-to-all-start.3) | async-done | bytes 524320 | tf_op jit(solution)/shard_map/all_to_all | solution.py:325
  141.8 2.7 %shard_map.115 = bf16[128,640]{1,0:T(8,128)(2,1)} custom-call(s32[4]{0:T(128)S(1)} %pad_add_fusion.place_ref, bf16[512,512]{1,0:T(8,128)(2,1)S(1)} %bitcast.26, bf16[128,512]{1,0:T(8,128)(2,1)S(1)} %slice_bitcast_fusion.asked_ref, s32[256,2]{1,0:T(8,128)S(1)} %copy.13.range_ref), custom_call_target="tpu_custom_call" | custom-call | tf_op jit(solution)/shard_map/pallas_call | solution.py:48
  144.5 7.4 %all-to-all-start.4 = ((bf16[16,8,640]{2,1,0:T(8,128)(2,1)}), bf16[16,8,640]{2,1,0:T(8,128)(2,1)S(1)}, u32[]{:S(2)}, u32[]{:S(2)}) async-start(bf16[16,8,640]{2,1,0:T(8,128)(2,1)} %bitcast.11), calls=%async_computation.4 | async-start | bytes 327680 | tf_op jit(solution)/shard_map/all_to_all | solution.py:335
  151.9 0.0 copy-done.5
  152.0 0.0 copy-done.4
  152.0 0.0 copy-done.3
  152.0 0.9 shard_map.116
  152.9 13.2 %all-to-all-done.4 = bf16[16,8,640]{2,1,0:T(8,128)(2,1)S(1)} async-done(((bf16[16,8,640]{2,1,0:T(8,128)(2,1)}), bf16[16,8,640]{2,1,0:T(8,128)(2,1)S(1)}, u32[]{:S(2)}, u32[]{:S(2)}) %all-to-all-start.4) | async-done | bytes 163872 | tf_op jit(solution)/shard_map/all_to_all | solution.py:335
  166.1 1.1 shard_map.117
  (16 shorter events, 0.1 us)
Async XLA Ops:
  8.1 10.0 %all-to-all-start = ((bf16[4,40,2,256]{3,2,1,0:T(2,128)(2,1)}), bf16[4,40,2,256]{3,2,1,0:T(2,128)(2,1)S(1)}, u32[]{:S(2)}, u32[]{:S(2)}) async-start(bf16[4,40,2,256]{3,2,1,0:T(2,128)(2,1)} %broadcast_in_dim.13), calls=%async_computation | async-start | bytes 327680 | tf_op jit(solution)/shard_map/all_to_all | solution.py:284
  13.1 93.9 %all-gather.3.cloned.1.call-start = ((), (), s32[]{:S(2)}) async-start(), calls=%async_computation.5 | async-start | bytes 3063808 | tf_op jit(solution)/shard_map/all_gather | solution.py:291
  19.0 43.4 %copy-start.6 = (f32[1280]{0:T(1024)S(1)}, f32[1280]{0:T(1024)}, u32[]{:S(2)}) copy-start(f32[1280]{0:T(1024)} %param.12) | copy-start | bytes 15364
  19.0 43.4 %copy-start.1 = (bf16[256,1280]{1,0:T(8,128)(2,1)S(1)}, bf16[256,1280]{1,0:T(8,128)(2,1)}, u32[]{:S(2)}) copy-start(bf16[256,1280]{1,0:T(8,128)(2,1)} %patches_ref.1) | copy-start | bytes 1966084
  19.0 43.4 %copy-start.2 = (s32[1,64]{1,0:T(1,128)S(1)}, s32[1,64]{1,0:T(1,128)}, u32[]{:S(2)}) copy-start(s32[1,64]{1,0:T(1,128)} %window_ref) | copy-start | bytes 772
  58.8 24.4 %all-to-all-start.1 = ((bf16[4,160,1280]{2,1,0:T(8,128)(2,1)}), bf16[4,160,1280]{2,1,0:T(8,128)(2,1)S(1)}, u32[]{:S(2)}, u32[]{:S(2)}) async-start(bf16[4,160,1280]{2,1,0:T(8,128)(2,1)} %shard_map.109), calls=%async_computation.1 | async-start | bytes 3276800 | tf_op jit(solution)/shard_map/all_to_all | solution.py:302
  83.2 13.3 %copy-start.7 = (f32[1280]{0:T(1024)S(1)}, f32[1280]{0:T(1024)}, u32[]{:S(2)}) copy-start(f32[1280]{0:T(1024)} %param.16) | copy-start | bytes 15364
  83.2 5.5 %collective-permute-start = (bf16[640,1280]{1,0:T(8,128)(2,1)S(1)}, bf16[640,1280]{1,0:T(8,128)(2,1)S(1)}, u32[]{:S(2)}, u32[]{:S(2)}) collective-permute-start(bf16[640,1280]{1,0:T(8,128)(2,1)S(1)} %bitcast.20), channel_id=1, source_target_pairs={{0,4},{4,0},{1,5},{5,1},{2,6},{6,2},{3,7},{7,3},{8,12},{12,8},{9,1... | collective-permute-start | bytes 4915208 | tf_op jit(solution)/shard_map/ppermute | solution.py:304
  92.8 14.2 %all-to-all-start.2 = ((bf16[4,64,1280]{2,1,0:T(8,128)(2,1)}), bf16[4,64,1280]{2,1,0:T(8,128)(2,1)S(1)}, u32[]{:S(2)}, u32[]{:S(2)}) async-start(bf16[4,64,1280]{2,1,0:T(8,128)(2,1)} %bitcast.6), calls=%async_computation.2 | async-start | bytes 1310720 | tf_op jit(solution)/shard_map/all_to_all | solution.py:316
  107.0 15.7 %collective-permute-start.1 = (bf16[16,176,512]{2,1,0:T(8,128)(2,1)}, bf16[16,176,512]{2,1,0:T(8,128)(2,1)S(1)}, u32[]{:S(2)}, u32[]{:S(2)}) collective-permute-start(bf16[16,176,512]{2,1,0:T(8,128)(2,1)} %bitcast.22), channel_id=1, source_target_pairs={{0,4},{4,0},{1,5},{5,1},{2,6},{6,2},{3,7},{7,3},{8,12},{12,8},{9,1... | collective-permute-start | bytes 8650760 | tf_op jit(solution)/shard_map/ppermute | solution.py:320
  122.6 1.8 %copy-start = (bf16[2816,512]{1,0:T(8,128)(2,1)S(1)}, bf16[2816,512]{1,0:T(8,128)(2,1)}, u32[]{:S(2)}) copy-start(bf16[2816,512]{1,0:T(8,128)(2,1)} %all-gather.3.cloned.1.call-done) | copy-start | bytes 8650756
  124.5 7.9 %copy-start.8 = (s32[256,2]{0,1:T(2,128)S(1)}, s32[256,2]{0,1:T(2,128)}, u32[]{:S(2)}) copy-start(s32[256,2]{0,1:T(2,128)} %param.21) | copy-start | bytes 6148
  124.5 27.5 %copy-start.5 = (bf16[2,2048]{1,0:T(2,128)(2,1)S(1)}, bf16[2,2048]{1,0:T(2,128)(2,1)}, u32[]{:S(2)}) copy-start(bf16[2,2048]{1,0:T(2,128)(2,1)} %param.18) | copy-start | bytes 24580
  124.5 27.5 %copy-start.4 = (bf16[2,64,2,256]{3,2,1,0:T(2,128)(2,1)S(1)}, bf16[2,64,2,256]{3,2,1,0:T(2,128)(2,1)}, u32[]{:S(2)}) copy-start(bf16[2,64,2,256]{3,2,1,0:T(2,128)(2,1)} %param.19) | copy-start | bytes 393220
  126.3 25.7 %copy-start.3 = (s32[2]{0:T(128)S(1)}, s32[2]{0:T(128)}, u32[]{:S(2)}) copy-start(s32[2]{0:T(128)} %length_ref) | copy-start | bytes 28
  126.3 15.5 %all-to-all-start.3 = ((bf16[8,64,512]{2,1,0:T(8,128)(2,1)}), bf16[8,64,512]{2,1,0:T(8,128)(2,1)S(1)}, u32[]{:S(2)}, u32[]{:S(2)}) async-start(bf16[8,64,512]{2,1,0:T(8,128)(2,1)} %shard_map.114), calls=%async_computation.3 | async-start | bytes 1048576 | tf_op jit(solution)/shard_map/all_to_all | solution.py:325
  144.5 21.5 %all-to-all-start.4 = ((bf16[16,8,640]{2,1,0:T(8,128)(2,1)}), bf16[16,8,640]{2,1,0:T(8,128)(2,1)S(1)}, u32[]{:S(2)}, u32[]{:S(2)}) async-start(bf16[16,8,640]{2,1,0:T(8,128)(2,1)} %bitcast.11), calls=%async_computation.4 | async-start | bytes 327680 | tf_op jit(solution)/shard_map/all_to_all | solution.py:335
Sparse Core Ops, SparseCore 0:
  19.0 75.9 all-gather.2

commit v8 on v6

--- a/solution.py
+++ b/solution.py
@@ -180,15 +180,29 @@
     out_ref[:, half:] = jnp.where(first, right, left).astype(bf16)
 
 
-def visual_kernel(merged_ref, own_ref, other_ref, out_ref):
+def visual_kernel(merged_ref, own_ref, other_ref, out_ref, held_ref, sems):
     rows = 4 * NY * ROWS
     half = VD // 2
+    sides = (own_ref, other_ref)
+
+    def copy(side, k):
+        return pltpu.make_async_copy(
+            sides[side].at[k, pl.ds(0, rows)],
+            held_ref.at[pl.ds((side * NZ + k) * rows, rows)],
+            sems.at[side * NZ + k],
+        )
+
+    for k in range(NZ):
+        for side in range(2):
+            copy(side, k).start()
     total = jnp.zeros((UNITS, 512), f32)
     for i in range(4):
-        merged = merged_ref[i * UNITS : (i + 1) * UNITS]
-        for part, ref in ((merged[:, :half], own_ref), (merged[:, half:], other_ref)):
-            weights = jnp.concatenate([ref[i * 4 + k, :rows] for k in range(4)], axis=0)
-            total += dot(part, weights)
+        for side in range(2):
+            for k in range(4):
+                copy(side, i * 4 + k).wait()
+            merged = merged_ref[i * UNITS : (i + 1) * UNITS, side * half : (side + 1) * half]
+            at = (side * 4 + i) * half
+            total += dot(merged, held_ref[at : at + half])
     visual = total.astype(bf16)
     for k in range(LAYER):
         out_ref[k] = visual
@@ -317,7 +331,15 @@
     far_other = lax.ppermute(far, "seq_2", [(0, 1), (1, 0)])
     merged = call(merge_kernel, sds((UNITS, VD), bf16), (place, partial, gains, turn), [SMEM] + [VMEM] * 3)
     merged = lax.all_gather(merged, "head", axis=0, tiled=True)
-    visual = call(visual_kernel, sds((LAYER, UNITS, 512), bf16), (merged, far, far_other), vmem=24 << 20)
+    anywhere = pl.BlockSpec(memory_space=pl.ANY)
+    visual = pl.pallas_call(
+        visual_kernel,
+        out_shape=sds((LAYER, UNITS, 512), bf16),
+        in_specs=[VMEM, anywhere, anywhere],
+        out_specs=VMEM,
+        scratch_shapes=[pltpu.VMEM((4 * VD, 512), bf16), pltpu.SemaphoreType.DMA((2 * NZ,))],
+        compiler_params=pltpu.CompilerParams(vmem_limit_bytes=58 << 20),
+    )(merged, far, far_other)
     asked = far[:, -16:-8].reshape(NZ * 8, 512)
     visual = lax.all_to_all(
         visual, ("seq_1", "seq_2"), split_axis=0, concat_axis=0, tiled=True

time: 172 us -> 173 us (level)
  Pallas kernels: 20.4 us -> 23.7 us
  local copies, waits for them, and re-layouts: 6.21 us -> 4.38 us
    pallas_call x0 -> x1, Pallas kernels: none -> 5.13 us  [on_device(): pl.pallas_call(visual_kernel, out_shape=sds((LAYER, UNITS, 512), bf16), i...]
    pallas_call x9 -> x8, Pallas kernels: 20.4 us -> 18.6 us  [call(): pl.pallas_call(body, out_shape=outs, in_specs=specs or [vm] * len(operand...]
    unnamed x21 -> x19, local copies, waits for them, and re-layouts: 2.01 us -> 0.2 us
where the time goes in v8:
time: 173 us; the launch traced here: 170 us
  blocking collectives  45.8 us (26%)
  waiting for transfers between devices  41.3 us (24%)
  starting transfers between devices  40 us (23%)
  Pallas kernels  23.7 us (14%)
  between operations  13.6 us (8%)
  local copies, waits for them, and re-layouts  4.38 us (3%)
    all_gather x1, blocking collectives, on_device(): got = lax.all_gather(packed, 'seq_0', axis=0, tiled=True)  33.6 us
    pallas_call x8, Pallas kernels, call(): pl.pallas_call(body, out_shape=outs, in_specs=specs or [vm] * len(operand...  18.6 us
    ppermute x1, starting transfers between devices, on_device(): other = lax.ppermute(own, 'seq_2', [(0, 1), (1, 0)])  12.5 us
    all_gather x1, blocking collectives, on_device(): merged = lax.all_gather(merged, 'head', axis=0, tiled=True)  12.1 us
    all_to_all x1, waiting for transfers between devices, on_device(): lax.all_to_all(sent.reshape(NZ, 8, 5 * HD), 'seq_0', split_axis=0, concat...  11.2 us
    all_to_all x1, waiting for transfers between devices, on_device(): lax.all_to_all(weights, 'seq_1', split_axis=0, concat_axis=0, tiled=True)  10 us
    all_to_all x1, waiting for transfers between devices, on_device(): lax.all_to_all(visual, ('seq_1', 'seq_2'), split_axis=0, concat_axis=0, t...  8.43 us
    all_to_all x1, waiting for transfers between devices, on_device(): lax.all_to_all(partial.reshape(NX, UNITS, VD), 'head', split_axis=0, conc...  5.99 us
  transfers between devices with their start and end apart: 8, of which 6 were waited for; matrix products, arithmetic and copies ran while one was open for 2% of the time, Pallas kernels for 9%

profile of v8, /device:TPU:1, one launch (start us, length us, event | category | flops | bytes accessed | tf_op | source)
XLA Modules:
  0.0 170.3 jit_solution(11068443154522926607)
XLA Ops:
  6.5 1.5 broadcast_in_dim.13
  8.1 5.0 %all-to-all-start = ((bf16[4,40,2,256]{3,2,1,0:T(2,128)(2,1)}), bf16[4,40,2,256]{3,2,1,0:T(2,128)(2,1)S(1)}, u32[]{:S(2)}, u32[]{:S(2)}) async-start(bf16[4,40,2,256]{3,2,1,0:T(2,128)(2,1)} %broadcast_in_dim.13), calls=%async_computation | async-start | bytes 327680 | tf_op jit(solution)/shard_map/all_to_all | solution.py:295
  13.1 0.0 all-gather.3.cloned.1.call-start
  13.1 0.8 reshape.43
  13.9 0.7 reshape.49
  14.6 0.1 pad.9.clone
  14.7 0.1 pad.2.clone
  14.8 0.8 fusion.1
  15.6 2.5 %all-to-all-done = bf16[4,40,2,256]{3,2,1,0:T(2,128)(2,1)S(1)} async-done(((bf16[4,40,2,256]{3,2,1,0:T(2,128)(2,1)}), bf16[4,40,2,256]{3,2,1,0:T(2,128)(2,1)S(1)}, u32[]{:S(2)}, u32[]{:S(2)}) %all-to-all-start) | async-done | bytes 163872 | tf_op jit(solution)/shard_map/all_to_all | solution.py:295
  18.1 0.8 maximum_maximum_fusion
  18.9 0.0 all-gather.3.cloned.1.call-update
  18.9 0.1 pad_add_fusion.place_ref
  19.0 0.0 copy-start.5
  19.0 0.0 copy-start
  19.0 33.6 %all_gather.12.got_ref = bf16[384,640]{1,0:T(8,128)(2,1)S(1)} all-gather(bf16[24,640]{1,0:T(8,128)(2,1)S(1)} %fusion.1), channel_id=1, replica_groups=mesh['seq_0'=16,'seq_1'=4,'seq_2'=2,'head'=4] {'seq_0'}, dimensions={0}, use_global_device_ids=true | all-gather | bytes 522240 | tf_op jit(solution)/shard_map/all_gather | solution.py:303
  52.6 1.6 shard_map.109
  54.2 3.6 %all-to-all-start.1 = ((bf16[4,160,1280]{2,1,0:T(8,128)(2,1)}), bf16[4,160,1280]{2,1,0:T(8,128)(2,1)S(1)}, u32[]{:S(2)}, u32[]{:S(2)}) async-start(bf16[4,160,1280]{2,1,0:T(8,128)(2,1)} %shard_map.109), calls=%async_computation.1 | async-start | bytes 3276800 | tf_op jit(solution)/shard_map/all_to_all | solution.py:313
  57.8 0.0 copy-done.5
  57.8 0.0 copy-done
  57.8 0.0 copy-done.1
  57.9 2.9 %shard_map.110 = (bf16[256,1280]{1,0:T(8,128)(2,1)S(1)}, bf16[256,128]{1,0:T(8,128)(2,1)S(1)}) custom-call(s32[4]{0:T(128)S(1)} %pad_add_fusion.place_ref, bf16[256,1280]{1,0:T(8,128)(2,1)S(1)} %copy-done, f32[1,1280]{1,0:T(1,128)S(1)} %reshape.46.gain_ref, s32[1,64]{1,0:T(1,128)S(1)} %copy-done.1), custom_call_target="tpu_custom_call" | custom-call | tf_op jit(solution)/shard_map/pallas_call | solution.py:47
  60.7 10.0 %all-to-all-done.1 = bf16[4,160,1280]{2,1,0:T(8,128)(2,1)S(1)} async-done(((bf16[4,160,1280]{2,1,0:T(8,128)(2,1)}), bf16[4,160,1280]{2,1,0:T(8,128)(2,1)S(1)}, u32[]{:S(2)}, u32[]{:S(2)}) %all-to-all-start.1) | async-done | bytes 1638432 | tf_op jit(solution)/shard_map/all_to_all | solution.py:313
  70.7 12.5 %collective-permute-start = (bf16[640,1280]{1,0:T(8,128)(2,1)S(1)}, bf16[640,1280]{1,0:T(8,128)(2,1)S(1)}, u32[]{:S(2)}, u32[]{:S(2)}) collective-permute-start(bf16[640,1280]{1,0:T(8,128)(2,1)S(1)} %bitcast.20), channel_id=1, source_target_pairs={{0,4},{4,0},{1,5},{5,1},{2,6},{6,2},{3,7},{7,3},{8,12},{12,8},{9,1... | collective-permute-start | bytes 4915208 | tf_op jit(solution)/shard_map/ppermute | solution.py:315
  83.2 3.1 %collective-permute-done.other_ref = bf16[640,1280]{1,0:T(8,128)(2,1)S(1)} collective-permute-done((bf16[640,1280]{1,0:T(8,128)(2,1)S(1)}, bf16[640,1280]{1,0:T(8,128)(2,1)S(1)}, u32[]{:S(2)}, u32[]{:S(2)}) %collective-permute-start) | collective-permute-done | bytes 1638432 | tf_op jit(solution)/shard_map/ppermute | solution.py:315
  86.3 4.1 %shard_map.111 = bf16[256,1280]{1,0:T(8,128)(2,1)} custom-call(bf16[256,1280]{1,0:T(8,128)(2,1)S(1)} %get-tuple-element.41.normed_ref, bf16[640,1280]{1,0:T(8,128)(2,1)S(1)} %bitcast.21, bf16[640,1280]{1,0:T(8,128)(2,1)S(1)} %collective-permute-done.other_ref, bf16[256,128]{1,0:T(8,128)(2,1)S(1)} %get-tuple-element.43.member_ref), custom_call_target="tpu_custom_call" | custom-call | tf_op jit(solution)/shard_map/pallas_call | solution.py:47
  90.5 3.9 %all-to-all-start.2 = ((bf16[4,64,1280]{2,1,0:T(8,128)(2,1)}), bf16[4,64,1280]{2,1,0:T(8,128)(2,1)S(1)}, u32[]{:S(2)}, u32[]{:S(2)}) async-start(bf16[4,64,1280]{2,1,0:T(8,128)(2,1)} %bitcast.6), calls=%async_computation.2 | async-start | bytes 1310720 | tf_op jit(solution)/shard_map/all_to_all | solution.py:327
  94.3 0.0 copy-done.6
  94.4 4.3 %shard_map.112 = (bf16[768,640]{1,0:T(8,128)(2,1)S(1)}, f32[1,1280]{1,0:T(1,128)S(1)}) custom-call(s32[4]{0:T(128)S(1)} %pad_add_fusion.place_ref, bf16[256,1280]{1,0:T(8,128)(2,1)S(1)} %copy-done, f32[1,1280]{1,0:T(1,128)S(1)} %reshape.50.gain_ref), custom_call_target="tpu_custom_call" | custom-call | tf_op jit(solution)/shard_map/pallas_call | solution.py:47
  98.7 6.0 %all-to-all-done.2 = bf16[4,64,1280]{2,1,0:T(8,128)(2,1)S(1)} async-done(((bf16[4,64,1280]{2,1,0:T(8,128)(2,1)}), bf16[4,64,1280]{2,1,0:T(8,128)(2,1)S(1)}, u32[]{:S(2)}, u32[]{:S(2)}) %all-to-all-start.2) | async-done | bytes 655392 | tf_op jit(solution)/shard_map/all_to_all | solution.py:327
  104.7 3.4 %collective-permute-start.1 = (bf16[16,176,512]{2,1,0:T(8,128)(2,1)}, bf16[16,176,512]{2,1,0:T(8,128)(2,1)}, u32[]{:S(2)}, u32[]{:S(2)}) collective-permute-start(bf16[16,176,512]{2,1,0:T(8,128)(2,1)} %bitcast.26), channel_id=1, source_target_pairs={{0,4},{4,0},{1,5},{5,1},{2,6},{6,2},{3,7},{7,3},{8,12},{12,8},{9,1... | collective-permute-start | bytes 8650760 | tf_op jit(solution)/shard_map/ppermute | solution.py:331
  108.1 1.1 shard_map.113
  109.2 12.1 %all_gather.15.merged_ref = bf16[256,1280]{1,0:T(8,128)(2,1)} all-gather(bf16[64,1280]{1,0:T(8,128)(2,1)S(1)} %shard_map.113), channel_id=1, replica_groups=mesh['seq_0'=16,'seq_1'=4,'seq_2'=2,'head'=4] {'head'}, dimensions={0}, use_global_device_ids=true | all-gather | bytes 819200 | tf_op jit(solution)/shard_map/all_gather | solution.py:333
  121.3 0.0 collective-permute-done.1.other_ref
  121.3 5.1 %shard_map.114 = bf16[8,64,512]{2,1,0:T(8,128)(2,1)} custom-call(bf16[256,1280]{1,0:T(8,128)(2,1)} %all_gather.15.merged_ref, bf16[16,176,512]{2,1,0:T(8,128)(2,1)} %bitcast.27, bf16[16,176,512]{2,1,0:T(8,128)(2,1)} %collective-permute-done.1.other_ref), custom_call_target="tpu_custom_call" | custom-call | tf_op jit(solution)/shard_map/pallas_call | solution.py:335
  126.5 0.0 copy-start.2
  126.5 5.7 %all-to-all-start.3 = ((bf16[8,64,512]{2,1,0:T(8,128)(2,1)}), bf16[8,64,512]{2,1,0:T(8,128)(2,1)S(1)}, u32[]{:S(2)}, u32[]{:S(2)}) async-start(bf16[8,64,512]{2,1,0:T(8,128)(2,1)} %shard_map.114), calls=%async_computation.3 | async-start | bytes 1048576 | tf_op jit(solution)/shard_map/all_to_all | solution.py:344
  132.2 0.0 copy-done.7
  132.2 0.1 copy.13.range_ref
  132.3 0.9 slice_bitcast_fusion.asked_ref
  133.3 8.4 %all-to-all-done.3 = bf16[8,64,512]{2,1,0:T(8,128)(2,1)S(1)} async-done(((bf16[8,64,512]{2,1,0:T(8,128)(2,1)}), bf16[8,64,512]{2,1,0:T(8,128)(2,1)S(1)}, u32[]{:S(2)}, u32[]{:S(2)}) %all-to-all-start.3) | async-done | bytes 524320 | tf_op jit(solution)/shard_map/all_to_all | solution.py:344
  141.7 2.6 %shard_map.115 = bf16[128,640]{1,0:T(8,128)(2,1)} custom-call(s32[4]{0:T(128)S(1)} %pad_add_fusion.place_ref, bf16[512,512]{1,0:T(8,128)(2,1)S(1)} %bitcast.23, bf16[128,512]{1,0:T(8,128)(2,1)S(1)} %slice_bitcast_fusion.asked_ref, s32[256,2]{1,0:T(8,128)S(1)} %copy.13.range_ref), custom_call_target="tpu_custom_call" | custom-call | tf_op jit(solution)/shard_map/pallas_call | solution.py:47
  144.3 5.9 %all-to-all-start.4 = ((bf16[16,8,640]{2,1,0:T(8,128)(2,1)}), bf16[16,8,640]{2,1,0:T(8,128)(2,1)S(1)}, u32[]{:S(2)}, u32[]{:S(2)}) async-start(bf16[16,8,640]{2,1,0:T(8,128)(2,1)} %bitcast.11), calls=%async_computation.4 | async-start | bytes 327680 | tf_op jit(solution)/shard_map/all_to_all | solution.py:354
  150.2 0.0 copy-done.4
  150.2 0.0 copy-done.3
  150.2 0.0 copy-done.2
  150.2 0.9 shard_map.116
  151.1 11.2 %all-to-all-done.4 = bf16[16,8,640]{2,1,0:T(8,128)(2,1)S(1)} async-done(((bf16[16,8,640]{2,1,0:T(8,128)(2,1)}), bf16[16,8,640]{2,1,0:T(8,128)(2,1)S(1)}, u32[]{:S(2)}, u32[]{:S(2)}) %all-to-all-start.4) | async-done | bytes 163872 | tf_op jit(solution)/shard_map/all_to_all | solution.py:354
  162.4 1.1 shard_map.117
  (14 shorter events, 0.1 us)
Async XLA Ops:
  8.1 10.0 %all-to-all-start = ((bf16[4,40,2,256]{3,2,1,0:T(2,128)(2,1)}), bf16[4,40,2,256]{3,2,1,0:T(2,128)(2,1)S(1)}, u32[]{:S(2)}, u32[]{:S(2)}) async-start(bf16[4,40,2,256]{3,2,1,0:T(2,128)(2,1)} %broadcast_in_dim.13), calls=%async_computation | async-start | bytes 327680 | tf_op jit(solution)/shard_map/all_to_all | solution.py:295
  13.1 91.6 %all-gather.3.cloned.1.call-start = ((), (), s32[]{:S(2)}) async-start(), calls=%async_computation.5 | async-start | bytes 3063808 | tf_op jit(solution)/shard_map/all_gather | solution.py:302
  19.0 38.8 %copy-start.5 = (f32[1280]{0:T(1024)S(1)}, f32[1280]{0:T(1024)}, u32[]{:S(2)}) copy-start(f32[1280]{0:T(1024)} %param.12) | copy-start | bytes 15364
  19.0 38.9 %copy-start = (bf16[256,1280]{1,0:T(8,128)(2,1)S(1)}, bf16[256,1280]{1,0:T(8,128)(2,1)}, u32[]{:S(2)}) copy-start(bf16[256,1280]{1,0:T(8,128)(2,1)} %patches_ref.1) | copy-start | bytes 1966084
  19.0 38.9 %copy-start.1 = (s32[1,64]{1,0:T(1,128)S(1)}, s32[1,64]{1,0:T(1,128)}, u32[]{:S(2)}) copy-start(s32[1,64]{1,0:T(1,128)} %window_ref) | copy-start | bytes 772
  54.2 16.5 %all-to-all-start.1 = ((bf16[4,160,1280]{2,1,0:T(8,128)(2,1)}), bf16[4,160,1280]{2,1,0:T(8,128)(2,1)S(1)}, u32[]{:S(2)}, u32[]{:S(2)}) async-start(bf16[4,160,1280]{2,1,0:T(8,128)(2,1)} %shard_map.109), calls=%async_computation.1 | async-start | bytes 3276800 | tf_op jit(solution)/shard_map/all_to_all | solution.py:313
  70.7 23.6 %copy-start.6 = (f32[1280]{0:T(1024)S(1)}, f32[1280]{0:T(1024)}, u32[]{:S(2)}) copy-start(f32[1280]{0:T(1024)} %param.16) | copy-start | bytes 15364
  70.7 15.6 %collective-permute-start = (bf16[640,1280]{1,0:T(8,128)(2,1)S(1)}, bf16[640,1280]{1,0:T(8,128)(2,1)S(1)}, u32[]{:S(2)}, u32[]{:S(2)}) collective-permute-start(bf16[640,1280]{1,0:T(8,128)(2,1)S(1)} %bitcast.20), channel_id=1, source_target_pairs={{0,4},{4,0},{1,5},{5,1},{2,6},{6,2},{3,7},{7,3},{8,12},{12,8},{9,1... | collective-permute-start | bytes 4915208 | tf_op jit(solution)/shard_map/ppermute | solution.py:315
  90.5 14.2 %all-to-all-start.2 = ((bf16[4,64,1280]{2,1,0:T(8,128)(2,1)}), bf16[4,64,1280]{2,1,0:T(8,128)(2,1)S(1)}, u32[]{:S(2)}, u32[]{:S(2)}) async-start(bf16[4,64,1280]{2,1,0:T(8,128)(2,1)} %bitcast.6), calls=%async_computation.2 | async-start | bytes 1310720 | tf_op jit(solution)/shard_map/all_to_all | solution.py:327
  104.7 16.6 %collective-permute-start.1 = (bf16[16,176,512]{2,1,0:T(8,128)(2,1)}, bf16[16,176,512]{2,1,0:T(8,128)(2,1)}, u32[]{:S(2)}, u32[]{:S(2)}) collective-permute-start(bf16[16,176,512]{2,1,0:T(8,128)(2,1)} %bitcast.26), channel_id=1, source_target_pairs={{0,4},{4,0},{1,5},{5,1},{2,6},{6,2},{3,7},{7,3},{8,12},{12,8},{9,1... | collective-permute-start | bytes 8650760 | tf_op jit(solution)/shard_map/ppermute | solution.py:331
  121.3 10.9 %copy-start.7 = (s32[256,2]{0,1:T(2,128)S(1)}, s32[256,2]{0,1:T(2,128)}, u32[]{:S(2)}) copy-start(s32[256,2]{0,1:T(2,128)} %param.21) | copy-start | bytes 6148
  121.3 28.9 %copy-start.4 = (bf16[2,2048]{1,0:T(2,128)(2,1)S(1)}, bf16[2,2048]{1,0:T(2,128)(2,1)}, u32[]{:S(2)}) copy-start(bf16[2,2048]{1,0:T(2,128)(2,1)} %param.18) | copy-start | bytes 24580
  121.3 28.9 %copy-start.3 = (bf16[2,64,2,256]{3,2,1,0:T(2,128)(2,1)S(1)}, bf16[2,64,2,256]{3,2,1,0:T(2,128)(2,1)}, u32[]{:S(2)}) copy-start(bf16[2,64,2,256]{3,2,1,0:T(2,128)(2,1)} %param.19) | copy-start | bytes 393220
  126.5 23.8 %copy-start.2 = (s32[2]{0:T(128)S(1)}, s32[2]{0:T(128)}, u32[]{:S(2)}) copy-start(s32[2]{0:T(128)} %length_ref) | copy-start | bytes 28
  126.5 15.2 %all-to-all-start.3 = ((bf16[8,64,512]{2,1,0:T(8,128)(2,1)}), bf16[8,64,512]{2,1,0:T(8,128)(2,1)S(1)}, u32[]{:S(2)}, u32[]{:S(2)}) async-start(bf16[8,64,512]{2,1,0:T(8,128)(2,1)} %shard_map.114), calls=%async_computation.3 | async-start | bytes 1048576 | tf_op jit(solution)/shard_map/all_to_all | solution.py:344
  144.3 18.1 %all-to-all-start.4 = ((bf16[16,8,640]{2,1,0:T(8,128)(2,1)}), bf16[16,8,640]{2,1,0:T(8,128)(2,1)S(1)}, u32[]{:S(2)}, u32[]{:S(2)}) async-start(bf16[16,8,640]{2,1,0:T(8,128)(2,1)} %bitcast.11), calls=%async_computation.4 | async-start | bytes 327680 | tf_op jit(solution)/shard_map/all_to_all | solution.py:354
Sparse Core Ops, SparseCore 0:
  19.0 71.9 all-gather.2
